TPU v7x, 32 devices: a whole 2x2x4 slice. The times are simulated.
32 devices in a mesh: group: 2 (over x), serve: 8 (over z, y), tensor: 2 (over core).
Axes of the slice: x: 2, y: 2, z: 4, core: 2. Of those that a mesh axis runs over, the one named last changes fastest.
Arguments:
- tokens: bfloat16 [2048, 8192], P(('group', 'serve'), 'tensor'), parts along dimension 0, may hold values from -70 to 70
- query_weight: bfloat16 [8192, 512], P(None, 'tensor'), may hold values from -0.0625 to 0.0625
- key_value_weight: bfloat16 [8192, 256], P(None, 'tensor'), may hold values from -0.0625 to 0.0625
- output_weight: bfloat16 [512, 8192], P('tensor'), may hold values from -0.25 to 0.25
- adapter_down_maps: bfloat16 [32, 48, 8192], P(('group', 'serve'), None, 'tensor'), parts along dimension 0, may hold values from -0.0625 to 0.0625
- adapter_query_up: bfloat16 [32, 16, 512], P(('group', 'serve'), None, 'tensor'), parts along dimension 0, may hold values from -1.5 to 1.5
- adapter_key_value_up: bfloat16 [32, 16, 256], P(('group', 'serve'), None, 'tensor'), parts along dimension 0, may hold values from -1.5 to 1.5
- adapter_output_down: bfloat16 [32, 16, 512], P(('group', 'serve'), None, 'tensor'), parts along dimension 0, may hold values from -0.25 to 0.25
- adapter_output_up: bfloat16 [32, 16, 8192], P(('group', 'serve'), None, 'tensor'), parts along dimension 0, may hold values from -1.5 to 1.5
- request_adapter: int32 [16], P('group'), parts along dimension 0, may hold values from 0 to 15, as said below
- adapter_pool_row: int32 [32], P('group'), parts along dimension 0, may hold values from 0 to 15, as said below
- lengths: int32 [16], P(('group', 'serve')), parts along dimension 0, may hold values from 16 to 128
Outputs:
- attention_out: bfloat16 [2048, 8192], P(('group', 'serve'), 'tensor'), parts along dimension 0
There are 2 independent parts, one for each index of `group`. A program takes and returns all parts, laid end to end along the dimension named above; an argument that names none is the same for every part. Nothing has to cross between parts.
Inputs may be any that keep to these rules, and one draw needn't show every extreme that they name: Grouping requests by adapter_pool_row[request_adapter[r]] // 2, no group holds more than 4 requests, and some group holds exactly 4. `adapter_pool_row`: each value appears once.
All inputs are finite; a program needn't handle non-finite values.
Results may differ from a plain program's by a relative error of at most 0.012.
The roundings to bfloat16 on the way count: a program that leaves them out, or rounds other values in their place, can miss the bound.
Values may be sent and summed in bfloat16 or wider, within the bound.
No kernel may reach another device: no remote copies, remote signals or barrier semaphores. Data moves between devices by JAX's collectives and lax.ppermute only.
A program may use at most 128 MiB of HBM per device.

v0:
```python
import jax
import jax.numpy as jnp
from jax import lax
from jax.sharding import PartitionSpec as P

HEAD_SIZE = 128


def for_sending(x):

    def short(part):
        return part.astype(jnp.bfloat16) if part.dtype == jnp.float32 else part

    return jax.tree.map(short, x)


def rotate(vectors):
    rows_count, width = vectors.shape
    half_width = width // 2
    freqs = 500000.0 ** (-(jnp.arange(half_width, dtype=jnp.float32) * 2.0 / width))
    angles = jnp.arange(rows_count, dtype=jnp.float32)[:, None] * freqs[None, :]
    cosine = jnp.cos(angles)
    sine_part = jnp.sin(angles)
    first = vectors[:, :half_width]
    second = vectors[:, half_width:]
    return jnp.concatenate(
        [first * cosine - second * sine_part, second * cosine + first * sine_part], axis=1
    )


def attend(query_rows, key_rows, value_rows, length):
    rows_count = query_rows.shape[0]
    scores = lax.dot_general(
        query_rows, key_rows, (((1,), (1,)), ((), ())), preferred_element_type=jnp.float32
    ) * query_rows.shape[1] ** (-0.5)
    positions = jnp.arange(rows_count)
    allowed = (positions[None, :] <= positions[:, None]) & (positions[None, :] < length)
    scores = jnp.where(allowed, scores, -1e30)
    highest = jnp.max(scores, axis=1, keepdims=True)
    expo = jnp.exp(scores - highest)
    weights = (expo / jnp.sum(expo, axis=1, keepdims=True)).astype(jnp.bfloat16)
    return jnp.dot(weights, value_rows, preferred_element_type=jnp.float32).astype(jnp.bfloat16)


def masked_take(member, picks, keep):
    return jnp.where(
        keep[:, None, None], jnp.take(member, picks, axis=0), jnp.zeros((), member.dtype)
    )


def local(
    tokens,
    query_weight,
    key_value_weight,
    output_weight,
    adapter_down_maps,
    adapter_query_up,
    adapter_key_value_up,
    adapter_output_down,
    adapter_output_up,
    request_adapter,
    adapter_pool_row,
    lengths,
):
    server = lax.axis_index("serve")
    tensor_index = lax.axis_index("tensor")
    held_locally = adapter_down_maps.shape[0]
    wanted = adapter_pool_row[request_adapter]
    owners = wanted // held_locally
    local_slot = wanted % held_locally
    group_members = (
        adapter_down_maps,
        adapter_query_up,
        adapter_key_value_up,
        adapter_output_down,
        adapter_output_up,
    )
    mine = owners == server
    incoming = lax.all_to_all(
        for_sending(tuple((masked_take(member, local_slot, mine) for member in group_members))),
        "serve",
        split_axis=0,
        concat_axis=0,
        tiled=True,
    )
    source = owners[server]
    fetched = [lax.dynamic_index_in_dim(member, source, 0, keepdims=False) for member in incoming]
    down_map_rows, query_up_map, key_value_up, output_down, output_up = fetched
    all_rows = lax.all_gather(tokens, "tensor", axis=1, tiled=True)
    half_width = down_map_rows.shape[1]
    model_cols = lax.dynamic_slice_in_dim(all_rows, tensor_index * half_width, half_width, 1)
    partial_shrink = lax.dot_general(
        model_cols, down_map_rows, (((1,), (1,)), ((), ())), preferred_element_type=jnp.float32
    )
    shrink = lax.psum(partial_shrink, "tensor").astype(jnp.bfloat16)
    low_rank = output_down.shape[0]
    query_all = jnp.dot(all_rows, query_weight, preferred_element_type=jnp.float32) + jnp.dot(
        shrink[:, :low_rank], query_up_map, preferred_element_type=jnp.float32
    )
    pair_shrink = lax.dynamic_slice_in_dim(shrink, low_rank + tensor_index * low_rank, low_rank, 1)
    own_part = (
        jnp.dot(all_rows, key_value_weight, preferred_element_type=jnp.float32)
        + jnp.dot(pair_shrink, key_value_up, preferred_element_type=jnp.float32)
    ).astype(jnp.bfloat16)
    both_parts = lax.all_gather(own_part, "tensor", axis=1, tiled=True)
    key_rows = rotate(both_parts[:, :HEAD_SIZE].astype(jnp.float32)).astype(jnp.bfloat16)
    value_rows = both_parts[:, HEAD_SIZE:]
    heads_here = query_weight.shape[1] // HEAD_SIZE
    attended_list = []
    for head in range(heads_here):
        query_rows = rotate(query_all[:, head * HEAD_SIZE : (head + 1) * HEAD_SIZE]).astype(
            jnp.bfloat16
        )
        attended_list.append(attend(query_rows, key_rows, value_rows, lengths[0]))
    attended = jnp.concatenate(attended_list, axis=1)
    partial_out = jnp.dot(attended, output_weight, preferred_element_type=jnp.float32)
    base_out = lax.psum_scatter(
        partial_out.astype(jnp.bfloat16), "tensor", scatter_dimension=1, tiled=True
    ).astype(jnp.float32)
    partial_low = lax.dot_general(
        attended, output_down, (((1,), (1,)), ((), ())), preferred_element_type=jnp.float32
    )
    low_out = lax.psum(partial_low, "tensor").astype(jnp.bfloat16)
    delta_out = jnp.dot(low_out, output_up, preferred_element_type=jnp.float32)
    valid_rows = (jnp.arange(all_rows.shape[0]) < lengths[0])[:, None]
    return jnp.where(valid_rows, base_out + delta_out, 0.0).astype(jnp.bfloat16)


def solution(mesh):
    placed = (
        P(("group", "serve"), "tensor"),
        P(None, "tensor"),
        P(None, "tensor"),
        P("tensor", None),
        P(("group", "serve"), None, "tensor"),
        P(("group", "serve"), None, "tensor"),
        P(("group", "serve"), None, "tensor"),
        P(("group", "serve"), None, "tensor"),
        P(("group", "serve"), None, "tensor"),
        P("group"),
        P("group"),
        P(("group", "serve")),
    )
    return jax.shard_map(
        local,
        mesh=mesh,
        in_specs=placed,
        out_specs=P(("group", "serve"), "tensor"),
        check_vma=False,
    )
```

profile of v0, /device:TPU:0, one launch (start us, length us, event | category | flops | bytes accessed | tf_op | source)
XLA Modules:
  0.0 171.0 jit_solution(3683610692139840472)
XLA Ops:
  6.5 0.8 compare_select_fusion.2
  7.4 1.3 gather_fusion
  8.7 3.6 %gather_fusion.1 = bf16[8,48,4096]{2,1,0:T(8,128)(2,1)} fusion(bf16[2,48,4096]{2,1,0:T(8,128)(2,1)} %param.18, s32[1024]{0:T(1024)S(1)} %pad_clamp_fusion.1), kind=kCustom, calls=%fused_computation.3 | custom fusion | bytes 6291488 | tf_op jit(solution)/shard_map/jit(_take)/gather | solution.py:47
  12.3 4.0 %select_select_fusion = bf16[8,48,4096]{2,1,0:T(8,128)(2,1)} fusion(bf16[8,48,4096]{2,1,0:T(8,128)(2,1)} %gather_fusion.1, pred[8]{0:T(512)(128)(4,1)S(1)} %get-tuple-element.20, pred[8]{0:T(512)(128)(4,1)S(1)} %get-tuple-element.6), kind=kLoop, calls=%fused_computation.10 | loop fusion | flops 3145728 | bytes 6291472 | tf_op jit(solution)/shard_map/jit(_where)/select_n | solution.py:46
  16.3 7.4 %all-to-all-start = ((bf16[8,48,4096]{2,1,0:T(8,128)(2,1)}), bf16[8,48,4096]{2,1,0:T(8,128)(2,1)}, u32[]{:S(2)}, u32[]{:S(2)}) async-start(bf16[8,48,4096]{2,1,0:T(8,128)(2,1)} %select_select_fusion), calls=%async_computation | async-start | bytes 6291456 | tf_op jit(solution)/shard_map/all_to_all | solution.py:79
  23.7 0.7 all-gather.2.cloned.1.call-update
  24.4 0.6 dynamic_slice.29
  26.3 0.6 gather_fusion.4
  26.9 0.6 gather_fusion.5
  27.5 0.6 gather_fusion.2
  29.3 0.7 select_select_fusion.4
  30.0 0.7 select_select_fusion.2
  30.8 7.3 %all-gather.2.cloned.1.call-done = bf16[128,8192]{1,0:T(8,128)(2,1)} async-done(((bf16[128,4096]{1,0:T(8,128)(2,1)}), bf16[128,8192]{1,0:T(8,128)(2,1)}) %all-gather.2.cloned.1.call-update) | async-done | bytes 2097168 | tf_op jit(solution)/shard_map/all_gather | solution.py:89
  38.1 2.3 %fusion.52 = f32[128,128]{1,0:T(8,128)S(1)} fusion(bf16[128,8192]{1,0:T(8,128)(2,1)} %all-gather.2.cloned.1.call-done, bf16[8192,128]{1,0:T(8,128)(2,1)S(1)} %copy-done), kind=kOutput, calls=%fused_computation.104 | convolution fusion | flops 268435456 | bytes 4259840 | tf_op jit(solution)/shard_map/dot_general | solution.py:102
  40.4 54.1 %all-to-all-done = bf16[8,48,4096]{2,1,0:T(8,128)(2,1)} async-done(((bf16[8,48,4096]{2,1,0:T(8,128)(2,1)}), bf16[8,48,4096]{2,1,0:T(8,128)(2,1)}, u32[]{:S(2)}, u32[]{:S(2)}) %all-to-all-start) | async-done | bytes 3145760 | tf_op jit(solution)/shard_map/all_to_all | solution.py:79
  94.5 3.6 %all-to-all-start.2 = ((bf16[8,16,128]{2,1,0:T(8,128)(2,1)}), bf16[8,16,128]{2,1,0:T(8,128)(2,1)S(1)}, u32[]{:S(2)}, u32[]{:S(2)}) async-start(bf16[8,16,128]{2,1,0:T(8,128)(2,1)} %select_select_fusion.4), calls=%async_computation.2 | async-start | bytes 65536 | tf_op jit(solution)/shard_map/all_to_all | solution.py:79
  98.1 1.8 %fusion.5 = f32[128,48]{0,1:T(8,128)S(1)} fusion(bf16[128,8192]{1,0:T(8,128)(2,1)} %all-gather.2.cloned.1.call-done, s32[]{:T(128)S(6)} %select_n.117, bf16[8,48,4096]{2,1,0:T(8,128)(2,1)} %all-to-all-done, s32[]{:T(128)S(6)} %select_n.127), kind=kOutput, calls=%fused_computation.21 | convolution fusion | flops 50331648 | bytes 1466376 | tf_op jit(solution)/shard_map/dot_general | solution.py:92
  99.9 3.4 %psum.14 = bf16[128,48]{0,1:T(8,128)(2,1)S(1)} all-reduce(f32[128,48]{0,1:T(8,128)S(1)} %fusion.5), channel_id=1, replica_groups=mesh['group'=2,'serve'=8,'tensor'=2] {'tensor'}, use_global_device_ids=true, to_apply=%region_0.1 | all-reduce | flops 6144 | bytes 36864 | tf_op jit(solution)/shard_map/psum | solution.py:95
  103.3 1.5 all-to-all-done.2
  104.8 4.5 %all-to-all-start.1 = ((bf16[8,16,256]{2,1,0:T(8,128)(2,1)}), bf16[8,16,256]{2,1,0:T(8,128)(2,1)S(1)}, u32[]{:S(2)}, u32[]{:S(2)}) async-start(bf16[8,16,256]{2,1,0:T(8,128)(2,1)} %get-tuple-element.17), calls=%async_computation.1 | async-start | bytes 131072 | tf_op jit(solution)/shard_map/all_to_all | solution.py:79
  109.6 1.9 %all_gather.7 = bf16[128,256]{1,0:T(8,128)(2,1)S(1)} all-gather(bf16[128,128]{1,0:T(8,128)(2,1)S(1)} %fusion.4), channel_id=1, replica_groups=mesh['group'=2,'serve'=8,'tensor'=2] {'tensor'}, dimensions={1}, use_global_device_ids=true | all-gather | bytes 98304 | tf_op jit(solution)/shard_map/all_gather | solution.py:105
  111.5 4.8 %all-to-all-done.1 = bf16[8,16,256]{2,1,0:T(8,128)(2,1)S(1)} async-done(((bf16[8,16,256]{2,1,0:T(8,128)(2,1)}), bf16[8,16,256]{2,1,0:T(8,128)(2,1)S(1)}, u32[]{:S(2)}, u32[]{:S(2)}) %all-to-all-start.1) | async-done | bytes 65568 | tf_op jit(solution)/shard_map/all_to_all | solution.py:79
  116.5 3.7 %convolution_add_fusion.1 = f32[128,256]{1,0:T(8,128)S(1)} fusion(f32[128,256]{1,0:T(8,128)S(1)} %fusion.31, bf16[128,8192]{1,0:T(8,128)(2,1)} %all-gather.2.cloned.1.call-done, bf16[8192,256]{1,0:T(8,128)(2,1)} %param.15), kind=kOutput, calls=%fused_computation.11 | convolution fusion | flops 536903680 | bytes 6553600 | tf_op jit(solution)/shard_map/dot_general | solution.py:97
  121.5 2.1 %convolution_convert_fusion = bf16[128,8192]{1,0:T(8,128)(2,1)} fusion(bf16[256,8192]{1,0:T(8,128)(2,1)S(1)} %copy-done.2, bf16[128,128]{0,1:T(8,128)(2,1)S(1)} %convolution_convert_fusion.1, bf16[128,128]{0,1:T(8,128)(2,1)S(1)} %convolution_convert_fusion.2), kind=kOutput, calls=%fused_computation.6 | convolution fusion | flops 538050560 | bytes 6356992 | tf_op jit(solution)/shard_map/dot_general | solution.py:116
  123.7 3.4 %all-to-all-start.3 = ((bf16[8,16,256]{2,1,0:T(8,128)(2,1)}), bf16[8,16,256]{2,1,0:T(8,128)(2,1)S(1)}, u32[]{:S(2)}, u32[]{:S(2)}) async-start(bf16[8,16,256]{2,1,0:T(8,128)(2,1)} %get-tuple-element.16), calls=%async_computation.4 | async-start | bytes 131072 | tf_op jit(solution)/shard_map/all_to_all | solution.py:79
  127.0 0.6 gather_fusion.3
  127.7 1.2 select_select_fusion.1
  128.8 5.1 %all-to-all-done.3 = bf16[8,16,256]{2,1,0:T(8,128)(2,1)S(1)} async-done(((bf16[8,16,256]{2,1,0:T(8,128)(2,1)}), bf16[8,16,256]{2,1,0:T(8,128)(2,1)S(1)}, u32[]{:S(2)}, u32[]{:S(2)}) %all-to-all-start.3) | async-done | bytes 65568 | tf_op jit(solution)/shard_map/all_to_all | solution.py:79
  133.9 3.6 %all-to-all-start.4 = ((bf16[8,16,4096]{2,1,0:T(8,128)(2,1)}), bf16[8,16,4096]{2,1,0:T(8,128)(2,1)S(1)}, u32[]{:S(2)}, u32[]{:S(2)}) async-start(bf16[8,16,4096]{2,1,0:T(8,128)(2,1)} %select_select_fusion.1), calls=%async_computation.5 | async-start | bytes 2097152 | tf_op jit(solution)/shard_map/all_to_all | solution.py:79
  137.6 3.6 %psum.15 = bf16[128,16]{1,0:T(8,128)(2,1)S(1)} all-reduce(f32[128,16]{1,0:T(8,128)S(1)} %fusion.16), channel_id=1, replica_groups=mesh['group'=2,'serve'=8,'tensor'=2] {'tensor'}, use_global_device_ids=true, to_apply=%region_6.8 | all-reduce | flops 2048 | bytes 12288 | tf_op jit(solution)/shard_map/psum | solution.py:123
  141.2 20.3 %all-to-all-done.4 = bf16[8,16,4096]{2,1,0:T(8,128)(2,1)S(1)} async-done(((bf16[8,16,4096]{2,1,0:T(8,128)(2,1)}), bf16[8,16,4096]{2,1,0:T(8,128)(2,1)S(1)}, u32[]{:S(2)}, u32[]{:S(2)}) %all-to-all-start.4) | async-done | bytes 1048608 | tf_op jit(solution)/shard_map/all_to_all | solution.py:79
  161.5 2.6 %fusion.1 = bf16[128,4096]{1,0:T(8,128)(2,1)} fusion(bf16[128,4096]{1,0:T(8,128)(2,1)} %reduce-scatter.2.cloned.1.call-done, pred[128]{0:T(512)(128)(4,1)S(1)} %iota_compare_fusion.1, bf16[8,16,4096]{2,1,0:T(8,128)(2,1)S(1)} %all-to-all-done.4, s32[]{:T(128)S(6)} %select_n.127, bf16[128,16]{1,0:T(8,128)(2,1)S(1)} %psum.15), kind=kOutput, calls=%fused_computation.9 | convolution fusion | flops 18874368 | bytes 2261508 | tf_op jit(solution)/shard_map/dot_general | solution.py:124
  (34 shorter events, 2.1 us)
Async XLA Ops:
  6.5 31.5 %copy-start = (bf16[8192,128]{1,0:T(8,128)(2,1)S(1)}, bf16[8192,128]{1,0:T(8,128)(2,1)}, u32[]{:S(2)}) copy-start(bf16[8192,128]{1,0:T(8,128)(2,1)} %param.16) | copy-start | bytes 6291460
  16.2 10.1 %copy-start.3 = (bf16[2,16,256]{2,1,0:T(8,128)(2,1)S(1)}, bf16[2,16,256]{2,1,0:T(8,128)(2,1)}, u32[]{:S(2)}) copy-start(bf16[2,16,256]{2,1,0:T(8,128)(2,1)} %param.19) | copy-start | bytes 49156
  16.2 10.6 %copy-start.4 = (bf16[2,16,256]{2,1,0:T(8,128)(2,1)S(1)}, bf16[2,16,256]{2,1,0:T(8,128)(2,1)}, u32[]{:S(2)}) copy-start(bf16[2,16,256]{2,1,0:T(8,128)(2,1)} %param.21) | copy-start | bytes 49156
  16.2 11.2 %copy-start.5 = (bf16[2,16,128]{2,1,0:T(8,128)(2,1)S(1)}, bf16[2,16,128]{2,1,0:T(8,128)(2,1)}, u32[]{:S(2)}) copy-start(bf16[2,16,128]{2,1,0:T(8,128)(2,1)} %param.20) | copy-start | bytes 24580
  16.3 78.2 %all-to-all-start = ((bf16[8,48,4096]{2,1,0:T(8,128)(2,1)}), bf16[8,48,4096]{2,1,0:T(8,128)(2,1)}, u32[]{:S(2)}, u32[]{:S(2)}) async-start(bf16[8,48,4096]{2,1,0:T(8,128)(2,1)} %select_select_fusion), calls=%async_computation | async-start | bytes 6291456 | tf_op jit(solution)/shard_map/all_to_all | solution.py:79
  23.7 14.4 %all-gather.2.cloned.1.call-start = ((), (), s32[]{:S(2)}) async-start(), calls=%async_computation.6 | async-start | bytes 3145728 | tf_op jit(solution)/shard_map/all_gather | solution.py:89
  94.5 10.3 %all-to-all-start.2 = ((bf16[8,16,128]{2,1,0:T(8,128)(2,1)}), bf16[8,16,128]{2,1,0:T(8,128)(2,1)S(1)}, u32[]{:S(2)}, u32[]{:S(2)}) async-start(bf16[8,16,128]{2,1,0:T(8,128)(2,1)} %select_select_fusion.4), calls=%async_computation.2 | async-start | bytes 65536 | tf_op jit(solution)/shard_map/all_to_all | solution.py:79
  104.8 11.4 %all-to-all-start.1 = ((bf16[8,16,256]{2,1,0:T(8,128)(2,1)}), bf16[8,16,256]{2,1,0:T(8,128)(2,1)S(1)}, u32[]{:S(2)}, u32[]{:S(2)}) async-start(bf16[8,16,256]{2,1,0:T(8,128)(2,1)} %get-tuple-element.17), calls=%async_computation.1 | async-start | bytes 131072 | tf_op jit(solution)/shard_map/all_to_all | solution.py:79
  109.3 52.2 %reduce-scatter.2.cloned.1.call-start = ((), (), s32[]{:S(2)}) async-start(), calls=%async_computation.7 | async-start | bytes 3145728 | tf_op jit(solution)/shard_map/reduce_scatter | solution.py:117
  116.4 5.1 %copy-start.2 = (bf16[256,8192]{1,0:T(8,128)(2,1)S(1)}, bf16[256,8192]{1,0:T(8,128)(2,1)}, u32[]{:S(2)}) copy-start(bf16[256,8192]{1,0:T(8,128)(2,1)} %param.17) | copy-start | bytes 12582916
  121.5 5.5 %copy-start.1 = (bf16[2,16,4096]{2,1,0:T(8,128)(2,1)S(1)}, bf16[2,16,4096]{2,1,0:T(8,128)(2,1)}, u32[]{:S(2)}) copy-start(bf16[2,16,4096]{2,1,0:T(8,128)(2,1)} %param.22) | copy-start | bytes 786436
  123.7 10.2 %all-to-all-start.3 = ((bf16[8,16,256]{2,1,0:T(8,128)(2,1)}), bf16[8,16,256]{2,1,0:T(8,128)(2,1)S(1)}, u32[]{:S(2)}, u32[]{:S(2)}) async-start(bf16[8,16,256]{2,1,0:T(8,128)(2,1)} %get-tuple-element.16), calls=%async_computation.4 | async-start | bytes 131072 | tf_op jit(solution)/shard_map/all_to_all | solution.py:79
  133.9 27.7 %all-to-all-start.4 = ((bf16[8,16,4096]{2,1,0:T(8,128)(2,1)}), bf16[8,16,4096]{2,1,0:T(8,128)(2,1)S(1)}, u32[]{:S(2)}, u32[]{:S(2)}) async-start(bf16[8,16,4096]{2,1,0:T(8,128)(2,1)} %select_select_fusion.1), calls=%async_computation.5 | async-start | bytes 2097152 | tf_op jit(solution)/shard_map/all_to_all | solution.py:79
Sparse Core Ops, SparseCore 0:
  26.0 11.9 all-gather.1
  123.8 7.1 reduce-scatter.1
where the time goes:
time: 172 us; the launch traced here: 171 us
  waiting for transfers between devices  93.7 us (54%)
  starting transfers between devices  22.6 us (13%)
  between operations  16.2 us (9%)
  matrix products  14 us (8%)
  blocking collectives  8.9 us (5%)
  other arithmetic  7.87 us (5%)
  local copies, waits for them, and re-layouts  7.76 us (5%)
    all_to_all x5, waiting for transfers between devices, local(): lax.all_to_all(for_sending(tuple((masked_take(member, local_slot, mine) f...  85.7 us
    all_to_all x5, starting transfers between devices, local(): lax.all_to_all(for_sending(tuple((masked_take(member, local_slot, mine) f...  22.5 us
    all_gather x1, waiting for transfers between devices, local(): all_rows = lax.all_gather(tokens, 'tensor', axis=1, tiled=True)  7.27 us
    select_n x4, other arithmetic, masked_take(): jnp.where(keep[:, None, None], jnp.take(member, picks, axis=0), jnp.zeros...  6.58 us
    gather x5, local copies, waits for them, and re-layouts, masked_take(): jnp.take(member, picks, axis=0)  5.84 us
    dot_general x1, matrix products, local(): jnp.dot(all_rows, query_weight, preferred_element_type=jnp.float32)  3.68 us
    psum x1, blocking collectives, local(): low_out = lax.psum(partial_low, 'tensor').astype(jnp.bfloat16)  3.62 us
  transfers between devices with their start and end apart: 7, of which 6 were waited for; matrix products, arithmetic and copies ran while one was open for 6% of the time, Pallas kernels for 0%

commit v1 on v0

v1 whole, which is shorter than its diff:
```python
import functools

import jax
import jax.numpy as jnp
import numpy as np
from jax import lax
from jax.experimental import pallas as pl
from jax.experimental.pallas import tpu as pltpu
from jax.sharding import PartitionSpec as P

HEAD_SIZE = 128
MIB = 1 << 20
VMEM = pl.BlockSpec(memory_space=pltpu.VMEM)
SMEM = pl.BlockSpec(memory_space=pltpu.SMEM)
ANY = pl.BlockSpec(memory_space=pl.ANY)


def span(bits):
    masks = [0]
    for bit in bits:
        masks += [mask ^ bit for mask in masks]
    return masks


def params(mib):
    return pltpu.CompilerParams(vmem_limit_bytes=mib * MIB)


def cost(flops, bytes_accessed):
    return pl.CostEstimate(flops=flops, transcendentals=0, bytes_accessed=bytes_accessed)


class Route:
    def __init__(self, part, order, devices, request_adapter, adapter_pool_row):
        self.parts, self.masks = [part], [0]
        self.packets, self.known = [], []
        self.bits = [1 << bit for bit in order]
        self.done = 0
        self.devices = devices
        self.tables = (request_adapter, adapter_pool_row)
        self.held = part.shape[0]

    def arrays(self):
        return self.parts + self.packets

    def choose(self, tables, refs, slot, store):
        requests, pool = tables
        here = lax.axis_index("serve")
        wanted = pool[requests[here ^ slot]]
        offset = (wanted // self.held) ^ here
        for ref, mask in zip(refs, self.masks):

            @pl.when(offset == mask)
            def _(ref=ref):
                store(ref, wanted % self.held)

        for ref, (masks, slots) in zip(refs[len(self.masks):], self.known):
            arrived = functools.reduce(lambda a, b: a | b, [offset == mask for mask in masks])

            @pl.when(arrived)
            def _(ref=ref, slots=slots):
                store(ref, slots.index(slot))

    def step(self, after=()):
        bit = self.bits[self.done]
        slots = span(self.bits[self.done + 1:])
        pairs = [(i, i ^ bit) for i in range(self.devices)]
        out = None
        if not self.known and self.held * len(self.parts) <= len(slots):
            self.parts += [lax.ppermute(part, "serve", pairs) for part in self.parts]
            self.masks += [mask ^ bit for mask in self.masks]
        else:
            out = self.pick([bit ^ slot for slot in slots], after)
            self.packets.append(lax.ppermute(out, "serve", pairs))
            self.known.append(([bit ^ mask for mask in span(self.bits[:self.done])], slots))
        self.done += 1
        return out

    def pick(self, slots, after):
        arrays = self.arrays()
        shape = (len(slots),) + arrays[0].shape[1:]

        def kernel(requests, pool, *refs):
            out = refs[-1]
            for place, slot in enumerate(slots):
                out[place] = refs[0][0]

                def store(ref, index, place=place):
                    out[place] = ref[index]

                self.choose((requests, pool), refs, slot, store)

        return pl.pallas_call(
            kernel,
            in_specs=[SMEM, SMEM] + [VMEM] * len(arrays) + [ANY] * len(after),
            out_specs=VMEM,
            out_shape=jax.ShapeDtypeStruct(shape, arrays[0].dtype),
            compiler_params=params(4),
            cost_estimate=cost(0, 4 * int(np.prod(shape))),
            name="pick",
        )(*self.tables, *arrays, *after)


def base_kernel(tensor, own_tokens, other_tokens, query_weight, key_value_weight, out):
    step = pl.program_id(0)
    steps = pl.num_programs(0)
    width = query_weight.shape[1]

    @pl.when(step == 0)
    def _():
        out[...] = jnp.zeros_like(out)

    def add(rows):
        out[:, :width] += jnp.dot(rows[...], query_weight[...], preferred_element_type=jnp.float32)
        out[:, width:] += jnp.dot(rows[...], key_value_weight[...], preferred_element_type=jnp.float32)

    @pl.when(step < steps // 2)
    def _():
        add(own_tokens)

    @pl.when(step >= steps // 2)
    def _():
        add(other_tokens)


def base_products(tensor, own_tokens, other_tokens, query_weight, key_value_weight):
    rows, half = own_tokens.shape
    blocks = 4
    depth = half // blocks
    columns = query_weight.shape[1] + key_value_weight.shape[1]

    def weight_block(step, tensor):
        own = step < blocks
        return (jnp.where(own, tensor[0], 1 - tensor[0]) * blocks + step % blocks, 0)

    return pl.pallas_call(
        base_kernel,
        grid_spec=pltpu.PrefetchScalarGridSpec(
            num_scalar_prefetch=1,
            grid=(2 * blocks,),
            in_specs=[
                pl.BlockSpec((rows, depth), lambda i, t: (0, jnp.minimum(i, blocks - 1))),
                pl.BlockSpec((rows, depth), lambda i, t: (0, jnp.maximum(i - blocks, 0))),
                pl.BlockSpec((depth, query_weight.shape[1]), weight_block),
                pl.BlockSpec((depth, key_value_weight.shape[1]), weight_block),
            ],
            out_specs=pl.BlockSpec((rows, columns), lambda i, t: (0, 0)),
        ),
        out_shape=jax.ShapeDtypeStruct((rows, columns), jnp.float32),
        compiler_params=params(8),
        cost_estimate=cost(4 * rows * half * columns, 4 * half * (rows + columns)),
        name="base",
    )(tensor, own_tokens, other_tokens, query_weight, key_value_weight)


def shrink_partial(routes, tokens, small_width):
    rows, half = tokens.shape
    rank = routes[0].parts[0].shape[1]
    counts = [len(route.arrays()) for route in routes]
    arrays = sum([route.arrays() for route in routes], [])

    def kernel(requests, pool, rows_ref, *refs):
        inputs, (out, small) = refs[:-2 - len(routes)], refs[-2 - len(routes):-len(routes)]
        held = refs[-len(routes):]
        at = 0
        for place, (route, count) in enumerate(zip(routes, counts)):

            def store(ref, index, place=place):
                held[place][...] = ref[index]

            route.choose((requests, pool), inputs[at:at + count], 0, store)
            at += count
        for place in range(len(routes)):
            out[:, place * rank:(place + 1) * rank] = lax.dot_general(
                rows_ref[...], held[place][:, :half], (((1,), (1,)), ((), ())),
                preferred_element_type=jnp.float32)
        small[...] = held[0][:, half:]

    return pl.pallas_call(
        kernel,
        in_specs=[SMEM, SMEM] + [VMEM] * (1 + len(arrays)),
        out_specs=(VMEM, VMEM),
        out_shape=(
            jax.ShapeDtypeStruct((rows, rank * len(routes)), jnp.float32),
            jax.ShapeDtypeStruct((rank, small_width), tokens.dtype),
        ),
        scratch_shapes=[pltpu.VMEM(route.parts[0].shape[1:], tokens.dtype) for route in routes],
        compiler_params=params(6),
        cost_estimate=cost(2 * rows * half * rank * len(routes), 2 * rows * half),
        name="shrink",
    )(*routes[0].tables, tokens, *arrays)


def rotary_tables(rows, width):
    half = width // 2
    freqs = np.float32(500000.0) ** (-(np.arange(half, dtype=np.float32) * np.float32(2.0) / np.float32(width)))
    angles = np.arange(rows, dtype=np.float32)[:, None] * freqs.astype(np.float32)[None, :]
    cosine, sine = np.cos(angles), np.sin(angles)
    return (
        np.concatenate([cosine, cosine], axis=1).astype(np.float32),
        np.concatenate([-sine, sine], axis=1).astype(np.float32),
    )


def attention_kernel(
    place, base_own, base_other, shrink_own, shrink_other, small_own, small_other, cosine, sine,
    weight_own, weight_other, out, low_out, *, query_columns, key_columns,
):
    tensor, length = place[0], place[1]
    rank = small_own.shape[0]
    rows = out.shape[0]
    size = HEAD_SIZE
    shrink = (shrink_own[...] + shrink_other[...]).astype(jnp.bfloat16)
    first = tensor == 0

    def up(part, base, small, start, base_start, width):
        return base[:, base_start:base_start + width] + jnp.dot(
            part, small[:, start:start + width], preferred_element_type=jnp.float32)

    def rotate(v):
        return v * cosine[...] + pltpu.roll(v, size // 2, 1) * sine[...]

    own_side = shrink[:, rank:2 * rank], shrink[:, 2 * rank:3 * rank]
    own_part = jnp.where(first, own_side[0], own_side[1])
    other_part = jnp.where(first, own_side[1], own_side[0])
    own_kv = up(own_part, base_own, small_own, query_columns, query_columns, key_columns).astype(jnp.bfloat16)
    other_kv = up(other_part, base_other, small_other, query_columns, query_columns, key_columns).astype(jnp.bfloat16)
    keys = jnp.where(first, own_kv, other_kv)
    values = jnp.where(first, other_kv, own_kv)
    keys = rotate(keys.astype(jnp.float32)).astype(jnp.bfloat16)

    at = lax.broadcasted_iota(jnp.int32, (rows, rows), 0)
    to = lax.broadcasted_iota(jnp.int32, (rows, rows), 1)
    allowed = (to <= at) & (to < length)

    def heads(base, small):
        queries = up(shrink[:, :rank], base, small, 0, 0, query_columns)
        done = []
        for start in range(0, query_columns, size):
            query = rotate(queries[:, start:start + size]).astype(jnp.bfloat16)
            scores = lax.dot_general(
                query, keys, (((1,), (1,)), ((), ())), preferred_element_type=jnp.float32) * size ** (-0.5)
            scores = jnp.where(allowed, scores, -1e30)
            expo = jnp.exp(scores - jnp.max(scores, axis=1, keepdims=True))
            weights = (expo / jnp.sum(expo, axis=1, keepdims=True)).astype(jnp.bfloat16)
            done.append(jnp.dot(weights, values, preferred_element_type=jnp.float32).astype(jnp.bfloat16))
        return jnp.concatenate(done, axis=1)

    attended_own = heads(base_own, small_own)
    attended_other = heads(base_other, small_other)

    def down(attended, small):
        return lax.dot_general(
            attended, small[:, query_columns + key_columns:], (((1,), (1,)), ((), ())),
            preferred_element_type=jnp.float32)

    low_out[...] = (down(attended_own, small_own) + down(attended_other, small_other)).astype(jnp.bfloat16)
    columns = out.shape[1]
    tile = 512
    for start in range(0, columns, tile):
        cut = slice(start, start + tile)
        own = jnp.dot(attended_own, weight_own[:, cut], preferred_element_type=jnp.float32)
        other = jnp.dot(attended_other, weight_other[:, cut], preferred_element_type=jnp.float32)
        out[:, cut] = own.astype(jnp.bfloat16).astype(jnp.float32) + other.astype(jnp.bfloat16).astype(jnp.float32)


def attention(place, base, shrink, small, weight, query_columns, key_columns):
    rows = base[0].shape[0]
    columns = weight[0].shape[1]
    rank = small[0].shape[0]
    cosine, sine = rotary_tables(rows, HEAD_SIZE)
    operands = (*base, *shrink, *small, cosine, sine, *weight)
    return pl.pallas_call(
        functools.partial(attention_kernel, query_columns=query_columns, key_columns=key_columns),
        in_specs=[SMEM] + [VMEM] * len(operands),
        out_specs=(VMEM, VMEM),
        out_shape=(
            jax.ShapeDtypeStruct((rows, columns), jnp.float32),
            jax.ShapeDtypeStruct((rows, rank), jnp.bfloat16),
        ),
        compiler_params=params(16),
        cost_estimate=cost(4 * rows * query_columns * columns, 4 * query_columns * columns),
        name="attention",
    )(place, *operands)


def finish(route, place, base, low):
    rows, columns = base.shape
    arrays = route.arrays()

    def kernel(requests, pool, place, base_ref, low_ref, *refs):
        inputs, out, held = refs[:len(arrays)], refs[-2], refs[-1]

        def store(ref, index):
            held[...] = ref[index]

        route.choose((requests, pool), inputs, 0, store)
        valid = lax.broadcasted_iota(jnp.int32, (rows, 1), 0) < place[1]
        tile = 512
        for start in range(0, columns, tile):
            cut = slice(start, start + tile)
            delta = jnp.dot(low_ref[...], held[:, cut], preferred_element_type=jnp.float32)
            out[:, cut] = jnp.where(valid, base_ref[:, cut] + delta, 0.0).astype(out.dtype)

    return pl.pallas_call(
        kernel,
        in_specs=[SMEM, SMEM, SMEM] + [VMEM] * (2 + len(arrays)),
        out_specs=VMEM,
        out_shape=jax.ShapeDtypeStruct((rows, columns), jnp.bfloat16),
        scratch_shapes=[pltpu.VMEM(arrays[0].shape[1:], arrays[0].dtype)],
        compiler_params=params(8),
        cost_estimate=cost(2 * rows * low.shape[1] * columns, 6 * rows * columns),
        name="finish",
    )(*route.tables, place, base, low, *arrays)


def orders(bits):
    each = list(range(bits))
    first = each
    second = [1, 0] + each[2:] if bits > 1 else each
    third = [each[-1]] + each[:-1]
    return first, second, third


def local(
    devices,
    tokens,
    query_weight,
    key_value_weight,
    output_weight,
    adapter_down_maps,
    adapter_query_up,
    adapter_key_value_up,
    adapter_output_down,
    adapter_output_up,
    request_adapter,
    adapter_pool_row,
    lengths,
):
    tensor = lax.axis_index("tensor")
    pair = [(0, 1), (1, 0)]
    half = tokens.shape[1]
    rank = adapter_query_up.shape[1]
    query_columns = query_weight.shape[1]
    key_columns = key_value_weight.shape[1]
    place = jnp.stack([tensor, lengths[0]]).astype(jnp.int32)

    def swap(x):
        return lax.ppermute(x, "tensor", pair)

    small = jnp.concatenate([adapter_query_up, adapter_key_value_up, adapter_output_down], axis=2)
    first, second, third = orders(devices.bit_length() - 1)

    def route(part, order):
        return Route(part, order, devices, request_adapter, adapter_pool_row)

    down = [adapter_down_maps[:, i * rank:(i + 1) * rank] for i in range(3)]
    routes = [
        route(jnp.concatenate([down[0], small], axis=2), first),
        route(down[1], second),
        route(down[2], third),
    ]
    up_route = route(adapter_output_up, first)
    for _ in range(devices.bit_length() - 1):
        for each in (*routes, up_route):
            each.step()

    other_tokens = swap(tokens)
    base_own = base_products(place, tokens, other_tokens, query_weight, key_value_weight)
    base_other = swap(base_own)
    weight_own = lax.dynamic_slice_in_dim(output_weight, tensor * half, half, 1)
    weight_other = swap(lax.dynamic_slice_in_dim(output_weight, (1 - tensor) * half, half, 1))

    shrink_own, small_own = shrink_partial(routes, tokens, small.shape[2])
    base, low = attention(
        place, (base_own, base_other), (shrink_own, swap(shrink_own)), (small_own, swap(small_own)),
        (weight_own, weight_other), query_columns, key_columns)
    return finish(up_route, place, base, low)


def solution(mesh):
    placed = (
        P(("group", "serve"), "tensor"),
        P(None, "tensor"),
        P(None, "tensor"),
        P("tensor", None),
        P(("group", "serve"), None, "tensor"),
        P(("group", "serve"), None, "tensor"),
        P(("group", "serve"), None, "tensor"),
        P(("group", "serve"), None, "tensor"),
        P(("group", "serve"), None, "tensor"),
        P("group"),
        P("group"),
        P(("group", "serve")),
    )
    return jax.shard_map(
        functools.partial(local, mesh.shape["serve"]),
        mesh=mesh,
        in_specs=placed,
        out_specs=P(("group", "serve"), "tensor"),
        check_vma=False,
    )
```

time: 172 us -> 71 us (0.41)
  waiting for transfers between devices: 93.7 us -> 33.7 us
  between operations: 16.2 us -> 0.95 us
  Pallas kernels: 0 us -> 14.4 us
  matrix products: 14 us -> 0 us
  blocking collectives: 8.9 us -> 0 us
  other arithmetic: 7.87 us -> 0.1 us
  local copies, waits for them, and re-layouts: 7.76 us -> 2.97 us
  starting transfers between devices: 22.6 us -> 18.7 us
    all_to_all x5 -> x0, waiting for transfers between devices: 85.7 us -> none  [local(): lax.all_to_all(for_sending(tuple((masked_take(member, local_slot, mine) f...]
    ppermute x0 -> x17, waiting for transfers between devices: none -> 33.7 us  [the longest x8 17.7 us: step(): self.packets.append(lax.ppermute(out, 'serve', pairs))]
    all_to_all x5 -> x0, starting transfers between devices: 22.5 us -> none  [local(): lax.all_to_all(for_sending(tuple((masked_take(member, local_slot, mine) f...]
    ppermute x0 -> x17, starting transfers between devices: none -> 18.7 us  [the longest x8 9.82 us: step(): self.packets.append(lax.ppermute(out, 'serve', pairs))]
    pallas_call x0 -> x12, Pallas kernels: none -> 14.4 us  [the longest x8 4.74 us: pick(): pl.pallas_call(kernel, in_specs=[SMEM, SMEM] + [VMEM] * len(arrays) + [AN...]
    dot_general x12 -> x0, matrix products: 14 us -> none  [the longest x1 3.68 us: local(): jnp.dot(all_rows, query_weight, preferred_element_type=jnp.float32)]
    select_n x6 -> x0, other arithmetic: 7.4 us -> none  [the longest x4 6.58 us: masked_take(): jnp.where(keep[:, None, None], jnp.take(member, picks, axis=0), jnp.zeros...]
    all_gather x1 -> x0, waiting for transfers between devices: 7.27 us -> none  [local(): all_rows = lax.all_gather(tokens, 'tensor', axis=1, tiled=True)]
  transfers between devices with their start and end apart: 7 -> 17, of which waited for: 6 -> 5; matrix products, arithmetic and copies ran while one was open for 6% -> 0% of each run, Pallas kernels for 0% -> 18%
where the time goes in v1:
time: 71 us; the launch traced here: 70.8 us
  waiting for transfers between devices  33.7 us (47%)
  starting transfers between devices  18.7 us (26%)
  Pallas kernels  14.4 us (20%)
  local copies, waits for them, and re-layouts  2.97 us (4%)
  between operations  0.95 us (1%)
    ppermute x8, waiting for transfers between devices, step(): self.packets.append(lax.ppermute(out, 'serve', pairs))  17.7 us
    ppermute x4, waiting for transfers between devices, step(): self.parts += [lax.ppermute(part, 'serve', pairs) for part in self.parts]  15.1 us
    ppermute x8, starting transfers between devices, step(): self.packets.append(lax.ppermute(out, 'serve', pairs))  9.82 us
    ppermute x4, starting transfers between devices, step(): self.parts += [lax.ppermute(part, 'serve', pairs) for part in self.parts]  7.62 us
    pallas_call x8, Pallas kernels, pick(): pl.pallas_call(kernel, in_specs=[SMEM, SMEM] + [VMEM] * len(arrays) + [AN...  4.74 us
    pallas_call x1, Pallas kernels, base_products(): pl.pallas_call(base_kernel, grid_spec=pltpu.PrefetchScalarGridSpec(num_sc...  3.35 us
    dynamic_slice x1, local copies, waits for them, and re-layouts, local(): lax.dynamic_slice_in_dim(output_weight, (1 - tensor) * half, half, 1)  2.86 us
    pallas_call x1, Pallas kernels, attention(): pl.pallas_call(functools.partial(attention_kernel, query_columns=query_co...  2.67 us
  transfers between devices with their start and end apart: 17, of which 5 were waited for; matrix products, arithmetic and copies ran while one was open for 0% of the time, Pallas kernels for 18%

profile of v1, /device:TPU:0, one launch (start us, length us, event | category | flops | bytes accessed | tf_op | source)
XLA Modules:
  0.0 70.8 jit_solution(12360979114167370533)
XLA Ops:
  0.0 2.9 %constant_dynamic-slice_fusion = (bf16[256,4096]{1,0:T(8,128)(2,1)S(1)}, bf16[256,4096]{1,0:T(8,128)(2,1)S(1)}) fusion(bf16[256,8192]{1,0:T(8,128)(2,1)} %param.17, s32[]{:T(128)S(6)} %select_n.7, s32[]{:T(128)S(6)} %select_n.6), kind=kLoop, calls=%fused_computation.2 | loop fusion | bytes 8388616 | tf_op jit(solution)/shard_map/dynamic_slice | solution.py:372
  2.9 0.5 collective-permute-start.13
  3.7 3.0 %collective-permute-start.2 = (bf16[2,16,4736]{2,1,0:T(8,128)(2,1)S(1)}, bf16[2,16,4736]{2,1,0:T(8,128)(2,1)S(1)}, u32[]{:S(2)}, u32[]{:S(2)}) collective-permute-start(bf16[2,16,4736]{2,1,0:T(8,128)(2,1)S(1)} %pad_maximum_fusion.refs_0_), channel_id=1, source_target_pairs={{0,2},{2,0},{4,6},{6,4},{8,10},{10,8},{12,14},{14,12},{1,3},{3,1},... | collective-permute-start | bytes 909320 | tf_op jit(solution)/shard_map/ppermute | solution.py:70
  6.7 2.6 %collective-permute-start.8 = (bf16[2,16,4096]{2,1,0:T(8,128)(2,1)S(1)}, bf16[2,16,4096]{2,1,0:T(8,128)(2,1)S(1)}, u32[]{:S(2)}, u32[]{:S(2)}) collective-permute-start(bf16[2,16,4096]{2,1,0:T(8,128)(2,1)S(1)} %get-tuple-element.15.refs_0_.refs_8_), channel_id=1, source_target_pairs={{0,8},{2,10},{4,12},{6,14},{8,0},{10,2},{12,4},{14,6},{1,9},{3,11}... | collective-permute-start | bytes 786440 | tf_op jit(solution)/shard_map/ppermute | solution.py:70
  9.3 1.6 %collective-permute-start.5 = (bf16[2,16,4096]{2,1,0:T(8,128)(2,1)S(1)}, bf16[2,16,4096]{2,1,0:T(8,128)(2,1)S(1)}, u32[]{:S(2)}, u32[]{:S(2)}) collective-permute-start(bf16[2,16,4096]{2,1,0:T(8,128)(2,1)S(1)} %get-tuple-element.17.refs_0_.refs_4_), channel_id=1, source_target_pairs={{0,4},{2,6},{4,0},{6,2},{8,12},{10,14},{12,8},{14,10},{1,5},{3,7},... | collective-permute-start | bytes 786440 | tf_op jit(solution)/shard_map/ppermute | solution.py:70
  10.8 10.5 %collective-permute-done.8.refs_1_.refs_9_ = bf16[2,16,4096]{2,1,0:T(8,128)(2,1)S(1)} collective-permute-done((bf16[2,16,4096]{2,1,0:T(8,128)(2,1)S(1)}, bf16[2,16,4096]{2,1,0:T(8,128)(2,1)S(1)}, u32[]{:S(2)}, u32[]{:S(2)}) %collective-permute-start.8) | collective-permute-done | bytes 262176 | tf_op jit(solution)/shard_map/ppermute | solution.py:70
  21.3 0.5 collective-permute-start.14
  21.8 0.6 pick.12
  22.4 1.6 %collective-permute-start.9 = (bf16[2,16,4096]{2,1,0:T(8,128)(2,1)S(1)}, bf16[2,16,4096]{2,1,0:T(8,128)(2,1)S(1)}, u32[]{:S(2)}, u32[]{:S(2)}) collective-permute-start(bf16[2,16,4096]{2,1,0:T(8,128)(2,1)S(1)} %pick.12), channel_id=1, source_target_pairs={{0,2},{2,0},{4,6},{6,4},{8,10},{10,8},{12,14},{14,12},{1,3},{3,1},... | collective-permute-start | bytes 786440 | tf_op jit(solution)/shard_map/ppermute | solution.py:74
  24.0 0.6 pick.8
  24.7 0.6 collective-permute-start.3
  25.3 0.6 pick.10
  25.9 4.7 %collective-permute-done.14.refs_1_ = bf16[2,16,4096]{2,1,0:T(8,128)(2,1)S(1)} collective-permute-done((bf16[2,16,4096]{2,1,0:T(8,128)(2,1)S(1)}, bf16[2,16,4096]{2,1,0:T(8,128)(2,1)S(1)}, u32[]{:S(2)}, u32[]{:S(2)}) %collective-permute-start.14) | collective-permute-done | bytes 262176 | tf_op jit(solution)/shard_map/ppermute | solution.py:70
  30.6 0.5 collective-permute-start.6
  31.0 0.6 pick.14
  31.6 4.6 %collective-permute-done.9.refs_2_.refs_10_ = bf16[2,16,4096]{2,1,0:T(8,128)(2,1)S(1)} collective-permute-done((bf16[2,16,4096]{2,1,0:T(8,128)(2,1)S(1)}, bf16[2,16,4096]{2,1,0:T(8,128)(2,1)S(1)}, u32[]{:S(2)}, u32[]{:S(2)}) %collective-permute-start.9) | collective-permute-done | bytes 262176 | tf_op jit(solution)/shard_map/ppermute | solution.py:74
  36.2 0.5 collective-permute-start.15
  37.4 0.6 pick.13
  38.0 1.6 %collective-permute-start.10 = (bf16[1,16,4096]{2,1,0:T(8,128)(2,1)S(1)}, bf16[1,16,4096]{2,1,0:T(8,128)(2,1)S(1)}, u32[]{:S(2)}, u32[]{:S(2)}) collective-permute-start(bf16[1,16,4096]{2,1,0:T(8,128)(2,1)S(1)} %pick.13), channel_id=1, source_target_pairs={{0,4},{2,6},{4,0},{6,2},{8,12},{10,14},{12,8},{14,10},{1,5},{3,7},... | collective-permute-start | bytes 393224 | tf_op jit(solution)/shard_map/ppermute | solution.py:74
  39.6 3.4 %base.1.base_own = f32[128,384]{1,0:T(8,128)S(1)} custom-call(s32[2]{0:T(128)S(1)} %pad_add_fusion.tensor.place, bf16[128,4096]{1,0:T(8,128)(2,1)S(1)} %copy-done, bf16[128,4096]{1,0:T(8,128)(2,1)S(1)} %collective-permute-done.other_tokens, bf16[8192,256]{1,0:T(8,128)(2,1)S(1)} %copy-done.1, bf16[8192,128]{1,0:T(8,128)(2,1)S(1)} %copy-done.3), custom_call_target="tpu_custom_call" | custom-call | flops 805306368 | bytes 8388608 | tf_op jit(solution)/shard_map/base/pallas_call | solution.py:136
  43.1 0.6 pick.9
  43.7 1.9 %collective-permute-start.4 = (bf16[1,16,4736]{2,1,0:T(8,128)(2,1)S(1)}, bf16[1,16,4736]{2,1,0:T(8,128)(2,1)S(1)}, u32[]{:S(2)}, u32[]{:S(2)}) collective-permute-start(bf16[1,16,4736]{2,1,0:T(8,128)(2,1)S(1)} %pick.9), channel_id=1, source_target_pairs={{0,8},{2,10},{4,12},{6,14},{8,0},{10,2},{12,4},{14,6},{1,9},{3,11}... | collective-permute-start | bytes 454664 | tf_op jit(solution)/shard_map/ppermute | solution.py:74
  45.6 0.6 pick.11
  46.2 1.1 %collective-permute-start.7 = (bf16[1,16,4096]{2,1,0:T(8,128)(2,1)S(1)}, bf16[1,16,4096]{2,1,0:T(8,128)(2,1)S(1)}, u32[]{:S(2)}, u32[]{:S(2)}) collective-permute-start(bf16[1,16,4096]{2,1,0:T(8,128)(2,1)S(1)} %pick.11), channel_id=1, source_target_pairs={{0,8},{2,10},{4,12},{6,14},{8,0},{10,2},{12,4},{14,6},{1,9},{3,11}... | collective-permute-start | bytes 393224 | tf_op jit(solution)/shard_map/ppermute | solution.py:74
  47.3 0.6 pick.15
  48.0 1.9 %collective-permute-start.16 = (bf16[1,16,4096]{2,1,0:T(8,128)(2,1)S(1)}, bf16[1,16,4096]{2,1,0:T(8,128)(2,1)S(1)}, u32[]{:S(2)}, u32[]{:S(2)}) collective-permute-start(bf16[1,16,4096]{2,1,0:T(8,128)(2,1)S(1)} %pick.15), channel_id=1, source_target_pairs={{0,8},{2,10},{4,12},{6,14},{8,0},{10,2},{12,4},{14,6},{1,9},{3,11}... | collective-permute-start | bytes 393224 | tf_op jit(solution)/shard_map/ppermute | solution.py:74
  49.9 13.1 %collective-permute-done.7.refs_7_ = bf16[1,16,4096]{2,1,0:T(8,128)(2,1)S(1)} collective-permute-done((bf16[1,16,4096]{2,1,0:T(8,128)(2,1)S(1)}, bf16[1,16,4096]{2,1,0:T(8,128)(2,1)S(1)}, u32[]{:S(2)}, u32[]{:S(2)}) %collective-permute-start.7) | collective-permute-done | bytes 131104 | tf_op jit(solution)/shard_map/ppermute | solution.py:74
  63.0 1.7 %shrink.1 = (f32[128,48]{1,0:T(8,128)S(1)}, bf16[16,640]{1,0:T(8,128)(2,1)S(1)}) custom-call(s32[8]{0:T(128)S(1)} %copy-done.6, s32[16]{0:T(128)S(1)} %copy-done.7, bf16[128,4096]{1,0:T(8,128)(2,1)S(1)} %copy-done, bf16[2,16,4736]{2,1,0:T(8,128)(2,1)S(1)} %pad_maximum_fusion.refs_0_, bf16[2,16,4736]{2,1,0:T(8,128)(2,1)S(1)} %collective-permute-done.2.refs_1_, ...), custom_call_target="tpu_custom_call" | custom-call | flops 50331648 | bytes 1048576 | tf_op jit(solution)/shard_map/shrink/pallas_call | solution.py:179
  64.8 0.5 collective-permute-start.12
  65.3 0.8 %collective-permute-done.12.small_other = bf16[16,640]{1,0:T(8,128)(2,1)S(1)} collective-permute-done((bf16[16,640]{1,0:T(8,128)(2,1)S(1)}, bf16[16,640]{1,0:T(8,128)(2,1)S(1)}, u32[]{:S(2)}, u32[]{:S(2)}) %collective-permute-start.12) | collective-permute-done | bytes 20512 | tf_op jit(solution)/shard_map/ppermute | solution.py:349
  66.2 2.7 %attention.1 = (f32[128,4096]{1,0:T(8,128)S(1)}, bf16[128,16]{1,0:T(8,128)(2,1)S(1)}) custom-call(s32[2]{0:T(128)S(1)} %pad_add_fusion.tensor.place, f32[128,384]{1,0:T(8,128)S(1)} %base.1.base_own, f32[128,384]{1,0:T(8,128)S(1)} %collective-permute-done.1.base_other, f32[128,48]{1,0:T(8,128)S(1)} %get-tuple-element.9.shrink_own, ...), custom_call_target="tpu_custom_call" | custom-call | flops 536870912 | bytes 4194304 | tf_op jit(solution)/shard_map/attention/pallas_call | solution.py:273
  68.9 2.0 %finish.1 = bf16[128,4096]{1,0:T(8,128)(2,1)} custom-call(s32[8]{0:T(128)S(1)} %copy-done.6, s32[16]{0:T(128)S(1)} %copy-done.7, s32[2]{0:T(128)S(1)} %pad_add_fusion.tensor.place, f32[128,4096]{1,0:T(8,128)S(1)} %get-tuple-element.11.base_ref, bf16[128,16]{1,0:T(8,128)(2,1)S(1)} %get-tuple-element.12.low_ref, bf16[2,16,4096]{2,1,0:T(8,128)(2,1)S(1)} %copy-done.2, ...), custom_call_target="tpu_custom_call" | custom-call | flops 16777216 | bytes 3145728 | tf_op jit(solution)/shard_map/finish/pallas_call | solution.py:305
  (42 shorter events, 0.5 us)
Async XLA Ops:
  0.0 3.5 %copy-start = (bf16[128,4096]{1,0:T(8,128)(2,1)S(1)}, bf16[128,4096]{1,0:T(8,128)(2,1)}, u32[]{:S(2)}) copy-start(bf16[128,4096]{1,0:T(8,128)(2,1)} %rows_ref.1) | copy-start | bytes 3145732
  0.0 3.6 %copy-start.8 = (bf16[2,48,4096]{2,1,0:T(8,128)(2,1)S(1)}, bf16[2,48,4096]{2,1,0:T(8,128)(2,1)}, u32[]{:S(2)}) copy-start(bf16[2,48,4096]{2,1,0:T(8,128)(2,1)} %param.18) | copy-start | bytes 2359300
  0.0 3.6 %copy-start.9 = (bf16[2,16,256]{2,1,0:T(8,128)(2,1)S(1)}, bf16[2,16,256]{2,1,0:T(8,128)(2,1)}, u32[]{:S(2)}) copy-start(bf16[2,16,256]{2,1,0:T(8,128)(2,1)} %param.21) | copy-start | bytes 49156
  0.0 3.6 %copy-start.10 = (bf16[2,16,256]{2,1,0:T(8,128)(2,1)S(1)}, bf16[2,16,256]{2,1,0:T(8,128)(2,1)}, u32[]{:S(2)}) copy-start(bf16[2,16,256]{2,1,0:T(8,128)(2,1)} %param.19) | copy-start | bytes 49156
  0.0 3.6 %copy-start.11 = (bf16[2,16,128]{2,1,0:T(8,128)(2,1)S(1)}, bf16[2,16,128]{2,1,0:T(8,128)(2,1)}, u32[]{:S(2)}) copy-start(bf16[2,16,128]{2,1,0:T(8,128)(2,1)} %param.20) | copy-start | bytes 24580
  0.0 39.6 %copy-start.3 = (bf16[8192,128]{1,0:T(8,128)(2,1)S(1)}, bf16[8192,128]{1,0:T(8,128)(2,1)}, u32[]{:S(2)}) copy-start(bf16[8192,128]{1,0:T(8,128)(2,1)} %key_value_weight.1) | copy-start | bytes 6291460
  2.9 18.4 %copy-start.2 = (bf16[2,16,4096]{2,1,0:T(8,128)(2,1)S(1)}, bf16[2,16,4096]{2,1,0:T(8,128)(2,1)}, u32[]{:S(2)}) copy-start(bf16[2,16,4096]{2,1,0:T(8,128)(2,1)} %refs_0_.5) | copy-start | bytes 786436
  2.9 18.9 %copy-start.6 = (s32[8]{0:T(128)S(1)}, s32[8]{0:T(128)}, u32[]{:S(2)}) copy-start(s32[8]{0:T(128)} %requests.19) | copy-start | bytes 100
  2.9 18.9 %copy-start.7 = (s32[16]{0:T(128)S(1)}, s32[16]{0:T(128)}, u32[]{:S(2)}) copy-start(s32[16]{0:T(128)} %pool.19) | copy-start | bytes 196
  2.9 63.2 %collective-permute-start.13 = (bf16[256,4096]{1,0:T(8,128)(2,1)S(1)}, bf16[256,4096]{1,0:T(8,128)(2,1)S(1)}, u32[]{:S(2)}, u32[]{:S(2)}) collective-permute-start(bf16[256,4096]{1,0:T(8,128)(2,1)S(1)} %get-tuple-element.13), channel_id=1, source_target_pairs={{0,1},{1,0},{2,3},{3,2},{4,5},{5,4},{6,7},{7,6},{8,9},{9,8},{10,11... | collective-permute-start | bytes 6291464 | tf_op jit(solution)/shard_map/ppermute | solution.py:349
  3.5 34.5 %collective-permute-start = (bf16[128,4096]{1,0:T(8,128)(2,1)S(1)}, bf16[128,4096]{1,0:T(8,128)(2,1)S(1)}, u32[]{:S(2)}, u32[]{:S(2)}) collective-permute-start(bf16[128,4096]{1,0:T(8,128)(2,1)S(1)} %copy-done), channel_id=1, source_target_pairs={{0,1},{1,0},{2,3},{3,2},{4,5},{5,4},{6,7},{7,6},{8,9},{9,8},{10,11... | collective-permute-start | bytes 3145736 | tf_op jit(solution)/shard_map/ppermute | solution.py:349
  3.7 18.7 %collective-permute-start.2 = (bf16[2,16,4736]{2,1,0:T(8,128)(2,1)S(1)}, bf16[2,16,4736]{2,1,0:T(8,128)(2,1)S(1)}, u32[]{:S(2)}, u32[]{:S(2)}) collective-permute-start(bf16[2,16,4736]{2,1,0:T(8,128)(2,1)S(1)} %pad_maximum_fusion.refs_0_), channel_id=1, source_target_pairs={{0,2},{2,0},{4,6},{6,4},{8,10},{10,8},{12,14},{14,12},{1,3},{3,1},... | collective-permute-start | bytes 909320 | tf_op jit(solution)/shard_map/ppermute | solution.py:70
  6.7 14.6 %collective-permute-start.8 = (bf16[2,16,4096]{2,1,0:T(8,128)(2,1)S(1)}, bf16[2,16,4096]{2,1,0:T(8,128)(2,1)S(1)}, u32[]{:S(2)}, u32[]{:S(2)}) collective-permute-start(bf16[2,16,4096]{2,1,0:T(8,128)(2,1)S(1)} %get-tuple-element.15.refs_0_.refs_8_), channel_id=1, source_target_pairs={{0,8},{2,10},{4,12},{6,14},{8,0},{10,2},{12,4},{14,6},{1,9},{3,11}... | collective-permute-start | bytes 786440 | tf_op jit(solution)/shard_map/ppermute | solution.py:70
  9.3 30.3 %copy-start.1 = (bf16[8192,256]{1,0:T(8,128)(2,1)S(1)}, bf16[8192,256]{1,0:T(8,128)(2,1)}, u32[]{:S(2)}) copy-start(bf16[8192,256]{1,0:T(8,128)(2,1)} %query_weight.1) | copy-start | bytes 12582916
  9.3 15.4 %collective-permute-start.5 = (bf16[2,16,4096]{2,1,0:T(8,128)(2,1)S(1)}, bf16[2,16,4096]{2,1,0:T(8,128)(2,1)S(1)}, u32[]{:S(2)}, u32[]{:S(2)}) collective-permute-start(bf16[2,16,4096]{2,1,0:T(8,128)(2,1)S(1)} %get-tuple-element.17.refs_0_.refs_4_), channel_id=1, source_target_pairs={{0,4},{2,6},{4,0},{6,2},{8,12},{10,14},{12,8},{14,10},{1,5},{3,7},... | collective-permute-start | bytes 786440 | tf_op jit(solution)/shard_map/ppermute | solution.py:70
  21.3 9.2 %collective-permute-start.14 = (bf16[2,16,4096]{2,1,0:T(8,128)(2,1)S(1)}, bf16[2,16,4096]{2,1,0:T(8,128)(2,1)S(1)}, u32[]{:S(2)}, u32[]{:S(2)}) collective-permute-start(bf16[2,16,4096]{2,1,0:T(8,128)(2,1)S(1)} %copy-done.2), channel_id=1, source_target_pairs={{0,2},{2,0},{4,6},{6,4},{8,10},{10,8},{12,14},{14,12},{1,3},{3,1},... | collective-permute-start | bytes 786440 | tf_op jit(solution)/shard_map/ppermute | solution.py:70
  22.4 13.8 %collective-permute-start.9 = (bf16[2,16,4096]{2,1,0:T(8,128)(2,1)S(1)}, bf16[2,16,4096]{2,1,0:T(8,128)(2,1)S(1)}, u32[]{:S(2)}, u32[]{:S(2)}) collective-permute-start(bf16[2,16,4096]{2,1,0:T(8,128)(2,1)S(1)} %pick.12), channel_id=1, source_target_pairs={{0,2},{2,0},{4,6},{6,4},{8,10},{10,8},{12,14},{14,12},{1,3},{3,1},... | collective-permute-start | bytes 786440 | tf_op jit(solution)/shard_map/ppermute | solution.py:74
  24.7 18.3 %collective-permute-start.3 = (bf16[2,16,4736]{2,1,0:T(8,128)(2,1)S(1)}, bf16[2,16,4736]{2,1,0:T(8,128)(2,1)S(1)}, u32[]{:S(2)}, u32[]{:S(2)}) collective-permute-start(bf16[2,16,4736]{2,1,0:T(8,128)(2,1)S(1)} %pick.8), channel_id=1, source_target_pairs={{0,4},{2,6},{4,0},{6,2},{8,12},{10,14},{12,8},{14,10},{1,5},{3,7},... | collective-permute-start | bytes 909320 | tf_op jit(solution)/shard_map/ppermute | solution.py:74
  30.6 13.1 %collective-permute-start.6 = (bf16[2,16,4096]{2,1,0:T(8,128)(2,1)S(1)}, bf16[2,16,4096]{2,1,0:T(8,128)(2,1)S(1)}, u32[]{:S(2)}, u32[]{:S(2)}) collective-permute-start(bf16[2,16,4096]{2,1,0:T(8,128)(2,1)S(1)} %pick.10), channel_id=1, source_target_pairs={{0,2},{2,0},{4,6},{6,4},{8,10},{10,8},{12,14},{14,12},{1,3},{3,1},... | collective-permute-start | bytes 786440 | tf_op jit(solution)/shard_map/ppermute | solution.py:74
  36.2 10.0 %collective-permute-start.15 = (bf16[2,16,4096]{2,1,0:T(8,128)(2,1)S(1)}, bf16[2,16,4096]{2,1,0:T(8,128)(2,1)S(1)}, u32[]{:S(2)}, u32[]{:S(2)}) collective-permute-start(bf16[2,16,4096]{2,1,0:T(8,128)(2,1)S(1)} %pick.14), channel_id=1, source_target_pairs={{0,4},{2,6},{4,0},{6,2},{8,12},{10,14},{12,8},{14,10},{1,5},{3,7},... | collective-permute-start | bytes 786440 | tf_op jit(solution)/shard_map/ppermute | solution.py:74
  38.0 9.9 %collective-permute-start.10 = (bf16[1,16,4096]{2,1,0:T(8,128)(2,1)S(1)}, bf16[1,16,4096]{2,1,0:T(8,128)(2,1)S(1)}, u32[]{:S(2)}, u32[]{:S(2)}) collective-permute-start(bf16[1,16,4096]{2,1,0:T(8,128)(2,1)S(1)} %pick.13), channel_id=1, source_target_pairs={{0,4},{2,6},{4,0},{6,2},{8,12},{10,14},{12,8},{14,10},{1,5},{3,7},... | collective-permute-start | bytes 393224 | tf_op jit(solution)/shard_map/ppermute | solution.py:74
  43.0 23.2 %collective-permute-start.1 = (f32[128,384]{1,0:T(8,128)S(1)}, f32[128,384]{1,0:T(8,128)S(1)}, u32[]{:S(2)}, u32[]{:S(2)}) collective-permute-start(f32[128,384]{1,0:T(8,128)S(1)} %base.1.base_own), channel_id=1, source_target_pairs={{0,1},{1,0},{2,3},{3,2},{4,5},{5,4},{6,7},{7,6},{8,9},{9,8},{10,11... | collective-permute-start | bytes 589832 | tf_op jit(solution)/shard_map/ppermute | solution.py:349
  43.7 19.4 %collective-permute-start.4 = (bf16[1,16,4736]{2,1,0:T(8,128)(2,1)S(1)}, bf16[1,16,4736]{2,1,0:T(8,128)(2,1)S(1)}, u32[]{:S(2)}, u32[]{:S(2)}) collective-permute-start(bf16[1,16,4736]{2,1,0:T(8,128)(2,1)S(1)} %pick.9), channel_id=1, source_target_pairs={{0,8},{2,10},{4,12},{6,14},{8,0},{10,2},{12,4},{14,6},{1,9},{3,11}... | collective-permute-start | bytes 454664 | tf_op jit(solution)/shard_map/ppermute | solution.py:74
  46.2 16.8 %collective-permute-start.7 = (bf16[1,16,4096]{2,1,0:T(8,128)(2,1)S(1)}, bf16[1,16,4096]{2,1,0:T(8,128)(2,1)S(1)}, u32[]{:S(2)}, u32[]{:S(2)}) collective-permute-start(bf16[1,16,4096]{2,1,0:T(8,128)(2,1)S(1)} %pick.11), channel_id=1, source_target_pairs={{0,8},{2,10},{4,12},{6,14},{8,0},{10,2},{12,4},{14,6},{1,9},{3,11}... | collective-permute-start | bytes 393224 | tf_op jit(solution)/shard_map/ppermute | solution.py:74
  47.9 18.2 %copy-start.4 = (f32[128,128]{1,0:T(8,128)S(1)}, f32[128,128]{1,0:T(8,128)}, u32[]{:S(2)}) copy-start(f32[128,128]{1,0:T(8,128)} %constant.16.clone.cosine) | copy-start | bytes 196612
  47.9 18.2 %copy-start.5 = (f32[128,128]{1,0:T(8,128)S(1)}, f32[128,128]{1,0:T(8,128)}, u32[]{:S(2)}) copy-start(f32[128,128]{1,0:T(8,128)} %constant.17.clone.sine) | copy-start | bytes 196612
  48.0 20.9 %collective-permute-start.16 = (bf16[1,16,4096]{2,1,0:T(8,128)(2,1)S(1)}, bf16[1,16,4096]{2,1,0:T(8,128)(2,1)S(1)}, u32[]{:S(2)}, u32[]{:S(2)}) collective-permute-start(bf16[1,16,4096]{2,1,0:T(8,128)(2,1)S(1)} %pick.15), channel_id=1, source_target_pairs={{0,8},{2,10},{4,12},{6,14},{8,0},{10,2},{12,4},{14,6},{1,9},{3,11}... | collective-permute-start | bytes 393224 | tf_op jit(solution)/shard_map/ppermute | solution.py:74
  64.7 1.4 %collective-permute-start.11 = (f32[128,48]{1,0:T(8,128)S(1)}, f32[128,48]{1,0:T(8,128)S(1)}, u32[]{:S(2)}, u32[]{:S(2)}) collective-permute-start(f32[128,48]{1,0:T(8,128)S(1)} %get-tuple-element.9.shrink_own), channel_id=1, source_target_pairs={{0,1},{1,0},{2,3},{3,2},{4,5},{5,4},{6,7},{7,6},{8,9},{9,8},{10,11... | collective-permute-start | bytes 73736 | tf_op jit(solution)/shard_map/ppermute | solution.py:349
  64.8 1.3 %collective-permute-start.12 = (bf16[16,640]{1,0:T(8,128)(2,1)S(1)}, bf16[16,640]{1,0:T(8,128)(2,1)S(1)}, u32[]{:S(2)}, u32[]{:S(2)}) collective-permute-start(bf16[16,640]{1,0:T(8,128)(2,1)S(1)} %get-tuple-element.10.small_own), channel_id=1, source_target_pairs={{0,1},{1,0},{2,3},{3,2},{4,5},{5,4},{6,7},{7,6},{8,9},{9,8},{10,11... | collective-permute-start | bytes 61448 | tf_op jit(solution)/shard_map/ppermute | solution.py:349

commit v2 on v1

--- a/solution.py
+++ b/solution.py
@@ -101,7 +101,7 @@
         )(*self.tables, *arrays, *after)
 
 
-def base_kernel(tensor, own_tokens, other_tokens, query_weight, key_value_weight, out):
+def base_kernel(place, own_tokens, other_tokens, query_weight, key_value_weight, out):
     step = pl.program_id(0)
     steps = pl.num_programs(0)
     width = query_weight.shape[1]
@@ -123,15 +123,15 @@
         add(other_tokens)
 
 
-def base_products(tensor, own_tokens, other_tokens, query_weight, key_value_weight):
+def base_products(place, own_tokens, other_tokens, query_weight, key_value_weight):
     rows, half = own_tokens.shape
     blocks = 4
     depth = half // blocks
     columns = query_weight.shape[1] + key_value_weight.shape[1]
 
-    def weight_block(step, tensor):
+    def weight_block(step, place):
         own = step < blocks
-        return (jnp.where(own, tensor[0], 1 - tensor[0]) * blocks + step % blocks, 0)
+        return (jnp.where(own, place[0], 1 - place[0]) * blocks + step % blocks, 0)
 
     return pl.pallas_call(
         base_kernel,
@@ -150,7 +150,7 @@
         compiler_params=params(8),
         cost_estimate=cost(4 * rows * half * columns, 4 * half * (rows + columns)),
         name="base",
-    )(tensor, own_tokens, other_tokens, query_weight, key_value_weight)
+    )(place, own_tokens, other_tokens, query_weight, key_value_weight)
 
 
 def shrink_partial(routes, tokens, small_width):
@@ -204,9 +204,17 @@
 
 def attention_kernel(
     place, base_own, base_other, shrink_own, shrink_other, small_own, small_other, cosine, sine,
-    weight_own, weight_other, out, low_out, *, query_columns, key_columns,
+    weight_own, weight_other, out, low_out, held_own, held_other, sems, *, query_columns, key_columns,
 ):
     tensor, length = place[0], place[1]
+    half = out.shape[1]
+    mine = pl.ds(pl.multiple_of(tensor * half, half), half)
+    fetches = [
+        pltpu.make_async_copy(weight.at[:, mine], held, sems.at[i])
+        for i, (weight, held) in enumerate(((weight_own, held_own), (weight_other, held_other)))
+    ]
+    for fetch in fetches:
+        fetch.start()
     rank = small_own.shape[0]
     rows = out.shape[0]
     size = HEAD_SIZE
@@ -255,29 +263,31 @@
             preferred_element_type=jnp.float32)
 
     low_out[...] = (down(attended_own, small_own) + down(attended_other, small_other)).astype(jnp.bfloat16)
-    columns = out.shape[1]
+    for fetch in fetches:
+        fetch.wait()
     tile = 512
-    for start in range(0, columns, tile):
+    for start in range(0, half, tile):
         cut = slice(start, start + tile)
-        own = jnp.dot(attended_own, weight_own[:, cut], preferred_element_type=jnp.float32)
-        other = jnp.dot(attended_other, weight_other[:, cut], preferred_element_type=jnp.float32)
+        own = jnp.dot(attended_own, held_own[:, cut], preferred_element_type=jnp.float32)
+        other = jnp.dot(attended_other, held_other[:, cut], preferred_element_type=jnp.float32)
         out[:, cut] = own.astype(jnp.bfloat16).astype(jnp.float32) + other.astype(jnp.bfloat16).astype(jnp.float32)
 
 
 def attention(place, base, shrink, small, weight, query_columns, key_columns):
     rows = base[0].shape[0]
-    columns = weight[0].shape[1]
+    heads, columns = weight[0].shape[0], weight[0].shape[1] // 2
     rank = small[0].shape[0]
     cosine, sine = rotary_tables(rows, HEAD_SIZE)
     operands = (*base, *shrink, *small, cosine, sine, *weight)
     return pl.pallas_call(
         functools.partial(attention_kernel, query_columns=query_columns, key_columns=key_columns),
-        in_specs=[SMEM] + [VMEM] * len(operands),
+        in_specs=[SMEM] + [VMEM] * (len(operands) - 2) + [ANY] * 2,
         out_specs=(VMEM, VMEM),
         out_shape=(
             jax.ShapeDtypeStruct((rows, columns), jnp.float32),
             jax.ShapeDtypeStruct((rows, rank), jnp.bfloat16),
         ),
+        scratch_shapes=[pltpu.VMEM((heads, columns), weight[0].dtype)] * 2 + [pltpu.SemaphoreType.DMA((2,))],
         compiler_params=params(16),
         cost_estimate=cost(4 * rows * query_columns * columns, 4 * query_columns * columns),
         name="attention",
@@ -355,26 +365,28 @@
         return Route(part, order, devices, request_adapter, adapter_pool_row)
 
     down = [adapter_down_maps[:, i * rank:(i + 1) * rank] for i in range(3)]
-    routes = [
-        route(jnp.concatenate([down[0], small], axis=2), first),
-        route(down[1], second),
-        route(down[2], third),
-    ]
+    first_route = route(jnp.concatenate([down[0], small], axis=2), first)
+    second_route = route(down[1], second)
+    third_route = route(down[2], third)
+    routes = [first_route, second_route, third_route]
     up_route = route(adapter_output_up, first)
-    for _ in range(devices.bit_length() - 1):
-        for each in (*routes, up_route):
-            each.step()
-
+    weight_other = swap(output_weight)
     other_tokens = swap(tokens)
+    for each in (third_route, second_route, first_route, up_route):
+        each.step()
     base_own = base_products(place, tokens, other_tokens, query_weight, key_value_weight)
     base_other = swap(base_own)
-    weight_own = lax.dynamic_slice_in_dim(output_weight, tensor * half, half, 1)
-    weight_other = swap(lax.dynamic_slice_in_dim(output_weight, (1 - tensor) * half, half, 1))
+    last = None
+    for turn, each in enumerate((second_route, first_route, third_route, up_route) * 2):
+        if turn == 0:
+            last = base_own
+        sent = each.step(() if last is None else (last,))
+        last = each.arrays()[-1] if sent is None else sent
 
     shrink_own, small_own = shrink_partial(routes, tokens, small.shape[2])
     base, low = attention(
         place, (base_own, base_other), (shrink_own, swap(shrink_own)), (small_own, swap(small_own)),
-        (weight_own, weight_other), query_columns, key_columns)
+        (output_weight, weight_other), query_columns, key_columns)
     return finish(up_route, place, base, low)
 
 

time: 71 us -> 59.5 us (0.84)
  waiting for transfers between devices: 33.7 us -> 15.6 us
  local copies, waits for them, and re-layouts: 2.97 us -> 6.2 us
  Pallas kernels: 14.4 us -> 16.1 us
  starting transfers between devices: 18.7 us -> 19.5 us
  other arithmetic: 0.1 us -> 0.85 us
    ppermute x4, waiting for transfers between devices: 15.1 us -> 0.01 us  [step(): self.parts += [lax.ppermute(part, 'serve', pairs) for part in self.parts]]
    unnamed x24 -> x20, local copies, waits for them, and re-layouts: 0.06 us -> 5.04 us
    ppermute x8, waiting for transfers between devices: 17.7 us -> 14.8 us  [step(): self.packets.append(lax.ppermute(out, 'serve', pairs))]
    dynamic_slice x1 -> x0, local copies, waits for them, and re-layouts: 2.86 us -> none  [local(): lax.dynamic_slice_in_dim(output_weight, (1 - tensor) * half, half, 1)]
    pallas_call x1, Pallas kernels: 2.67 us -> 4.31 us  [attention(): pl.pallas_call(functools.partial(attention_kernel, query_columns=query_co...]
    slice x1, local copies, waits for them, and re-layouts: 0.05 us -> 1.16 us  [local(): down = [adapter_down_maps[:, i * rank:(i + 1) * rank] for i in range(3)]]
    concatenate x1, other arithmetic: 0.02 us -> 0.78 us  [local(): first_route = route(jnp.concatenate([down[0], small], axis=2), first)]
    ppermute x4, starting transfers between devices: 7.62 us -> 8.36 us  [step(): self.parts += [lax.ppermute(part, 'serve', pairs) for part in self.parts]]
  transfers between devices with their start and end apart: 17 -> 17, of which waited for: 5 -> 6; matrix products, arithmetic and copies ran while one was open for 0% -> 3% of each run, Pallas kernels for 18% -> 24%
where the time goes in v2:
time: 59.5 us; the launch traced here: 59.1 us
  starting transfers between devices  19.5 us (33%)
  Pallas kernels  16.1 us (27%)
  waiting for transfers between devices  15.6 us (26%)
  local copies, waits for them, and re-layouts  6.2 us (10%)
  between operations  0.88 us (1%)
  other arithmetic  0.85 us (1%)
    ppermute x8, waiting for transfers between devices, step(): self.packets.append(lax.ppermute(out, 'serve', pairs))  14.8 us
    ppermute x8, starting transfers between devices, step(): self.packets.append(lax.ppermute(out, 'serve', pairs))  10 us
    ppermute x4, starting transfers between devices, step(): self.parts += [lax.ppermute(part, 'serve', pairs) for part in self.parts]  8.36 us
    unnamed x20, local copies, waits for them, and re-layouts  5.04 us
    pallas_call x8, Pallas kernels, pick(): pl.pallas_call(kernel, in_specs=[SMEM, SMEM] + [VMEM] * len(arrays) + [AN...  4.73 us
    pallas_call x1, Pallas kernels, attention(): pl.pallas_call(functools.partial(attention_kernel, query_columns=query_co...  4.31 us
    pallas_call x1, Pallas kernels, base_products(): pl.pallas_call(base_kernel, grid_spec=pltpu.PrefetchScalarGridSpec(num_sc...  3.39 us
    pallas_call x1, Pallas kernels, finish(): pl.pallas_call(kernel, in_specs=[SMEM, SMEM, SMEM] + [VMEM] * (2 + len(ar...  1.98 us
  transfers between devices with their start and end apart: 17, of which 6 were waited for; matrix products, arithmetic and copies ran while one was open for 3% of the time, Pallas kernels for 24%

profile of v2, /device:TPU:0, one launch (start us, length us, event | category | flops | bytes accessed | tf_op | source)
XLA Modules:
  0.0 59.1 jit_solution(935261245903433298)
XLA Ops:
  0.5 1.2 %fusion = (bf16[2,16,4096]{2,1,0:T(8,128)(2,1)S(1)}, bf16[2,16,4096]{2,1,0:T(8,128)(2,1)S(1)}, bf16[2,16,4096]{2,1,0:T(8,128)(2,1)S(1)}) fusion(bf16[2,48,4096]{2,1,0:T(8,128)(2,1)} %param.18), kind=kLoop, calls=%fused_computation.2 | loop fusion | bytes 1572864 | tf_op jit(solution)/shard_map/slice | solution.py:367
  1.7 0.8 %pad_maximum_fusion.refs_0_ = bf16[2,16,4736]{2,1,0:T(8,128)(2,1)S(1)} fusion(bf16[2,16,256]{2,1,0:T(8,128)(2,1)} %param.21, bf16[2,16,128]{2,1,0:T(8,128)(2,1)} %param.20, bf16[2,16,256]{2,1,0:T(8,128)(2,1)} %param.19, bf16[2,16,4096]{2,1,0:T(8,128)(2,1)S(1)} %get-tuple-element.14), kind=kLoop, calls=%fused_computation | loop fusion | flops 1212416 | bytes 606208 | tf_op jit(solution)/shard_map/concatenate | solution.py:368
  2.5 3.0 %collective-permute-start.2 = (bf16[2,16,4736]{2,1,0:T(8,128)(2,1)S(1)}, bf16[2,16,4736]{2,1,0:T(8,128)(2,1)S(1)}, u32[]{:S(2)}, u32[]{:S(2)}) collective-permute-start(bf16[2,16,4736]{2,1,0:T(8,128)(2,1)S(1)} %pad_maximum_fusion.refs_0_), channel_id=1, source_target_pairs={{0,2},{2,0},{4,6},{6,4},{8,10},{10,8},{12,14},{14,12},{1,3},{3,1},... | collective-permute-start | bytes 909320 | tf_op jit(solution)/shard_map/ppermute | solution.py:70
  5.5 1.6 %collective-permute-start.3 = (bf16[2,16,4096]{2,1,0:T(8,128)(2,1)S(1)}, bf16[2,16,4096]{2,1,0:T(8,128)(2,1)S(1)}, u32[]{:S(2)}, u32[]{:S(2)}) collective-permute-start(bf16[2,16,4096]{2,1,0:T(8,128)(2,1)S(1)} %get-tuple-element.15.refs_0_.refs_4_), channel_id=1, source_target_pairs={{0,4},{2,6},{4,0},{6,2},{8,12},{10,14},{12,8},{14,10},{1,5},{3,7},... | collective-permute-start | bytes 786440 | tf_op jit(solution)/shard_map/ppermute | solution.py:70
  7.1 2.6 %collective-permute-start.7 = (bf16[2,16,4096]{2,1,0:T(8,128)(2,1)S(1)}, bf16[2,16,4096]{2,1,0:T(8,128)(2,1)S(1)}, u32[]{:S(2)}, u32[]{:S(2)}) collective-permute-start(bf16[2,16,4096]{2,1,0:T(8,128)(2,1)S(1)} %get-tuple-element.13.refs_0_.refs_8_), channel_id=1, source_target_pairs={{0,8},{2,10},{4,12},{6,14},{8,0},{10,2},{12,4},{14,6},{1,9},{3,11}... | collective-permute-start | bytes 786440 | tf_op jit(solution)/shard_map/ppermute | solution.py:70
  10.3 1.2 %collective-permute-start.6 = (bf16[2,16,4096]{2,1,0:T(8,128)(2,1)}, bf16[2,16,4096]{2,1,0:T(8,128)(2,1)S(1)}, u32[]{:S(2)}, u32[]{:S(2)}) collective-permute-start(bf16[2,16,4096]{2,1,0:T(8,128)(2,1)} %refs_0_.5), channel_id=1, source_target_pairs={{0,2},{2,0},{4,6},{6,4},{8,10},{10,8},{12,14},{14,12},{1,3},{3,1},... | collective-permute-start | bytes 786440 | tf_op jit(solution)/shard_map/ppermute | solution.py:70
  11.6 1.2 %copy-done = bf16[128,4096]{1,0:T(8,128)(2,1)S(1)} copy-done((bf16[128,4096]{1,0:T(8,128)(2,1)S(1)}, bf16[128,4096]{1,0:T(8,128)(2,1)}, u32[]{:S(2)}) %copy-start) | copy-done | bytes 1048600
  12.8 2.2 %copy-done.2 = bf16[8192,256]{1,0:T(8,128)(2,1)S(1)} copy-done((bf16[8192,256]{1,0:T(8,128)(2,1)S(1)}, bf16[8192,256]{1,0:T(8,128)(2,1)}, u32[]{:S(2)}) %copy-start.2) | copy-done | bytes 4194328
  15.0 1.6 %copy-done.5 = bf16[8192,128]{1,0:T(8,128)(2,1)S(1)} copy-done((bf16[8192,128]{1,0:T(8,128)(2,1)S(1)}, bf16[8192,128]{1,0:T(8,128)(2,1)}, u32[]{:S(2)}) %copy-start.5) | copy-done | bytes 2097176
  16.6 3.4 %base.1.refs_2_.base_own = f32[128,384]{1,0:T(8,128)S(1)} custom-call(s32[2]{0:T(128)S(1)} %pad_add_fusion.place, bf16[128,4096]{1,0:T(8,128)(2,1)S(1)} %copy-done, bf16[128,4096]{1,0:T(8,128)(2,1)S(1)} %collective-permute-done.other_tokens, bf16[8192,256]{1,0:T(8,128)(2,1)S(1)} %copy-done.2, bf16[8192,128]{1,0:T(8,128)(2,1)S(1)} %copy-done.5), custom_call_target="tpu_custom_call" | custom-call | flops 805306368 | bytes 8388608 | tf_op jit(solution)/shard_map/base/pallas_call | solution.py:136
  20.0 0.6 %pick.8.refs_2_ = bf16[2,16,4096]{2,1,0:T(8,128)(2,1)S(1)} custom-call(s32[8]{0:T(128)S(1)} %copy-done.8, s32[16]{0:T(128)S(1)} %copy-done.9, bf16[2,16,4096]{2,1,0:T(8,128)(2,1)S(1)} %get-tuple-element.15.refs_0_.refs_4_, bf16[2,16,4096]{2,1,0:T(8,128)(2,1)S(1)} %collective-permute-done.3.refs_1_.refs_5_, f32[128,384]{1,0:T(8,128)S(1)} %base.1.refs_2_.base_own), custom_call_target="tpu_custom_call" | custom-call | bytes 524288 | tf_op jit(solution)/shard_map/pick/pallas_call | solution.py:93
  20.6 0.6 %pick.9.refs_2_ = bf16[2,16,4736]{2,1,0:T(8,128)(2,1)S(1)} custom-call(s32[8]{0:T(128)S(1)} %copy-done.8, s32[16]{0:T(128)S(1)} %copy-done.9, bf16[2,16,4736]{2,1,0:T(8,128)(2,1)S(1)} %pad_maximum_fusion.refs_0_, bf16[2,16,4736]{2,1,0:T(8,128)(2,1)S(1)} %collective-permute-done.2.refs_1_, bf16[2,16,4096]{2,1,0:T(8,128)(2,1)S(1)} %pick.8.refs_2_), custom_call_target="tpu_custom_call" | custom-call | bytes 606208 | tf_op jit(solution)/shard_map/pick/pallas_call | solution.py:93
  21.2 1.6 %collective-permute-start.4 = (bf16[2,16,4736]{2,1,0:T(8,128)(2,1)S(1)}, bf16[2,16,4736]{2,1,0:T(8,128)(2,1)S(1)}, u32[]{:S(2)}, u32[]{:S(2)}) collective-permute-start(bf16[2,16,4736]{2,1,0:T(8,128)(2,1)S(1)} %pick.9.refs_2_), channel_id=1, source_target_pairs={{0,4},{2,6},{4,0},{6,2},{8,12},{10,14},{12,8},{14,10},{1,5},{3,7},... | collective-permute-start | bytes 909320 | tf_op jit(solution)/shard_map/ppermute | solution.py:74
  22.9 0.5 collective-permute-start.5
  23.4 0.6 %pick.10.refs_2_ = bf16[2,16,4096]{2,1,0:T(8,128)(2,1)S(1)} custom-call(s32[8]{0:T(128)S(1)} %copy-done.8, s32[16]{0:T(128)S(1)} %copy-done.9, bf16[2,16,4096]{2,1,0:T(8,128)(2,1)S(1)} %get-tuple-element.13.refs_0_.refs_8_, bf16[2,16,4096]{2,1,0:T(8,128)(2,1)S(1)} %collective-permute-done.7.refs_1_.refs_9_, bf16[2,16,4736]{2,1,0:T(8,128)(2,1)S(1)} %pick.9.refs_2_), custom_call_target="tpu_custom_call" | custom-call | bytes 524288 | tf_op jit(solution)/shard_map/pick/pallas_call | solution.py:93
  24.0 1.6 %collective-permute-start.10 = (bf16[2,16,4096]{2,1,0:T(8,128)(2,1)S(1)}, bf16[2,16,4096]{2,1,0:T(8,128)(2,1)S(1)}, u32[]{:S(2)}, u32[]{:S(2)}) collective-permute-start(bf16[2,16,4096]{2,1,0:T(8,128)(2,1)S(1)} %pick.10.refs_2_), channel_id=1, source_target_pairs={{0,2},{2,0},{4,6},{6,4},{8,10},{10,8},{12,14},{14,12},{1,3},{3,1},... | collective-permute-start | bytes 786440 | tf_op jit(solution)/shard_map/ppermute | solution.py:74
  25.6 0.6 %pick.11.refs_3_ = bf16[2,16,4096]{2,1,0:T(8,128)(2,1)S(1)} custom-call(s32[8]{0:T(128)S(1)} %copy-done.8, s32[16]{0:T(128)S(1)} %copy-done.9, bf16[2,16,4096]{2,1,0:T(8,128)(2,1)S(1)} %copy-done.4, bf16[2,16,4096]{2,1,0:T(8,128)(2,1)S(1)} %collective-permute-done.6.refs_1_, bf16[2,16,4096]{2,1,0:T(8,128)(2,1)S(1)} %pick.10.refs_2_), custom_call_target="tpu_custom_call" | custom-call | bytes 524288 | tf_op jit(solution)/shard_map/pick/pallas_call | solution.py:93
  26.8 5.3 %collective-permute-done.5.refs_2_.refs_6_ = bf16[2,16,4096]{2,1,0:T(8,128)(2,1)S(1)} collective-permute-done((bf16[2,16,4096]{2,1,0:T(8,128)(2,1)S(1)}, bf16[2,16,4096]{2,1,0:T(8,128)(2,1)S(1)}, u32[]{:S(2)}, u32[]{:S(2)}) %collective-permute-start.5) | collective-permute-done | bytes 262176 | tf_op jit(solution)/shard_map/ppermute | solution.py:74
  32.1 0.6 pick.12.refs_3_
  32.7 2.7 %collective-permute-start.9 = (bf16[1,16,4096]{2,1,0:T(8,128)(2,1)S(1)}, bf16[1,16,4096]{2,1,0:T(8,128)(2,1)S(1)}, u32[]{:S(2)}, u32[]{:S(2)}) collective-permute-start(bf16[1,16,4096]{2,1,0:T(8,128)(2,1)S(1)} %pick.12.refs_3_), channel_id=1, source_target_pairs={{0,8},{2,10},{4,12},{6,14},{8,0},{10,2},{12,4},{14,6},{1,9},{3,11}... | collective-permute-start | bytes 393224 | tf_op jit(solution)/shard_map/ppermute | solution.py:74
  35.3 0.6 pick.13.refs_3_
  35.9 0.6 collective-permute-done.10.refs_2_.refs_10_
  36.5 2.6 %collective-permute-start.8 = (bf16[1,16,4736]{2,1,0:T(8,128)(2,1)S(1)}, bf16[1,16,4736]{2,1,0:T(8,128)(2,1)S(1)}, u32[]{:S(2)}, u32[]{:S(2)}) collective-permute-start(bf16[1,16,4736]{2,1,0:T(8,128)(2,1)S(1)} %pick.13.refs_3_), channel_id=1, source_target_pairs={{0,8},{2,10},{4,12},{6,14},{8,0},{10,2},{12,4},{14,6},{1,9},{3,11}... | collective-permute-start | bytes 454664 | tf_op jit(solution)/shard_map/ppermute | solution.py:74
  39.1 0.6 pick.14.refs_3_
  40.2 0.6 pick.15
  40.8 4.0 %collective-permute-done.9.refs_7_ = bf16[1,16,4096]{2,1,0:T(8,128)(2,1)S(1)} collective-permute-done((bf16[1,16,4096]{2,1,0:T(8,128)(2,1)S(1)}, bf16[1,16,4096]{2,1,0:T(8,128)(2,1)S(1)}, u32[]{:S(2)}, u32[]{:S(2)}) %collective-permute-start.9) | collective-permute-done | bytes 131104 | tf_op jit(solution)/shard_map/ppermute | solution.py:74
  44.9 2.1 %collective-permute-done.11.refs_11_ = bf16[1,16,4096]{2,1,0:T(8,128)(2,1)S(1)} collective-permute-done((bf16[1,16,4096]{2,1,0:T(8,128)(2,1)S(1)}, bf16[1,16,4096]{2,1,0:T(8,128)(2,1)S(1)}, u32[]{:S(2)}, u32[]{:S(2)}) %collective-permute-start.11) | collective-permute-done | bytes 131104 | tf_op jit(solution)/shard_map/ppermute | solution.py:74
  47.0 2.7 %collective-permute-done.8.refs_3_ = bf16[1,16,4736]{2,1,0:T(8,128)(2,1)S(1)} collective-permute-done((bf16[1,16,4736]{2,1,0:T(8,128)(2,1)S(1)}, bf16[1,16,4736]{2,1,0:T(8,128)(2,1)S(1)}, u32[]{:S(2)}, u32[]{:S(2)}) %collective-permute-start.8) | collective-permute-done | bytes 151584 | tf_op jit(solution)/shard_map/ppermute | solution.py:74
  49.7 1.7 %shrink.1 = (f32[128,48]{1,0:T(8,128)S(1)}, bf16[16,640]{1,0:T(8,128)(2,1)S(1)}) custom-call(s32[8]{0:T(128)S(1)} %copy-done.8, s32[16]{0:T(128)S(1)} %copy-done.9, bf16[128,4096]{1,0:T(8,128)(2,1)S(1)} %copy-done.1, bf16[2,16,4736]{2,1,0:T(8,128)(2,1)S(1)} %pad_maximum_fusion.refs_0_, bf16[2,16,4736]{2,1,0:T(8,128)(2,1)S(1)} %collective-permute-done.2.refs_1_, ...), custom_call_target="tpu_custom_call" | custom-call | flops 50331648 | bytes 1048576 | tf_op jit(solution)/shard_map/shrink/pallas_call | solution.py:179
  51.9 0.8 %collective-permute-done.13.small_other = bf16[16,640]{1,0:T(8,128)(2,1)S(1)} collective-permute-done((bf16[16,640]{1,0:T(8,128)(2,1)S(1)}, bf16[16,640]{1,0:T(8,128)(2,1)S(1)}, u32[]{:S(2)}, u32[]{:S(2)}) %collective-permute-start.13) | collective-permute-done | bytes 20512 | tf_op jit(solution)/shard_map/ppermute | solution.py:359
  52.8 4.3 %attention.1 = (f32[128,4096]{1,0:T(8,128)S(1)}, bf16[128,16]{1,0:T(8,128)(2,1)S(1)}) custom-call(s32[2]{0:T(128)S(1)} %pad_add_fusion.place, f32[128,384]{1,0:T(8,128)S(1)} %base.1.refs_2_.base_own, f32[128,384]{1,0:T(8,128)S(1)} %collective-permute-done.1.base_other, f32[128,48]{1,0:T(8,128)S(1)} %get-tuple-element.9.shrink_own, ...), custom_call_target="tpu_custom_call" | custom-call | flops 536870912 | bytes 4194304 | tf_op jit(solution)/shard_map/attention/pallas_call | solution.py:282
  57.1 2.0 %finish.1 = bf16[128,4096]{1,0:T(8,128)(2,1)} custom-call(s32[8]{0:T(128)S(1)} %copy-done.8, s32[16]{0:T(128)S(1)} %copy-done.9, s32[2]{0:T(128)S(1)} %pad_add_fusion.place, f32[128,4096]{1,0:T(8,128)S(1)} %get-tuple-element.11.base_ref, bf16[128,16]{1,0:T(8,128)(2,1)S(1)} %get-tuple-element.12.low_ref, bf16[2,16,4096]{2,1,0:T(8,128)(2,1)S(1)} %copy-done.4, ...), custom_call_target="tpu_custom_call" | custom-call | flops 16777216 | bytes 3145728 | tf_op jit(solution)/shard_map/finish/pallas_call | solution.py:315
  (37 shorter events, 2.3 us)
Async XLA Ops:
  0.0 52.8 %collective-permute-start.14 = (bf16[256,8192]{1,0:T(8,128)(2,1)}, bf16[256,8192]{1,0:T(8,128)(2,1)}, u32[]{:S(2)}, u32[]{:S(2)}) collective-permute-start(bf16[256,8192]{1,0:T(8,128)(2,1)} %weight_own.1), channel_id=1, source_target_pairs={{0,1},{1,0},{2,3},{3,2},{4,5},{5,4},{6,7},{7,6},{8,9},{9,8},{10,11... | collective-permute-start | bytes 12582920 | tf_op jit(solution)/shard_map/ppermute | solution.py:359
  0.5 9.9 %collective-permute-start = (bf16[128,4096]{1,0:T(8,128)(2,1)}, bf16[128,4096]{1,0:T(8,128)(2,1)S(1)}, u32[]{:S(2)}, u32[]{:S(2)}) collective-permute-start(bf16[128,4096]{1,0:T(8,128)(2,1)} %rows_ref.1), channel_id=1, source_target_pairs={{0,1},{1,0},{2,3},{3,2},{4,5},{5,4},{6,7},{7,6},{8,9},{9,8},{10,11... | collective-permute-start | bytes 3145736 | tf_op jit(solution)/shard_map/ppermute | solution.py:359
  2.5 18.2 %collective-permute-start.2 = (bf16[2,16,4736]{2,1,0:T(8,128)(2,1)S(1)}, bf16[2,16,4736]{2,1,0:T(8,128)(2,1)S(1)}, u32[]{:S(2)}, u32[]{:S(2)}) collective-permute-start(bf16[2,16,4736]{2,1,0:T(8,128)(2,1)S(1)} %pad_maximum_fusion.refs_0_), channel_id=1, source_target_pairs={{0,2},{2,0},{4,6},{6,4},{8,10},{10,8},{12,14},{14,12},{1,3},{3,1},... | collective-permute-start | bytes 909320 | tf_op jit(solution)/shard_map/ppermute | solution.py:70
  5.5 14.5 %collective-permute-start.3 = (bf16[2,16,4096]{2,1,0:T(8,128)(2,1)S(1)}, bf16[2,16,4096]{2,1,0:T(8,128)(2,1)S(1)}, u32[]{:S(2)}, u32[]{:S(2)}) collective-permute-start(bf16[2,16,4096]{2,1,0:T(8,128)(2,1)S(1)} %get-tuple-element.15.refs_0_.refs_4_), channel_id=1, source_target_pairs={{0,4},{2,6},{4,0},{6,2},{8,12},{10,14},{12,8},{14,10},{1,5},{3,7},... | collective-permute-start | bytes 786440 | tf_op jit(solution)/shard_map/ppermute | solution.py:70
  7.1 16.3 %collective-permute-start.7 = (bf16[2,16,4096]{2,1,0:T(8,128)(2,1)S(1)}, bf16[2,16,4096]{2,1,0:T(8,128)(2,1)S(1)}, u32[]{:S(2)}, u32[]{:S(2)}) collective-permute-start(bf16[2,16,4096]{2,1,0:T(8,128)(2,1)S(1)} %get-tuple-element.13.refs_0_.refs_8_), channel_id=1, source_target_pairs={{0,8},{2,10},{4,12},{6,14},{8,0},{10,2},{12,4},{14,6},{1,9},{3,11}... | collective-permute-start | bytes 786440 | tf_op jit(solution)/shard_map/ppermute | solution.py:70
  10.3 15.3 %collective-permute-start.6 = (bf16[2,16,4096]{2,1,0:T(8,128)(2,1)}, bf16[2,16,4096]{2,1,0:T(8,128)(2,1)S(1)}, u32[]{:S(2)}, u32[]{:S(2)}) collective-permute-start(bf16[2,16,4096]{2,1,0:T(8,128)(2,1)} %refs_0_.5), channel_id=1, source_target_pairs={{0,2},{2,0},{4,6},{6,4},{8,10},{10,8},{12,14},{14,12},{1,3},{3,1},... | collective-permute-start | bytes 786440 | tf_op jit(solution)/shard_map/ppermute | solution.py:70
  11.6 1.2 %copy-start = (bf16[128,4096]{1,0:T(8,128)(2,1)S(1)}, bf16[128,4096]{1,0:T(8,128)(2,1)}, u32[]{:S(2)}) copy-start(bf16[128,4096]{1,0:T(8,128)(2,1)} %rows_ref.1) | copy-start | bytes 3145732
  12.8 2.2 %copy-start.2 = (bf16[8192,256]{1,0:T(8,128)(2,1)S(1)}, bf16[8192,256]{1,0:T(8,128)(2,1)}, u32[]{:S(2)}) copy-start(bf16[8192,256]{1,0:T(8,128)(2,1)} %query_weight.1) | copy-start | bytes 12582916
  15.0 1.6 %copy-start.5 = (bf16[8192,128]{1,0:T(8,128)(2,1)S(1)}, bf16[8192,128]{1,0:T(8,128)(2,1)}, u32[]{:S(2)}) copy-start(bf16[8192,128]{1,0:T(8,128)(2,1)} %key_value_weight.1) | copy-start | bytes 6291460
  16.6 3.4 %copy-start.8 = (s32[8]{0:T(128)S(1)}, s32[8]{0:T(128)}, u32[]{:S(2)}) copy-start(s32[8]{0:T(128)} %requests.19) | copy-start | bytes 100
  16.6 3.4 %copy-start.9 = (s32[16]{0:T(128)S(1)}, s32[16]{0:T(128)}, u32[]{:S(2)}) copy-start(s32[16]{0:T(128)} %pool.19) | copy-start | bytes 196
  16.6 9.0 %copy-start.4 = (bf16[2,16,4096]{2,1,0:T(8,128)(2,1)S(1)}, bf16[2,16,4096]{2,1,0:T(8,128)(2,1)}, u32[]{:S(2)}) copy-start(bf16[2,16,4096]{2,1,0:T(8,128)(2,1)} %refs_0_.5) | copy-start | bytes 786436
  20.0 29.7 %copy-start.1 = (bf16[128,4096]{1,0:T(8,128)(2,1)S(1)}, bf16[128,4096]{1,0:T(8,128)(2,1)}, u32[]{:S(2)}) copy-start(bf16[128,4096]{1,0:T(8,128)(2,1)} %rows_ref.1) | copy-start | bytes 3145732
  21.2 14.1 %collective-permute-start.4 = (bf16[2,16,4736]{2,1,0:T(8,128)(2,1)S(1)}, bf16[2,16,4736]{2,1,0:T(8,128)(2,1)S(1)}, u32[]{:S(2)}, u32[]{:S(2)}) collective-permute-start(bf16[2,16,4736]{2,1,0:T(8,128)(2,1)S(1)} %pick.9.refs_2_), channel_id=1, source_target_pairs={{0,4},{2,6},{4,0},{6,2},{8,12},{10,14},{12,8},{14,10},{1,5},{3,7},... | collective-permute-start | bytes 909320 | tf_op jit(solution)/shard_map/ppermute | solution.py:74
  22.9 9.2 %collective-permute-start.5 = (bf16[2,16,4096]{2,1,0:T(8,128)(2,1)S(1)}, bf16[2,16,4096]{2,1,0:T(8,128)(2,1)S(1)}, u32[]{:S(2)}, u32[]{:S(2)}) collective-permute-start(bf16[2,16,4096]{2,1,0:T(8,128)(2,1)S(1)} %pick.8.refs_2_), channel_id=1, source_target_pairs={{0,2},{2,0},{4,6},{6,4},{8,10},{10,8},{12,14},{14,12},{1,3},{3,1},... | collective-permute-start | bytes 786440 | tf_op jit(solution)/shard_map/ppermute | solution.py:74
  24.0 12.5 %collective-permute-start.10 = (bf16[2,16,4096]{2,1,0:T(8,128)(2,1)S(1)}, bf16[2,16,4096]{2,1,0:T(8,128)(2,1)S(1)}, u32[]{:S(2)}, u32[]{:S(2)}) collective-permute-start(bf16[2,16,4096]{2,1,0:T(8,128)(2,1)S(1)} %pick.10.refs_2_), channel_id=1, source_target_pairs={{0,2},{2,0},{4,6},{6,4},{8,10},{10,8},{12,14},{14,12},{1,3},{3,1},... | collective-permute-start | bytes 786440 | tf_op jit(solution)/shard_map/ppermute | solution.py:74
  26.2 26.6 %copy-start.3 = (bf16[256,8192]{1,0:T(8,128)(2,1)S(1)}, bf16[256,8192]{1,0:T(8,128)(2,1)}, u32[]{:S(2)}) copy-start(bf16[256,8192]{1,0:T(8,128)(2,1)} %weight_own.1) | copy-start | bytes 12582916
  26.2 26.6 %copy-start.6 = (f32[128,128]{1,0:T(8,128)S(1)}, f32[128,128]{1,0:T(8,128)}, u32[]{:S(2)}) copy-start(f32[128,128]{1,0:T(8,128)} %constant.9.clone.sine) | copy-start | bytes 196612
  26.2 26.6 %copy-start.7 = (f32[128,128]{1,0:T(8,128)S(1)}, f32[128,128]{1,0:T(8,128)}, u32[]{:S(2)}) copy-start(f32[128,128]{1,0:T(8,128)} %constant.8.clone.cosine) | copy-start | bytes 196612
  26.2 13.5 %collective-permute-start.15 = (bf16[2,16,4096]{2,1,0:T(8,128)(2,1)S(1)}, bf16[2,16,4096]{2,1,0:T(8,128)(2,1)S(1)}, u32[]{:S(2)}, u32[]{:S(2)}) collective-permute-start(bf16[2,16,4096]{2,1,0:T(8,128)(2,1)S(1)} %pick.11.refs_3_), channel_id=1, source_target_pairs={{0,4},{2,6},{4,0},{6,2},{8,12},{10,14},{12,8},{14,10},{1,5},{3,7},... | collective-permute-start | bytes 786440 | tf_op jit(solution)/shard_map/ppermute | solution.py:74
  32.7 12.2 %collective-permute-start.9 = (bf16[1,16,4096]{2,1,0:T(8,128)(2,1)S(1)}, bf16[1,16,4096]{2,1,0:T(8,128)(2,1)S(1)}, u32[]{:S(2)}, u32[]{:S(2)}) collective-permute-start(bf16[1,16,4096]{2,1,0:T(8,128)(2,1)S(1)} %pick.12.refs_3_), channel_id=1, source_target_pairs={{0,8},{2,10},{4,12},{6,14},{8,0},{10,2},{12,4},{14,6},{1,9},{3,11}... | collective-permute-start | bytes 393224 | tf_op jit(solution)/shard_map/ppermute | solution.py:74
  35.3 16.6 %collective-permute-start.1 = (f32[128,384]{1,0:T(8,128)S(1)}, f32[128,384]{1,0:T(8,128)S(1)}, u32[]{:S(2)}, u32[]{:S(2)}) collective-permute-start(f32[128,384]{1,0:T(8,128)S(1)} %base.1.refs_2_.base_own), channel_id=1, source_target_pairs={{0,1},{1,0},{2,3},{3,2},{4,5},{5,4},{6,7},{7,6},{8,9},{9,8},{10,11... | collective-permute-start | bytes 589832 | tf_op jit(solution)/shard_map/ppermute | solution.py:359
  36.5 13.2 %collective-permute-start.8 = (bf16[1,16,4736]{2,1,0:T(8,128)(2,1)S(1)}, bf16[1,16,4736]{2,1,0:T(8,128)(2,1)S(1)}, u32[]{:S(2)}, u32[]{:S(2)}) collective-permute-start(bf16[1,16,4736]{2,1,0:T(8,128)(2,1)S(1)} %pick.13.refs_3_), channel_id=1, source_target_pairs={{0,8},{2,10},{4,12},{6,14},{8,0},{10,2},{12,4},{14,6},{1,9},{3,11}... | collective-permute-start | bytes 454664 | tf_op jit(solution)/shard_map/ppermute | solution.py:74
  39.7 7.3 %collective-permute-start.11 = (bf16[1,16,4096]{2,1,0:T(8,128)(2,1)S(1)}, bf16[1,16,4096]{2,1,0:T(8,128)(2,1)S(1)}, u32[]{:S(2)}, u32[]{:S(2)}) collective-permute-start(bf16[1,16,4096]{2,1,0:T(8,128)(2,1)S(1)} %pick.14.refs_3_), channel_id=1, source_target_pairs={{0,4},{2,6},{4,0},{6,2},{8,12},{10,14},{12,8},{14,10},{1,5},{3,7},... | collective-permute-start | bytes 393224 | tf_op jit(solution)/shard_map/ppermute | solution.py:74
  44.9 12.3 %collective-permute-start.16 = (bf16[1,16,4096]{2,1,0:T(8,128)(2,1)S(1)}, bf16[1,16,4096]{2,1,0:T(8,128)(2,1)S(1)}, u32[]{:S(2)}, u32[]{:S(2)}) collective-permute-start(bf16[1,16,4096]{2,1,0:T(8,128)(2,1)S(1)} %pick.15), channel_id=1, source_target_pairs={{0,8},{2,10},{4,12},{6,14},{8,0},{10,2},{12,4},{14,6},{1,9},{3,11}... | collective-permute-start | bytes 393224 | tf_op jit(solution)/shard_map/ppermute | solution.py:74
  51.4 1.4 %collective-permute-start.12 = (f32[128,48]{1,0:T(8,128)S(1)}, f32[128,48]{1,0:T(8,128)S(1)}, u32[]{:S(2)}, u32[]{:S(2)}) collective-permute-start(f32[128,48]{1,0:T(8,128)S(1)} %get-tuple-element.9.shrink_own), channel_id=1, source_target_pairs={{0,1},{1,0},{2,3},{3,2},{4,5},{5,4},{6,7},{7,6},{8,9},{9,8},{10,11... | collective-permute-start | bytes 73736 | tf_op jit(solution)/shard_map/ppermute | solution.py:359
  51.4 1.3 %collective-permute-start.13 = (bf16[16,640]{1,0:T(8,128)(2,1)S(1)}, bf16[16,640]{1,0:T(8,128)(2,1)S(1)}, u32[]{:S(2)}, u32[]{:S(2)}) collective-permute-start(bf16[16,640]{1,0:T(8,128)(2,1)S(1)} %get-tuple-element.10.small_own), channel_id=1, source_target_pairs={{0,1},{1,0},{2,3},{3,2},{4,5},{5,4},{6,7},{7,6},{8,9},{9,8},{10,11... | collective-permute-start | bytes 61448 | tf_op jit(solution)/shard_map/ppermute | solution.py:359

commit v3 on v1

--- a/solution.py
+++ b/solution.py
@@ -101,56 +101,18 @@
         )(*self.tables, *arrays, *after)
 
 
-def base_kernel(tensor, own_tokens, other_tokens, query_weight, key_value_weight, out):
-    step = pl.program_id(0)
-    steps = pl.num_programs(0)
-    width = query_weight.shape[1]
-
-    @pl.when(step == 0)
-    def _():
-        out[...] = jnp.zeros_like(out)
-
-    def add(rows):
-        out[:, :width] += jnp.dot(rows[...], query_weight[...], preferred_element_type=jnp.float32)
-        out[:, width:] += jnp.dot(rows[...], key_value_weight[...], preferred_element_type=jnp.float32)
-
-    @pl.when(step < steps // 2)
-    def _():
-        add(own_tokens)
-
-    @pl.when(step >= steps // 2)
-    def _():
-        add(other_tokens)
-
-
 def base_products(tensor, own_tokens, other_tokens, query_weight, key_value_weight):
-    rows, half = own_tokens.shape
-    blocks = 4
-    depth = half // blocks
-    columns = query_weight.shape[1] + key_value_weight.shape[1]
-
-    def weight_block(step, tensor):
-        own = step < blocks
-        return (jnp.where(own, tensor[0], 1 - tensor[0]) * blocks + step % blocks, 0)
-
-    return pl.pallas_call(
-        base_kernel,
-        grid_spec=pltpu.PrefetchScalarGridSpec(
-            num_scalar_prefetch=1,
-            grid=(2 * blocks,),
-            in_specs=[
-                pl.BlockSpec((rows, depth), lambda i, t: (0, jnp.minimum(i, blocks - 1))),
-                pl.BlockSpec((rows, depth), lambda i, t: (0, jnp.maximum(i - blocks, 0))),
-                pl.BlockSpec((depth, query_weight.shape[1]), weight_block),
-                pl.BlockSpec((depth, key_value_weight.shape[1]), weight_block),
-            ],
-            out_specs=pl.BlockSpec((rows, columns), lambda i, t: (0, 0)),
-        ),
-        out_shape=jax.ShapeDtypeStruct((rows, columns), jnp.float32),
-        compiler_params=params(8),
-        cost_estimate=cost(4 * rows * half * columns, 4 * half * (rows + columns)),
-        name="base",
-    )(tensor, own_tokens, other_tokens, query_weight, key_value_weight)
+    half = own_tokens.shape[1]
+    first = tensor == 0
+    low = jnp.where(first, own_tokens, other_tokens)
+    high = jnp.where(first, other_tokens, own_tokens)
+
+    both = jnp.concatenate([low, high], axis=1)
+
+    def product(weight):
+        return jnp.dot(both, weight, preferred_element_type=jnp.float32)
+
+    return jnp.concatenate([product(query_weight), product(key_value_weight)], axis=1)
 
 
 def shrink_partial(routes, tokens, small_width):
@@ -160,21 +122,19 @@
     arrays = sum([route.arrays() for route in routes], [])
 
     def kernel(requests, pool, rows_ref, *refs):
-        inputs, (out, small) = refs[:-2 - len(routes)], refs[-2 - len(routes):-len(routes)]
-        held = refs[-len(routes):]
+        inputs, (out, small, maps) = refs[:-3], refs[-3:]
         at = 0
         for place, (route, count) in enumerate(zip(routes, counts)):
 
             def store(ref, index, place=place):
-                held[place][...] = ref[index]
+                maps[place * rank:(place + 1) * rank, :] = ref[index, :, :half]
+                if place == 0:
+                    small[...] = ref[index, :, half:]
 
             route.choose((requests, pool), inputs[at:at + count], 0, store)
             at += count
-        for place in range(len(routes)):
-            out[:, place * rank:(place + 1) * rank] = lax.dot_general(
-                rows_ref[...], held[place][:, :half], (((1,), (1,)), ((), ())),
-                preferred_element_type=jnp.float32)
-        small[...] = held[0][:, half:]
+        out[...] = lax.dot_general(
+            rows_ref[...], maps[...], (((1,), (1,)), ((), ())), preferred_element_type=jnp.float32)
 
     return pl.pallas_call(
         kernel,
@@ -184,11 +144,45 @@
             jax.ShapeDtypeStruct((rows, rank * len(routes)), jnp.float32),
             jax.ShapeDtypeStruct((rank, small_width), tokens.dtype),
         ),
-        scratch_shapes=[pltpu.VMEM(route.parts[0].shape[1:], tokens.dtype) for route in routes],
+        scratch_shapes=[pltpu.VMEM((rank * len(routes), half), tokens.dtype)],
         compiler_params=params(6),
         cost_estimate=cost(2 * rows * half * rank * len(routes), 2 * rows * half),
         name="shrink",
     )(*routes[0].tables, tokens, *arrays)
+
+
+def cut_parts(down_maps, small, rank):
+    count, _, half = down_maps.shape
+    width = sum(each.shape[2] for each in small)
+
+    def kernel(down, *refs):
+        small_refs, outs, sems = refs[:-4], refs[-4:-1], refs[-1]
+        copies = [
+            pltpu.make_async_copy(
+                down.at[:, pl.ds(i * rank, rank), :], out.at[:, :, pl.ds(0, half)], sems.at[i])
+            for i, out in enumerate(outs)
+        ]
+        at = half
+        for i, each in enumerate(small_refs):
+            more = each.shape[2]
+            copies.append(pltpu.make_async_copy(each, outs[0].at[:, :, pl.ds(at, more)], sems.at[len(outs) + i]))
+            at += more
+        for copy in copies:
+            copy.start()
+        for copy in copies:
+            copy.wait()
+
+    return pl.pallas_call(
+        kernel,
+        in_specs=[ANY] * (1 + len(small)),
+        out_specs=(VMEM,) * 3,
+        out_shape=tuple(
+            jax.ShapeDtypeStruct((count, rank, half + more), down_maps.dtype) for more in (width, 0, 0)),
+        scratch_shapes=[pltpu.SemaphoreType.DMA((3 + len(small),))],
+        compiler_params=params(4),
+        cost_estimate=cost(0, 1 << 20),
+        name="cut",
+    )(down_maps, *small)
 
 
 def rotary_tables(rows, width):
@@ -203,12 +197,18 @@
 
 
 def attention_kernel(
-    place, base_own, base_other, shrink_own, shrink_other, small_own, small_other, cosine, sine,
-    weight_own, weight_other, out, low_out, *, query_columns, key_columns,
+    requests, pool, place, base_own, base_other, shrink_own, shrink_other, small_own, small_other, cosine, sine,
+    weight_own, weight_other, *refs, query_columns, key_columns, route,
 ):
+    out, up_map, tiles, sems = refs[-4:]
     tensor, length = place[0], place[1]
+
+    def store(ref, index):
+        up_map[...] = ref[index]
+
+    route.choose((requests, pool), refs[:-4], 0, store)
     rank = small_own.shape[0]
-    rows = out.shape[0]
+    rows = base_own.shape[0]
     size = HEAD_SIZE
     shrink = (shrink_own[...] + shrink_other[...]).astype(jnp.bfloat16)
     first = tensor == 0
@@ -254,64 +254,44 @@
             attended, small[:, query_columns + key_columns:], (((1,), (1,)), ((), ())),
             preferred_element_type=jnp.float32)
 
-    low_out[...] = (down(attended_own, small_own) + down(attended_other, small_other)).astype(jnp.bfloat16)
-    columns = out.shape[1]
-    tile = 512
-    for start in range(0, columns, tile):
-        cut = slice(start, start + tile)
+    low = (down(attended_own, small_own) + down(attended_other, small_other)).astype(jnp.bfloat16)
+    valid = lax.broadcasted_iota(jnp.int32, (rows, 1), 0) < length
+    count, _, tile = tiles.shape
+    copies = []
+    for i in range(count):
+        cut = slice(i * tile, (i + 1) * tile)
         own = jnp.dot(attended_own, weight_own[:, cut], preferred_element_type=jnp.float32)
         other = jnp.dot(attended_other, weight_other[:, cut], preferred_element_type=jnp.float32)
-        out[:, cut] = own.astype(jnp.bfloat16).astype(jnp.float32) + other.astype(jnp.bfloat16).astype(jnp.float32)
-
-
-def attention(place, base, shrink, small, weight, query_columns, key_columns):
+        base = own.astype(jnp.bfloat16).astype(jnp.float32) + other.astype(jnp.bfloat16).astype(jnp.float32)
+        delta = jnp.dot(low, up_map[:, cut], preferred_element_type=jnp.float32)
+        tiles[i] = jnp.where(valid, base + delta, 0.0).astype(tiles.dtype)
+        copies.append(pltpu.make_async_copy(tiles.at[i], out.at[:, pl.ds(i * tile, tile)], sems.at[i]))
+        copies[-1].start()
+    for copy in copies:
+        copy.wait()
+
+
+def attention(route, place, base, shrink, small, weight, query_columns, key_columns):
     rows = base[0].shape[0]
     columns = weight[0].shape[1]
-    rank = small[0].shape[0]
     cosine, sine = rotary_tables(rows, HEAD_SIZE)
-    operands = (*base, *shrink, *small, cosine, sine, *weight)
+    arrays = route.arrays()
+    operands = (*base, *shrink, *small, cosine, sine, *weight, *arrays)
+    tile = 512
     return pl.pallas_call(
-        functools.partial(attention_kernel, query_columns=query_columns, key_columns=key_columns),
-        in_specs=[SMEM] + [VMEM] * len(operands),
-        out_specs=(VMEM, VMEM),
-        out_shape=(
-            jax.ShapeDtypeStruct((rows, columns), jnp.float32),
-            jax.ShapeDtypeStruct((rows, rank), jnp.bfloat16),
-        ),
-        compiler_params=params(16),
+        functools.partial(attention_kernel, query_columns=query_columns, key_columns=key_columns, route=route),
+        in_specs=[SMEM] * 3 + [VMEM] * len(operands),
+        out_specs=ANY,
+        out_shape=jax.ShapeDtypeStruct((rows, columns), arrays[0].dtype),
+        scratch_shapes=[
+            pltpu.VMEM(arrays[0].shape[1:], arrays[0].dtype),
+            pltpu.VMEM((columns // tile, rows, tile), arrays[0].dtype),
+            pltpu.SemaphoreType.DMA((columns // tile,)),
+        ],
+        compiler_params=params(8),
         cost_estimate=cost(4 * rows * query_columns * columns, 4 * query_columns * columns),
         name="attention",
-    )(place, *operands)
-
-
-def finish(route, place, base, low):
-    rows, columns = base.shape
-    arrays = route.arrays()
-
-    def kernel(requests, pool, place, base_ref, low_ref, *refs):
-        inputs, out, held = refs[:len(arrays)], refs[-2], refs[-1]
-
-        def store(ref, index):
-            held[...] = ref[index]
-
-        route.choose((requests, pool), inputs, 0, store)
-        valid = lax.broadcasted_iota(jnp.int32, (rows, 1), 0) < place[1]
-        tile = 512
-        for start in range(0, columns, tile):
-            cut = slice(start, start + tile)
-            delta = jnp.dot(low_ref[...], held[:, cut], preferred_element_type=jnp.float32)
-            out[:, cut] = jnp.where(valid, base_ref[:, cut] + delta, 0.0).astype(out.dtype)
-
-    return pl.pallas_call(
-        kernel,
-        in_specs=[SMEM, SMEM, SMEM] + [VMEM] * (2 + len(arrays)),
-        out_specs=VMEM,
-        out_shape=jax.ShapeDtypeStruct((rows, columns), jnp.bfloat16),
-        scratch_shapes=[pltpu.VMEM(arrays[0].shape[1:], arrays[0].dtype)],
-        compiler_params=params(8),
-        cost_estimate=cost(2 * rows * low.shape[1] * columns, 6 * rows * columns),
-        name="finish",
-    )(*route.tables, place, base, low, *arrays)
+    )(*route.tables, place, *operands)
 
 
 def orders(bits):
@@ -348,34 +328,38 @@
     def swap(x):
         return lax.ppermute(x, "tensor", pair)
 
-    small = jnp.concatenate([adapter_query_up, adapter_key_value_up, adapter_output_down], axis=2)
+    small = (adapter_query_up, adapter_key_value_up, adapter_output_down)
+    small_width = sum(each.shape[2] for each in small)
     first, second, third = orders(devices.bit_length() - 1)
 
     def route(part, order):
         return Route(part, order, devices, request_adapter, adapter_pool_row)
 
-    down = [adapter_down_maps[:, i * rank:(i + 1) * rank] for i in range(3)]
-    routes = [
-        route(jnp.concatenate([down[0], small], axis=2), first),
-        route(down[1], second),
-        route(down[2], third),
-    ]
+    parts = cut_parts(adapter_down_maps, small, rank)
+    first_route, second_route, third_route = (
+        route(part, order) for part, order in zip(parts, (first, second, third)))
+    routes = [first_route, second_route, third_route]
     up_route = route(adapter_output_up, first)
-    for _ in range(devices.bit_length() - 1):
-        for each in (*routes, up_route):
-            each.step()
-
+    weight_other = swap(output_weight)
     other_tokens = swap(tokens)
-    base_own = base_products(place, tokens, other_tokens, query_weight, key_value_weight)
+    for each in (third_route, second_route, first_route, up_route):
+        each.step()
+    base_own = base_products(tensor, tokens, other_tokens, query_weight, key_value_weight)
     base_other = swap(base_own)
-    weight_own = lax.dynamic_slice_in_dim(output_weight, tensor * half, half, 1)
-    weight_other = swap(lax.dynamic_slice_in_dim(output_weight, (1 - tensor) * half, half, 1))
-
-    shrink_own, small_own = shrink_partial(routes, tokens, small.shape[2])
-    base, low = attention(
-        place, (base_own, base_other), (shrink_own, swap(shrink_own)), (small_own, swap(small_own)),
-        (weight_own, weight_other), query_columns, key_columns)
-    return finish(up_route, place, base, low)
+    weight_near, weight_far = (
+        lax.dynamic_slice_in_dim(weight, tensor * half, half, 1) for weight in (output_weight, weight_other))
+    last = (base_own,)
+    turns = (first_route, second_route, third_route, up_route, first_route, second_route, third_route, up_route) * 1
+    for turn, each in enumerate(turns):
+        if turn == 3:
+            last += (weight_near, weight_far)
+        sent = each.step(last)
+        last = (each.arrays()[-1] if sent is None else sent,)
+
+    shrink_own, small_own = shrink_partial(routes, tokens, small_width)
+    return attention(
+        up_route, place, (base_own, base_other), (shrink_own, swap(shrink_own)), (small_own, swap(small_own)),
+        (weight_near, weight_far), query_columns, key_columns)
 
 
 def solution(mesh):

time: 71 us -> 53.5 us (0.75)
  waiting for transfers between devices: 33.7 us -> 6.63 us
  starting transfers between devices: 18.7 us -> 24 us
  local copies, waits for them, and re-layouts: 2.97 us -> 7.23 us
  Pallas kernels: 14.4 us -> 11 us
  other arithmetic: 0.1 us -> 1.74 us
  matrix products: 0 us -> 1.45 us
    ppermute x8, waiting for transfers between devices: 17.7 us -> 2.85 us  [step(): self.packets.append(lax.ppermute(out, 'serve', pairs))]
    ppermute x4, waiting for transfers between devices: 15.1 us -> 3.01 us  [step(): self.parts += [lax.ppermute(part, 'serve', pairs) for part in self.parts]]
    ppermute x8, starting transfers between devices: 9.82 us -> 15.2 us  [step(): self.packets.append(lax.ppermute(out, 'serve', pairs))]
    pallas_call x2 -> x1, Pallas kernels: 5.33 us -> 0.13 us  [cut_parts(): pl.pallas_call(kernel, in_specs=[ANY] * (1 + len(small)), out_specs=(VMEM...]
    unnamed x24, local copies, waits for them, and re-layouts: 0.06 us -> 3.68 us
    select_n x0 -> x1, other arithmetic: none -> 1.65 us  [base_products(): low = jnp.where(first, own_tokens, other_tokens)]
    dot_general x0 -> x2, matrix products: none -> 1.45 us  [product(): return jnp.dot(both, weight, preferred_element_type=jnp.float32)]
    pallas_call x1, Pallas kernels: 2.67 us -> 3.79 us  [attention(): pl.pallas_call(functools.partial(attention_kernel, query_columns=query_co...]
  transfers between devices with their start and end apart: 17 -> 17, of which waited for: 5 -> 5; matrix products, arithmetic and copies ran while one was open for 0% -> 13% of each run, Pallas kernels for 18% -> 14%
where the time goes in v3:
time: 53.5 us; the launch traced here: 53 us
  starting transfers between devices  24 us (45%)
  Pallas kernels  11 us (21%)
  local copies, waits for them, and re-layouts  7.23 us (14%)
  waiting for transfers between devices  6.63 us (12%)
  other arithmetic  1.74 us (3%)
  matrix products  1.45 us (3%)
  between operations  0.93 us (2%)
    ppermute x8, starting transfers between devices, step(): self.packets.append(lax.ppermute(out, 'serve', pairs))  15.2 us
    ppermute x4, starting transfers between devices, step(): self.parts += [lax.ppermute(part, 'serve', pairs) for part in self.parts]  7.77 us
    pallas_call x8, Pallas kernels, pick(): pl.pallas_call(kernel, in_specs=[SMEM, SMEM] + [VMEM] * len(arrays) + [AN...  5.59 us
    pallas_call x1, Pallas kernels, attention(): pl.pallas_call(functools.partial(attention_kernel, query_columns=query_co...  3.79 us
    unnamed x24, local copies, waits for them, and re-layouts  3.68 us
    dynamic_slice x2, local copies, waits for them, and re-layouts, local(): lax.dynamic_slice_in_dim(weight, tensor * half, half, 1)  3.56 us
    ppermute x4, waiting for transfers between devices, step(): self.parts += [lax.ppermute(part, 'serve', pairs) for part in self.parts]  3.01 us
    ppermute x8, waiting for transfers between devices, step(): self.packets.append(lax.ppermute(out, 'serve', pairs))  2.85 us
  transfers between devices with their start and end apart: 17, of which 5 were waited for; matrix products, arithmetic and copies ran while one was open for 13% of the time, Pallas kernels for 14%

profile of v3, /device:TPU:0, one launch (start us, length us, event | category | flops | bytes accessed | tf_op | source)
XLA Modules:
  0.0 53.0 jit_solution(17031478141595541751)
XLA Ops:
  0.5 1.2 %copy-done.3 = bf16[2,48,4096]{2,1,0:T(8,128)(2,1)S(1)} copy-done((bf16[2,48,4096]{2,1,0:T(8,128)(2,1)S(1)}, bf16[2,48,4096]{2,1,0:T(8,128)(2,1)}, u32[]{:S(2)}) %copy-start.3) | copy-done | bytes 786456
  1.8 0.7 %copy-done.8 = bf16[2,16,256]{2,1,0:T(8,128)(2,1)S(1)} copy-done((bf16[2,16,256]{2,1,0:T(8,128)(2,1)S(1)}, bf16[2,16,256]{2,1,0:T(8,128)(2,1)}, u32[]{:S(2)}) %copy-start.8) | copy-done | bytes 16408
  2.5 0.7 %copy-done.9 = bf16[2,16,256]{2,1,0:T(8,128)(2,1)S(1)} copy-done((bf16[2,16,256]{2,1,0:T(8,128)(2,1)S(1)}, bf16[2,16,256]{2,1,0:T(8,128)(2,1)}, u32[]{:S(2)}) %copy-start.9) | copy-done | bytes 16408
  3.2 0.7 %copy-done.10 = bf16[2,16,128]{2,1,0:T(8,128)(2,1)S(1)} copy-done((bf16[2,16,128]{2,1,0:T(8,128)(2,1)S(1)}, bf16[2,16,128]{2,1,0:T(8,128)(2,1)}, u32[]{:S(2)}) %copy-start.10) | copy-done | bytes 8216
  4.0 3.0 %collective-permute-start.2 = (bf16[2,16,4736]{2,1,0:T(8,128)(2,1)S(1)}, bf16[2,16,4736]{2,1,0:T(8,128)(2,1)S(1)}, u32[]{:S(2)}, u32[]{:S(2)}) collective-permute-start(bf16[2,16,4736]{2,1,0:T(8,128)(2,1)S(1)} %get-tuple-element.10.refs_0_), channel_id=1, source_target_pairs={{0,2},{2,0},{4,6},{6,4},{8,10},{10,8},{12,14},{14,12},{1,3},{3,1},... | collective-permute-start | bytes 909320 | tf_op jit(solution)/shard_map/ppermute | solution.py:70
  7.1 1.6 %collective-permute-start.6 = (bf16[2,16,4096]{2,1,0:T(8,128)(2,1)S(1)}, bf16[2,16,4096]{2,1,0:T(8,128)(2,1)S(1)}, u32[]{:S(2)}, u32[]{:S(2)}) collective-permute-start(bf16[2,16,4096]{2,1,0:T(8,128)(2,1)S(1)} %get-tuple-element.12.refs_0_.refs_4_), channel_id=1, source_target_pairs={{0,4},{2,6},{4,0},{6,2},{8,12},{10,14},{12,8},{14,10},{1,5},{3,7},... | collective-permute-start | bytes 786440 | tf_op jit(solution)/shard_map/ppermute | solution.py:70
  8.6 2.6 %collective-permute-start.5 = (bf16[2,16,4096]{2,1,0:T(8,128)(2,1)S(1)}, bf16[2,16,4096]{2,1,0:T(8,128)(2,1)}, u32[]{:S(2)}, u32[]{:S(2)}) collective-permute-start(bf16[2,16,4096]{2,1,0:T(8,128)(2,1)S(1)} %get-tuple-element.11.refs_0_.refs_8_), channel_id=1, source_target_pairs={{0,8},{2,10},{4,12},{6,14},{8,0},{10,2},{12,4},{14,6},{1,9},{3,11}... | collective-permute-start | bytes 786440 | tf_op jit(solution)/shard_map/ppermute | solution.py:70
  11.2 1.8 %constant_dynamic-slice_fusion.1.refs_3_.weight_own = bf16[256,4096]{1,0:T(8,128)(2,1)S(1)} fusion(bf16[256,8192]{1,0:T(8,128)(2,1)} %param.17, s32[]{:T(128)S(6)} %select_n.19), kind=kLoop, calls=%fused_computation.8 | loop fusion | bytes 4194308 | tf_op jit(solution)/shard_map/dynamic_slice | solution.py:350
  13.1 0.6 %collective-permute-start.4 = (bf16[2,16,4096]{2,1,0:T(8,128)(2,1)S(1)}, bf16[2,16,4096]{2,1,0:T(8,128)(2,1)S(1)}, u32[]{:S(2)}, u32[]{:S(2)}) collective-permute-start(bf16[2,16,4096]{2,1,0:T(8,128)(2,1)S(1)} %copy-done.2), channel_id=1, source_target_pairs={{0,2},{2,0},{4,6},{6,4},{8,10},{10,8},{12,14},{14,12},{1,3},{3,1},... | collective-permute-start | bytes 786440 | tf_op jit(solution)/shard_map/ppermute | solution.py:70
  13.7 1.7 %broadcast_select_fusion.1 = (bf16[128,4096]{1,0:T(8,128)(2,1)S(1)}, bf16[128,4096]{1,0:T(8,128)(2,1)S(1)}) fusion(bf16[128,4096]{1,0:T(8,128)(2,1)S(1)} %copy-done.1, bf16[128,4096]{1,0:T(8,128)(2,1)} %collective-permute-done, pred[]{:T(512)S(6)} %eq.3), kind=kLoop, calls=%fused_computation.4 | loop fusion | flops 1048576 | bytes 4194305 | tf_op jit(solution)/shard_map/jit(_where)/select_n | solution.py:107
  15.6 0.7 %fusion.1 = f32[128,256]{1,0:T(8,128)S(1)} fusion(bf16[8192,256]{1,0:T(8,128)(2,1)S(1)} %copy-done.11, bf16[128,4096]{1,0:T(8,128)(2,1)S(1)} %get-tuple-element.16, bf16[128,4096]{1,0:T(8,128)(2,1)S(1)} %get-tuple-element.15), kind=kOutput, calls=%fused_computation.2 | convolution fusion | flops 541065216 | bytes 6422528 | tf_op jit(solution)/shard_map/dot_general | solution.py:113
  16.4 0.7 %fusion = f32[128,128]{1,0:T(8,128)S(1)} fusion(bf16[8192,128]{1,0:T(8,128)(2,1)S(1)} %copy-done, bf16[128,4096]{1,0:T(8,128)(2,1)S(1)} %get-tuple-element.16, bf16[128,4096]{1,0:T(8,128)(2,1)S(1)} %get-tuple-element.15), kind=kOutput, calls=%fused_computation.1 | convolution fusion | flops 272629760 | bytes 4259840 | tf_op jit(solution)/shard_map/dot_general | solution.py:113
  17.2 0.6 %pick.8.refs_2_ = bf16[2,16,4736]{2,1,0:T(8,128)(2,1)S(1)} custom-call(s32[8]{0:T(128)S(1)} %copy-done.6, s32[16]{0:T(128)S(1)} %copy-done.7, bf16[2,16,4736]{2,1,0:T(8,128)(2,1)S(1)} %get-tuple-element.10.refs_0_, bf16[2,16,4736]{2,1,0:T(8,128)(2,1)S(1)} %collective-permute-done.2.refs_1_, f32[128,384]{1,0:T(8,128)S(1)} %pad_maximum_fusion.3.refs_2_.base_own), custom_call_target="tpu_custom_call" | custom-call | bytes 606208 | tf_op jit(solution)/shard_map/pick/pallas_call | solution.py:93
  17.8 0.5 collective-permute-start.3
  18.3 3.0 %collective-permute-done.6.refs_1_.refs_5_ = bf16[2,16,4096]{2,1,0:T(8,128)(2,1)S(1)} collective-permute-done((bf16[2,16,4096]{2,1,0:T(8,128)(2,1)S(1)}, bf16[2,16,4096]{2,1,0:T(8,128)(2,1)S(1)}, u32[]{:S(2)}, u32[]{:S(2)}) %collective-permute-start.6) | collective-permute-done | bytes 262176 | tf_op jit(solution)/shard_map/ppermute | solution.py:70
  21.3 0.6 %pick.9.refs_2_ = bf16[2,16,4096]{2,1,0:T(8,128)(2,1)S(1)} custom-call(s32[8]{0:T(128)S(1)} %copy-done.6, s32[16]{0:T(128)S(1)} %copy-done.7, bf16[2,16,4096]{2,1,0:T(8,128)(2,1)S(1)} %get-tuple-element.12.refs_0_.refs_4_, bf16[2,16,4096]{2,1,0:T(8,128)(2,1)S(1)} %collective-permute-done.6.refs_1_.refs_5_, bf16[2,16,4736]{2,1,0:T(8,128)(2,1)S(1)} %pick.8.refs_2_), custom_call_target="tpu_custom_call" | custom-call | bytes 524288 | tf_op jit(solution)/shard_map/pick/pallas_call | solution.py:93
  22.0 1.0 %pick.10.refs_2_ = bf16[2,16,4096]{2,1,0:T(8,128)(2,1)S(1)} custom-call(s32[8]{0:T(128)S(1)} %copy-done.6, s32[16]{0:T(128)S(1)} %copy-done.7, bf16[2,16,4096]{2,1,0:T(8,128)(2,1)S(1)} %get-tuple-element.11.refs_0_.refs_8_, bf16[2,16,4096]{2,1,0:T(8,128)(2,1)} %collective-permute-done.5.refs_1_.refs_9_, bf16[2,16,4096]{2,1,0:T(8,128)(2,1)S(1)} %pick.9.refs_2_), custom_call_target="tpu_custom_call" | custom-call | bytes 524288 | tf_op jit(solution)/shard_map/pick/pallas_call | solution.py:93
  23.0 2.1 %collective-permute-start.11 = (bf16[2,16,4096]{2,1,0:T(8,128)(2,1)S(1)}, bf16[2,16,4096]{2,1,0:T(8,128)(2,1)S(1)}, u32[]{:S(2)}, u32[]{:S(2)}) collective-permute-start(bf16[2,16,4096]{2,1,0:T(8,128)(2,1)S(1)} %pick.10.refs_2_), channel_id=1, source_target_pairs={{0,2},{2,0},{4,6},{6,4},{8,10},{10,8},{12,14},{14,12},{1,3},{3,1},... | collective-permute-start | bytes 786440 | tf_op jit(solution)/shard_map/ppermute | solution.py:74
  25.1 1.7 %constant_dynamic-slice_fusion.refs_4_.weight_other = bf16[256,4096]{1,0:T(8,128)(2,1)S(1)} fusion(bf16[256,8192]{1,0:T(8,128)(2,1)} %collective-permute-done.7, s32[]{:T(128)S(6)} %select_n.19), kind=kLoop, calls=%fused_computation.7 | loop fusion | bytes 4194308 | tf_op jit(solution)/shard_map/dynamic_slice | solution.py:350
  26.9 0.6 %pick.11.refs_3_ = bf16[2,16,4096]{2,1,0:T(8,128)(2,1)S(1)} custom-call(s32[8]{0:T(128)S(1)} %copy-done.6, s32[16]{0:T(128)S(1)} %copy-done.7, bf16[2,16,4096]{2,1,0:T(8,128)(2,1)S(1)} %copy-done.2, bf16[2,16,4096]{2,1,0:T(8,128)(2,1)S(1)} %collective-permute-done.4.refs_1_, bf16[2,16,4096]{2,1,0:T(8,128)(2,1)S(1)} %pick.10.refs_2_, ...), custom_call_target="tpu_custom_call" | custom-call | bytes 524288 | tf_op jit(solution)/shard_map/pick/pallas_call | solution.py:93
  27.5 1.2 %collective-permute-start.15 = (bf16[2,16,4096]{2,1,0:T(8,128)(2,1)S(1)}, bf16[2,16,4096]{2,1,0:T(8,128)(2,1)S(1)}, u32[]{:S(2)}, u32[]{:S(2)}) collective-permute-start(bf16[2,16,4096]{2,1,0:T(8,128)(2,1)S(1)} %pick.11.refs_3_), channel_id=1, source_target_pairs={{0,4},{2,6},{4,0},{6,2},{8,12},{10,14},{12,8},{14,10},{1,5},{3,7},... | collective-permute-start | bytes 786440 | tf_op jit(solution)/shard_map/ppermute | solution.py:74
  28.7 0.6 %pick.12.refs_3_ = bf16[1,16,4736]{2,1,0:T(8,128)(2,1)S(1)} custom-call(s32[8]{0:T(128)S(1)} %copy-done.6, s32[16]{0:T(128)S(1)} %copy-done.7, bf16[2,16,4736]{2,1,0:T(8,128)(2,1)S(1)} %get-tuple-element.10.refs_0_, bf16[2,16,4736]{2,1,0:T(8,128)(2,1)S(1)} %collective-permute-done.2.refs_1_, bf16[2,16,4736]{2,1,0:T(8,128)(2,1)S(1)} %collective-permute-done.3.refs_2_, ...), custom_call_target="tpu_custom_call" | custom-call | bytes 303104 | tf_op jit(solution)/shard_map/pick/pallas_call | solution.py:93
  29.3 3.6 %collective-permute-start.8 = (bf16[1,16,4736]{2,1,0:T(8,128)(2,1)S(1)}, bf16[1,16,4736]{2,1,0:T(8,128)(2,1)S(1)}, u32[]{:S(2)}, u32[]{:S(2)}) collective-permute-start(bf16[1,16,4736]{2,1,0:T(8,128)(2,1)S(1)} %pick.12.refs_3_), channel_id=1, source_target_pairs={{0,8},{2,10},{4,12},{6,14},{8,0},{10,2},{12,4},{14,6},{1,9},{3,11}... | collective-permute-start | bytes 454664 | tf_op jit(solution)/shard_map/ppermute | solution.py:74
  32.8 0.6 %pick.13.refs_3_ = bf16[1,16,4096]{2,1,0:T(8,128)(2,1)S(1)} custom-call(s32[8]{0:T(128)S(1)} %copy-done.6, s32[16]{0:T(128)S(1)} %copy-done.7, bf16[2,16,4096]{2,1,0:T(8,128)(2,1)S(1)} %get-tuple-element.12.refs_0_.refs_4_, bf16[2,16,4096]{2,1,0:T(8,128)(2,1)S(1)} %collective-permute-done.6.refs_1_.refs_5_, ...), custom_call_target="tpu_custom_call" | custom-call | bytes 262144 | tf_op jit(solution)/shard_map/pick/pallas_call | solution.py:93
  33.8 1.0 %pick.14.refs_3_ = bf16[1,16,4096]{2,1,0:T(8,128)(2,1)S(1)} custom-call(s32[8]{0:T(128)S(1)} %copy-done.6, s32[16]{0:T(128)S(1)} %copy-done.7, bf16[2,16,4096]{2,1,0:T(8,128)(2,1)S(1)} %get-tuple-element.11.refs_0_.refs_8_, bf16[2,16,4096]{2,1,0:T(8,128)(2,1)} %collective-permute-done.5.refs_1_.refs_9_, ...), custom_call_target="tpu_custom_call" | custom-call | bytes 262144 | tf_op jit(solution)/shard_map/pick/pallas_call | solution.py:93
  34.9 3.2 %collective-permute-start.10 = (bf16[1,16,4096]{2,1,0:T(8,128)(2,1)S(1)}, bf16[1,16,4096]{2,1,0:T(8,128)(2,1)S(1)}, u32[]{:S(2)}, u32[]{:S(2)}) collective-permute-start(bf16[1,16,4096]{2,1,0:T(8,128)(2,1)S(1)} %pick.13.refs_3_), channel_id=1, source_target_pairs={{0,8},{2,10},{4,12},{6,14},{8,0},{10,2},{12,4},{14,6},{1,9},{3,11}... | collective-permute-start | bytes 393224 | tf_op jit(solution)/shard_map/ppermute | solution.py:74
  38.2 0.6 %pick.15 = bf16[1,16,4096]{2,1,0:T(8,128)(2,1)S(1)} custom-call(s32[8]{0:T(128)S(1)} %copy-done.6, s32[16]{0:T(128)S(1)} %copy-done.7, bf16[2,16,4096]{2,1,0:T(8,128)(2,1)S(1)} %copy-done.2, bf16[2,16,4096]{2,1,0:T(8,128)(2,1)S(1)} %collective-permute-done.4.refs_1_, bf16[2,16,4096]{2,1,0:T(8,128)(2,1)S(1)} %collective-permute-done.15.refs_2_, ...), custom_call_target="tpu_custom_call" | custom-call | bytes 262144 | tf_op jit(solution)/shard_map/pick/pallas_call | solution.py:93
  38.8 4.5 %collective-permute-start.16 = (bf16[1,16,4096]{2,1,0:T(8,128)(2,1)S(1)}, bf16[1,16,4096]{2,1,0:T(8,128)(2,1)S(1)}, u32[]{:S(2)}, u32[]{:S(2)}) collective-permute-start(bf16[1,16,4096]{2,1,0:T(8,128)(2,1)S(1)} %pick.15), channel_id=1, source_target_pairs={{0,8},{2,10},{4,12},{6,14},{8,0},{10,2},{12,4},{14,6},{1,9},{3,11}... | collective-permute-start | bytes 393224 | tf_op jit(solution)/shard_map/ppermute | solution.py:74
  43.9 1.5 %shrink.1 = (f32[128,48]{1,0:T(8,128)S(1)}, bf16[16,640]{1,0:T(8,128)(2,1)S(1)}) custom-call(s32[8]{0:T(128)S(1)} %copy-done.6, s32[16]{0:T(128)S(1)} %copy-done.7, bf16[128,4096]{1,0:T(8,128)(2,1)S(1)} %copy-done.1, bf16[2,16,4736]{2,1,0:T(8,128)(2,1)S(1)} %get-tuple-element.10.refs_0_, bf16[2,16,4736]{2,1,0:T(8,128)(2,1)S(1)} %collective-permute-done.2.refs_1_, ...), custom_call_target="tpu_custom_call" | custom-call | flops 50331648 | bytes 1048576 | tf_op jit(solution)/shard_map/shrink/pallas_call | solution.py:139
  46.1 0.8 %collective-permute-done.14.small_other = bf16[16,640]{1,0:T(8,128)(2,1)S(1)} collective-permute-done((bf16[16,640]{1,0:T(8,128)(2,1)S(1)}, bf16[16,640]{1,0:T(8,128)(2,1)S(1)}, u32[]{:S(2)}, u32[]{:S(2)}) %collective-permute-start.14) | collective-permute-done | bytes 20512 | tf_op jit(solution)/shard_map/ppermute | solution.py:329
  46.9 2.3 %collective-permute-done.16.refs_3_ = bf16[1,16,4096]{2,1,0:T(8,128)(2,1)S(1)} collective-permute-done((bf16[1,16,4096]{2,1,0:T(8,128)(2,1)S(1)}, bf16[1,16,4096]{2,1,0:T(8,128)(2,1)S(1)}, u32[]{:S(2)}, u32[]{:S(2)}) %collective-permute-start.16) | collective-permute-done | bytes 131104 | tf_op jit(solution)/shard_map/ppermute | solution.py:74
  49.2 3.8 %attention.1 = bf16[128,4096]{1,0:T(8,128)(2,1)} custom-call(s32[8]{0:T(128)S(1)} %copy-done.6, s32[16]{0:T(128)S(1)} %copy-done.7, s32[2]{0:T(128)S(1)} %pad_add_fusion.place, f32[128,384]{1,0:T(8,128)S(1)} %pad_maximum_fusion.3.refs_2_.base_own, f32[128,384]{1,0:T(8,128)S(1)} %collective-permute-done.1.base_other, ...), custom_call_target="tpu_custom_call" | custom-call | flops 536870912 | bytes 4194304 | tf_op jit(solution)/shard_map/attention/pallas_call | solution.py:281
  (44 shorter events, 2.3 us)
Async XLA Ops:
  0.0 16.3 %copy-start = (bf16[8192,128]{1,0:T(8,128)(2,1)S(1)}, bf16[8192,128]{1,0:T(8,128)(2,1)}, u32[]{:S(2)}) copy-start(bf16[8192,128]{1,0:T(8,128)(2,1)} %param.16) | copy-start | bytes 6291460
  0.0 25.1 %collective-permute-start.7 = (bf16[256,8192]{1,0:T(8,128)(2,1)}, bf16[256,8192]{1,0:T(8,128)(2,1)}, u32[]{:S(2)}, u32[]{:S(2)}) collective-permute-start(bf16[256,8192]{1,0:T(8,128)(2,1)} %param.17), channel_id=1, source_target_pairs={{0,1},{1,0},{2,3},{3,2},{4,5},{5,4},{6,7},{7,6},{8,9},{9,8},{10,11... | collective-permute-start | bytes 12582920 | tf_op jit(solution)/shard_map/ppermute | solution.py:329
  0.5 12.6 %collective-permute-start = (bf16[128,4096]{1,0:T(8,128)(2,1)}, bf16[128,4096]{1,0:T(8,128)(2,1)}, u32[]{:S(2)}, u32[]{:S(2)}) collective-permute-start(bf16[128,4096]{1,0:T(8,128)(2,1)} %rows_ref.1), channel_id=1, source_target_pairs={{0,1},{1,0},{2,3},{3,2},{4,5},{5,4},{6,7},{7,6},{8,9},{9,8},{10,11... | collective-permute-start | bytes 3145736 | tf_op jit(solution)/shard_map/ppermute | solution.py:329
  0.5 1.2 %copy-start.3 = (bf16[2,48,4096]{2,1,0:T(8,128)(2,1)S(1)}, bf16[2,48,4096]{2,1,0:T(8,128)(2,1)}, u32[]{:S(2)}) copy-start(bf16[2,48,4096]{2,1,0:T(8,128)(2,1)} %down.1) | copy-start | bytes 2359300
  1.8 0.7 %copy-start.8 = (bf16[2,16,256]{2,1,0:T(8,128)(2,1)S(1)}, bf16[2,16,256]{2,1,0:T(8,128)(2,1)}, u32[]{:S(2)}) copy-start(bf16[2,16,256]{2,1,0:T(8,128)(2,1)} %refs_0_.4) | copy-start | bytes 49156
  2.5 0.7 %copy-start.9 = (bf16[2,16,256]{2,1,0:T(8,128)(2,1)S(1)}, bf16[2,16,256]{2,1,0:T(8,128)(2,1)}, u32[]{:S(2)}) copy-start(bf16[2,16,256]{2,1,0:T(8,128)(2,1)} %refs_2_.1) | copy-start | bytes 49156
  3.2 0.7 %copy-start.10 = (bf16[2,16,128]{2,1,0:T(8,128)(2,1)S(1)}, bf16[2,16,128]{2,1,0:T(8,128)(2,1)}, u32[]{:S(2)}) copy-start(bf16[2,16,128]{2,1,0:T(8,128)(2,1)} %refs_1_.1) | copy-start | bytes 24580
  4.0 13.1 %collective-permute-start.2 = (bf16[2,16,4736]{2,1,0:T(8,128)(2,1)S(1)}, bf16[2,16,4736]{2,1,0:T(8,128)(2,1)S(1)}, u32[]{:S(2)}, u32[]{:S(2)}) collective-permute-start(bf16[2,16,4736]{2,1,0:T(8,128)(2,1)S(1)} %get-tuple-element.10.refs_0_), channel_id=1, source_target_pairs={{0,2},{2,0},{4,6},{6,4},{8,10},{10,8},{12,14},{14,12},{1,3},{3,1},... | collective-permute-start | bytes 909320 | tf_op jit(solution)/shard_map/ppermute | solution.py:70
  7.1 14.2 %collective-permute-start.6 = (bf16[2,16,4096]{2,1,0:T(8,128)(2,1)S(1)}, bf16[2,16,4096]{2,1,0:T(8,128)(2,1)S(1)}, u32[]{:S(2)}, u32[]{:S(2)}) collective-permute-start(bf16[2,16,4096]{2,1,0:T(8,128)(2,1)S(1)} %get-tuple-element.12.refs_0_.refs_4_), channel_id=1, source_target_pairs={{0,4},{2,6},{4,0},{6,2},{8,12},{10,14},{12,8},{14,10},{1,5},{3,7},... | collective-permute-start | bytes 786440 | tf_op jit(solution)/shard_map/ppermute | solution.py:70
  8.6 13.4 %collective-permute-start.5 = (bf16[2,16,4096]{2,1,0:T(8,128)(2,1)S(1)}, bf16[2,16,4096]{2,1,0:T(8,128)(2,1)}, u32[]{:S(2)}, u32[]{:S(2)}) collective-permute-start(bf16[2,16,4096]{2,1,0:T(8,128)(2,1)S(1)} %get-tuple-element.11.refs_0_.refs_8_), channel_id=1, source_target_pairs={{0,8},{2,10},{4,12},{6,14},{8,0},{10,2},{12,4},{14,6},{1,9},{3,11}... | collective-permute-start | bytes 786440 | tf_op jit(solution)/shard_map/ppermute | solution.py:70
  11.2 1.9 %copy-start.2 = (bf16[2,16,4096]{2,1,0:T(8,128)(2,1)S(1)}, bf16[2,16,4096]{2,1,0:T(8,128)(2,1)}, u32[]{:S(2)}) copy-start(bf16[2,16,4096]{2,1,0:T(8,128)(2,1)} %refs_0_.7) | copy-start | bytes 786436
  11.2 2.4 %copy-start.1 = (bf16[128,4096]{1,0:T(8,128)(2,1)S(1)}, bf16[128,4096]{1,0:T(8,128)(2,1)}, u32[]{:S(2)}) copy-start(bf16[128,4096]{1,0:T(8,128)(2,1)} %rows_ref.1) | copy-start | bytes 3145732
  13.1 2.5 %copy-start.11 = (bf16[8192,256]{1,0:T(8,128)(2,1)S(1)}, bf16[8192,256]{1,0:T(8,128)(2,1)}, u32[]{:S(2)}) copy-start(bf16[8192,256]{1,0:T(8,128)(2,1)} %param.15) | copy-start | bytes 12582916
  13.1 13.7 %collective-permute-start.4 = (bf16[2,16,4096]{2,1,0:T(8,128)(2,1)S(1)}, bf16[2,16,4096]{2,1,0:T(8,128)(2,1)S(1)}, u32[]{:S(2)}, u32[]{:S(2)}) collective-permute-start(bf16[2,16,4096]{2,1,0:T(8,128)(2,1)S(1)} %copy-done.2), channel_id=1, source_target_pairs={{0,2},{2,0},{4,6},{6,4},{8,10},{10,8},{12,14},{14,12},{1,3},{3,1},... | collective-permute-start | bytes 786440 | tf_op jit(solution)/shard_map/ppermute | solution.py:70
  16.3 0.8 %copy-start.6 = (s32[8]{0:T(128)S(1)}, s32[8]{0:T(128)}, u32[]{:S(2)}) copy-start(s32[8]{0:T(128)} %requests.19) | copy-start | bytes 100
  16.3 0.8 %copy-start.7 = (s32[16]{0:T(128)S(1)}, s32[16]{0:T(128)}, u32[]{:S(2)}) copy-start(s32[16]{0:T(128)} %pool.19) | copy-start | bytes 196
  17.8 10.9 %collective-permute-start.3 = (bf16[2,16,4736]{2,1,0:T(8,128)(2,1)S(1)}, bf16[2,16,4736]{2,1,0:T(8,128)(2,1)S(1)}, u32[]{:S(2)}, u32[]{:S(2)}) collective-permute-start(bf16[2,16,4736]{2,1,0:T(8,128)(2,1)S(1)} %pick.8.refs_2_), channel_id=1, source_target_pairs={{0,4},{2,6},{4,0},{6,2},{8,12},{10,14},{12,8},{14,10},{1,5},{3,7},... | collective-permute-start | bytes 909320 | tf_op jit(solution)/shard_map/ppermute | solution.py:74
  21.9 10.9 %collective-permute-start.9 = (bf16[2,16,4096]{2,1,0:T(8,128)(2,1)S(1)}, bf16[2,16,4096]{2,1,0:T(8,128)(2,1)S(1)}, u32[]{:S(2)}, u32[]{:S(2)}) collective-permute-start(bf16[2,16,4096]{2,1,0:T(8,128)(2,1)S(1)} %pick.9.refs_2_), channel_id=1, source_target_pairs={{0,2},{2,0},{4,6},{6,4},{8,10},{10,8},{12,14},{14,12},{1,3},{3,1},... | collective-permute-start | bytes 786440 | tf_op jit(solution)/shard_map/ppermute | solution.py:74
  23.0 10.8 %collective-permute-start.11 = (bf16[2,16,4096]{2,1,0:T(8,128)(2,1)S(1)}, bf16[2,16,4096]{2,1,0:T(8,128)(2,1)S(1)}, u32[]{:S(2)}, u32[]{:S(2)}) collective-permute-start(bf16[2,16,4096]{2,1,0:T(8,128)(2,1)S(1)} %pick.10.refs_2_), channel_id=1, source_target_pairs={{0,2},{2,0},{4,6},{6,4},{8,10},{10,8},{12,14},{14,12},{1,3},{3,1},... | collective-permute-start | bytes 786440 | tf_op jit(solution)/shard_map/ppermute | solution.py:74
  27.5 10.7 %collective-permute-start.15 = (bf16[2,16,4096]{2,1,0:T(8,128)(2,1)S(1)}, bf16[2,16,4096]{2,1,0:T(8,128)(2,1)S(1)}, u32[]{:S(2)}, u32[]{:S(2)}) collective-permute-start(bf16[2,16,4096]{2,1,0:T(8,128)(2,1)S(1)} %pick.11.refs_3_), channel_id=1, source_target_pairs={{0,4},{2,6},{4,0},{6,2},{8,12},{10,14},{12,8},{14,10},{1,5},{3,7},... | collective-permute-start | bytes 786440 | tf_op jit(solution)/shard_map/ppermute | solution.py:74
  29.3 14.7 %collective-permute-start.8 = (bf16[1,16,4736]{2,1,0:T(8,128)(2,1)S(1)}, bf16[1,16,4736]{2,1,0:T(8,128)(2,1)S(1)}, u32[]{:S(2)}, u32[]{:S(2)}) collective-permute-start(bf16[1,16,4736]{2,1,0:T(8,128)(2,1)S(1)} %pick.12.refs_3_), channel_id=1, source_target_pairs={{0,8},{2,10},{4,12},{6,14},{8,0},{10,2},{12,4},{14,6},{1,9},{3,11}... | collective-permute-start | bytes 454664 | tf_op jit(solution)/shard_map/ppermute | solution.py:74
  34.9 9.1 %collective-permute-start.12 = (bf16[1,16,4096]{2,1,0:T(8,128)(2,1)S(1)}, bf16[1,16,4096]{2,1,0:T(8,128)(2,1)S(1)}, u32[]{:S(2)}, u32[]{:S(2)}) collective-permute-start(bf16[1,16,4096]{2,1,0:T(8,128)(2,1)S(1)} %pick.14.refs_3_), channel_id=1, source_target_pairs={{0,4},{2,6},{4,0},{6,2},{8,12},{10,14},{12,8},{14,10},{1,5},{3,7},... | collective-permute-start | bytes 393224 | tf_op jit(solution)/shard_map/ppermute | solution.py:74
  34.9 9.0 %collective-permute-start.10 = (bf16[1,16,4096]{2,1,0:T(8,128)(2,1)S(1)}, bf16[1,16,4096]{2,1,0:T(8,128)(2,1)S(1)}, u32[]{:S(2)}, u32[]{:S(2)}) collective-permute-start(bf16[1,16,4096]{2,1,0:T(8,128)(2,1)S(1)} %pick.13.refs_3_), channel_id=1, source_target_pairs={{0,8},{2,10},{4,12},{6,14},{8,0},{10,2},{12,4},{14,6},{1,9},{3,11}... | collective-permute-start | bytes 393224 | tf_op jit(solution)/shard_map/ppermute | solution.py:74
  38.1 8.0 %collective-permute-start.1 = (f32[128,384]{1,0:T(8,128)S(1)}, f32[128,384]{1,0:T(8,128)S(1)}, u32[]{:S(2)}, u32[]{:S(2)}) collective-permute-start(f32[128,384]{1,0:T(8,128)S(1)} %pad_maximum_fusion.3.refs_2_.base_own), channel_id=1, source_target_pairs={{0,1},{1,0},{2,3},{3,2},{4,5},{5,4},{6,7},{7,6},{8,9},{9,8},{10,11... | collective-permute-start | bytes 589832 | tf_op jit(solution)/shard_map/ppermute | solution.py:329
  38.8 10.5 %copy-start.4 = (f32[128,128]{1,0:T(8,128)S(1)}, f32[128,128]{1,0:T(8,128)}, u32[]{:S(2)}) copy-start(f32[128,128]{1,0:T(8,128)} %constant.14.clone.cosine) | copy-start | bytes 196612
  38.8 10.5 %copy-start.5 = (f32[128,128]{1,0:T(8,128)S(1)}, f32[128,128]{1,0:T(8,128)}, u32[]{:S(2)}) copy-start(f32[128,128]{1,0:T(8,128)} %constant.15.clone.sine) | copy-start | bytes 196612
  38.8 10.5 %collective-permute-start.16 = (bf16[1,16,4096]{2,1,0:T(8,128)(2,1)S(1)}, bf16[1,16,4096]{2,1,0:T(8,128)(2,1)S(1)}, u32[]{:S(2)}, u32[]{:S(2)}) collective-permute-start(bf16[1,16,4096]{2,1,0:T(8,128)(2,1)S(1)} %pick.15), channel_id=1, source_target_pairs={{0,8},{2,10},{4,12},{6,14},{8,0},{10,2},{12,4},{14,6},{1,9},{3,11}... | collective-permute-start | bytes 393224 | tf_op jit(solution)/shard_map/ppermute | solution.py:74
  45.5 1.4 %collective-permute-start.13 = (f32[128,48]{1,0:T(8,128)S(1)}, f32[128,48]{1,0:T(8,128)S(1)}, u32[]{:S(2)}, u32[]{:S(2)}) collective-permute-start(f32[128,48]{1,0:T(8,128)S(1)} %get-tuple-element.13.shrink_own), channel_id=1, source_target_pairs={{0,1},{1,0},{2,3},{3,2},{4,5},{5,4},{6,7},{7,6},{8,9},{9,8},{10,11... | collective-permute-start | bytes 73736 | tf_op jit(solution)/shard_map/ppermute | solution.py:329
  45.5 1.3 %collective-permute-start.14 = (bf16[16,640]{1,0:T(8,128)(2,1)S(1)}, bf16[16,640]{1,0:T(8,128)(2,1)S(1)}, u32[]{:S(2)}, u32[]{:S(2)}) collective-permute-start(bf16[16,640]{1,0:T(8,128)(2,1)S(1)} %get-tuple-element.14.small_own), channel_id=1, source_target_pairs={{0,1},{1,0},{2,3},{3,2},{4,5},{5,4},{6,7},{7,6},{8,9},{9,8},{10,11... | collective-permute-start | bytes 61448 | tf_op jit(solution)/shard_map/ppermute | solution.py:329

commit v4 on v3

--- a/solution.py
+++ b/solution.py
@@ -149,40 +149,6 @@
         cost_estimate=cost(2 * rows * half * rank * len(routes), 2 * rows * half),
         name="shrink",
     )(*routes[0].tables, tokens, *arrays)
-
-
-def cut_parts(down_maps, small, rank):
-    count, _, half = down_maps.shape
-    width = sum(each.shape[2] for each in small)
-
-    def kernel(down, *refs):
-        small_refs, outs, sems = refs[:-4], refs[-4:-1], refs[-1]
-        copies = [
-            pltpu.make_async_copy(
-                down.at[:, pl.ds(i * rank, rank), :], out.at[:, :, pl.ds(0, half)], sems.at[i])
-            for i, out in enumerate(outs)
-        ]
-        at = half
-        for i, each in enumerate(small_refs):
-            more = each.shape[2]
-            copies.append(pltpu.make_async_copy(each, outs[0].at[:, :, pl.ds(at, more)], sems.at[len(outs) + i]))
-            at += more
-        for copy in copies:
-            copy.start()
-        for copy in copies:
-            copy.wait()
-
-    return pl.pallas_call(
-        kernel,
-        in_specs=[ANY] * (1 + len(small)),
-        out_specs=(VMEM,) * 3,
-        out_shape=tuple(
-            jax.ShapeDtypeStruct((count, rank, half + more), down_maps.dtype) for more in (width, 0, 0)),
-        scratch_shapes=[pltpu.SemaphoreType.DMA((3 + len(small),))],
-        compiler_params=params(4),
-        cost_estimate=cost(0, 1 << 20),
-        name="cut",
-    )(down_maps, *small)
 
 
 def rotary_tables(rows, width):
@@ -335,7 +301,8 @@
     def route(part, order):
         return Route(part, order, devices, request_adapter, adapter_pool_row)
 
-    parts = cut_parts(adapter_down_maps, small, rank)
+    down = [adapter_down_maps[:, i * rank:(i + 1) * rank] for i in range(3)]
+    parts = (jnp.concatenate([down[0], *small], axis=2), down[1], down[2])
     first_route, second_route, third_route = (
         route(part, order) for part, order in zip(parts, (first, second, third)))
     routes = [first_route, second_route, third_route]

time: 53.5 us -> 52 us (0.972)
  waiting for transfers between devices: 6.63 us -> 12.6 us
  starting transfers between devices: 24 us -> 18.2 us
  local copies, waits for them, and re-layouts: 7.23 us -> 5.13 us
  other arithmetic: 1.74 us -> 2.52 us
    ppermute x8, waiting for transfers between devices: 2.85 us -> 9.2 us  [step(): self.packets.append(lax.ppermute(out, 'serve', pairs))]
    ppermute x8, starting transfers between devices: 15.2 us -> 9.32 us  [step(): self.packets.append(lax.ppermute(out, 'serve', pairs))]
    unnamed x24 -> x16, local copies, waits for them, and re-layouts: 3.68 us -> 0.31 us
    slice x0 -> x1, local copies, waits for them, and re-layouts: none -> 1.26 us  [local(): down = [adapter_down_maps[:, i * rank:(i + 1) * rank] for i in range(3)]]
    concatenate x0 -> x1, other arithmetic: none -> 0.78 us  [local(): parts = (jnp.concatenate([down[0], *small], axis=2), down[1], down[2])]
  transfers between devices with their start and end apart: 17 -> 17, of which waited for: 5 -> 8; matrix products, arithmetic and copies ran while one was open for 13% -> 17% of each run, Pallas kernels for 14% -> 14%
where the time goes in v4:
time: 52 us; the launch traced here: 51.7 us
  starting transfers between devices  18.2 us (35%)
  waiting for transfers between devices  12.6 us (24%)
  Pallas kernels  10.9 us (21%)
  local copies, waits for them, and re-layouts  5.13 us (10%)
  other arithmetic  2.52 us (5%)
  matrix products  1.45 us (3%)
  between operations  0.9 us (2%)
    ppermute x8, starting transfers between devices, step(): self.packets.append(lax.ppermute(out, 'serve', pairs))  9.32 us
    ppermute x8, waiting for transfers between devices, step(): self.packets.append(lax.ppermute(out, 'serve', pairs))  9.2 us
    ppermute x4, starting transfers between devices, step(): self.parts += [lax.ppermute(part, 'serve', pairs) for part in self.parts]  7.77 us
    pallas_call x8, Pallas kernels, pick(): pl.pallas_call(kernel, in_specs=[SMEM, SMEM] + [VMEM] * len(arrays) + [AN...  5.56 us
    pallas_call x1, Pallas kernels, attention(): pl.pallas_call(functools.partial(attention_kernel, query_columns=query_co...  3.79 us
    dynamic_slice x2, local copies, waits for them, and re-layouts, local(): lax.dynamic_slice_in_dim(weight, tensor * half, half, 1)  3.56 us
    ppermute x4, waiting for transfers between devices, step(): self.parts += [lax.ppermute(part, 'serve', pairs) for part in self.parts]  2.63 us
    select_n x1, other arithmetic, base_products(): low = jnp.where(first, own_tokens, other_tokens)  1.65 us
  transfers between devices with their start and end apart: 17, of which 8 were waited for; matrix products, arithmetic and copies ran while one was open for 17% of the time, Pallas kernels for 14%

profile of v4, /device:TPU:0, one launch (start us, length us, event | category | flops | bytes accessed | tf_op | source)
XLA Modules:
  0.0 51.7 jit_solution(11927258092157940672)
XLA Ops:
  0.5 1.3 %fusion.4 = (bf16[2,16,4096]{2,1,0:T(8,128)(2,1)S(1)}, bf16[2,16,4096]{2,1,0:T(8,128)(2,1)S(1)}, bf16[2,16,4096]{2,1,0:T(8,128)(2,1)S(1)}) fusion(bf16[2,48,4096]{2,1,0:T(8,128)(2,1)} %param.18), kind=kLoop, calls=%fused_computation.12 | loop fusion | bytes 1572864 | tf_op jit(solution)/shard_map/slice | solution.py:304
  1.8 0.8 %pad_maximum_fusion.3.refs_0_ = bf16[2,16,4736]{2,1,0:T(8,128)(2,1)S(1)} fusion(bf16[2,16,256]{2,1,0:T(8,128)(2,1)} %param.21, bf16[2,16,128]{2,1,0:T(8,128)(2,1)} %param.20, bf16[2,16,256]{2,1,0:T(8,128)(2,1)} %param.19, bf16[2,16,4096]{2,1,0:T(8,128)(2,1)S(1)} %get-tuple-element.12), kind=kLoop, calls=%fused_computation.5 | loop fusion | flops 1212416 | bytes 606208 | tf_op jit(solution)/shard_map/concatenate | solution.py:305
  2.6 3.0 %collective-permute-start.2 = (bf16[2,16,4736]{2,1,0:T(8,128)(2,1)S(1)}, bf16[2,16,4736]{2,1,0:T(8,128)(2,1)S(1)}, u32[]{:S(2)}, u32[]{:S(2)}) collective-permute-start(bf16[2,16,4736]{2,1,0:T(8,128)(2,1)S(1)} %pad_maximum_fusion.3.refs_0_), channel_id=1, source_target_pairs={{0,2},{2,0},{4,6},{6,4},{8,10},{10,8},{12,14},{14,12},{1,3},{3,1},... | collective-permute-start | bytes 909320 | tf_op jit(solution)/shard_map/ppermute | solution.py:70
  5.6 1.6 %collective-permute-start.6 = (bf16[2,16,4096]{2,1,0:T(8,128)(2,1)S(1)}, bf16[2,16,4096]{2,1,0:T(8,128)(2,1)S(1)}, u32[]{:S(2)}, u32[]{:S(2)}) collective-permute-start(bf16[2,16,4096]{2,1,0:T(8,128)(2,1)S(1)} %get-tuple-element.11.refs_0_.refs_4_), channel_id=1, source_target_pairs={{0,4},{2,6},{4,0},{6,2},{8,12},{10,14},{12,8},{14,10},{1,5},{3,7},... | collective-permute-start | bytes 786440 | tf_op jit(solution)/shard_map/ppermute | solution.py:70
  7.2 2.6 %collective-permute-start.5 = (bf16[2,16,4096]{2,1,0:T(8,128)(2,1)S(1)}, bf16[2,16,4096]{2,1,0:T(8,128)(2,1)}, u32[]{:S(2)}, u32[]{:S(2)}) collective-permute-start(bf16[2,16,4096]{2,1,0:T(8,128)(2,1)S(1)} %get-tuple-element.13.refs_0_.refs_8_), channel_id=1, source_target_pairs={{0,8},{2,10},{4,12},{6,14},{8,0},{10,2},{12,4},{14,6},{1,9},{3,11}... | collective-permute-start | bytes 786440 | tf_op jit(solution)/shard_map/ppermute | solution.py:70
  9.8 1.8 %constant_dynamic-slice_fusion.1.refs_3_.weight_own = bf16[256,4096]{1,0:T(8,128)(2,1)S(1)} fusion(bf16[256,8192]{1,0:T(8,128)(2,1)} %param.17, s32[]{:T(128)S(6)} %select_n.19), kind=kLoop, calls=%fused_computation.9 | loop fusion | bytes 4194308 | tf_op jit(solution)/shard_map/dynamic_slice | solution.py:317
  11.6 0.6 %collective-permute-start.4 = (bf16[2,16,4096]{2,1,0:T(8,128)(2,1)S(1)}, bf16[2,16,4096]{2,1,0:T(8,128)(2,1)S(1)}, u32[]{:S(2)}, u32[]{:S(2)}) collective-permute-start(bf16[2,16,4096]{2,1,0:T(8,128)(2,1)S(1)} %copy-done.2), channel_id=1, source_target_pairs={{0,2},{2,0},{4,6},{6,4},{8,10},{10,8},{12,14},{14,12},{1,3},{3,1},... | collective-permute-start | bytes 786440 | tf_op jit(solution)/shard_map/ppermute | solution.py:70
  12.2 1.7 %broadcast_select_fusion.1 = (bf16[128,4096]{1,0:T(8,128)(2,1)S(1)}, bf16[128,4096]{1,0:T(8,128)(2,1)S(1)}) fusion(bf16[128,4096]{1,0:T(8,128)(2,1)S(1)} %copy-done.1, bf16[128,4096]{1,0:T(8,128)(2,1)} %collective-permute-done, pred[]{:T(512)S(6)} %eq.3), kind=kLoop, calls=%fused_computation.4 | loop fusion | flops 1048576 | bytes 4194305 | tf_op jit(solution)/shard_map/jit(_where)/select_n | solution.py:107
  14.1 0.7 %fusion.1 = f32[128,256]{1,0:T(8,128)S(1)} fusion(bf16[8192,256]{1,0:T(8,128)(2,1)S(1)} %copy-done.7, bf16[128,4096]{1,0:T(8,128)(2,1)S(1)} %get-tuple-element.10, bf16[128,4096]{1,0:T(8,128)(2,1)S(1)} %get-tuple-element.9), kind=kOutput, calls=%fused_computation.2 | convolution fusion | flops 541065216 | bytes 6422528 | tf_op jit(solution)/shard_map/dot_general | solution.py:113
  14.9 0.7 %fusion = f32[128,128]{1,0:T(8,128)S(1)} fusion(bf16[8192,128]{1,0:T(8,128)(2,1)S(1)} %copy-done, bf16[128,4096]{1,0:T(8,128)(2,1)S(1)} %get-tuple-element.10, bf16[128,4096]{1,0:T(8,128)(2,1)S(1)} %get-tuple-element.9), kind=kOutput, calls=%fused_computation.1 | convolution fusion | flops 272629760 | bytes 4259840 | tf_op jit(solution)/shard_map/dot_general | solution.py:113
  15.7 0.6 %pick.8.refs_2_ = bf16[2,16,4736]{2,1,0:T(8,128)(2,1)S(1)} custom-call(s32[8]{0:T(128)S(1)} %copy-done.5, s32[16]{0:T(128)S(1)} %copy-done.6, bf16[2,16,4736]{2,1,0:T(8,128)(2,1)S(1)} %pad_maximum_fusion.3.refs_0_, bf16[2,16,4736]{2,1,0:T(8,128)(2,1)S(1)} %collective-permute-done.2.refs_1_, f32[128,384]{1,0:T(8,128)S(1)} %pad_maximum_fusion.4.refs_2_.base_own), custom_call_target="tpu_custom_call" | custom-call | bytes 606208 | tf_op jit(solution)/shard_map/pick/pallas_call | solution.py:93
  16.3 0.9 %collective-permute-start.3 = (bf16[2,16,4736]{2,1,0:T(8,128)(2,1)S(1)}, bf16[2,16,4736]{2,1,0:T(8,128)(2,1)S(1)}, u32[]{:S(2)}, u32[]{:S(2)}) collective-permute-start(bf16[2,16,4736]{2,1,0:T(8,128)(2,1)S(1)} %pick.8.refs_2_), channel_id=1, source_target_pairs={{0,4},{2,6},{4,0},{6,2},{8,12},{10,14},{12,8},{14,10},{1,5},{3,7},... | collective-permute-start | bytes 909320 | tf_op jit(solution)/shard_map/ppermute | solution.py:74
  17.2 2.6 %collective-permute-done.6.refs_1_.refs_5_ = bf16[2,16,4096]{2,1,0:T(8,128)(2,1)S(1)} collective-permute-done((bf16[2,16,4096]{2,1,0:T(8,128)(2,1)S(1)}, bf16[2,16,4096]{2,1,0:T(8,128)(2,1)S(1)}, u32[]{:S(2)}, u32[]{:S(2)}) %collective-permute-start.6) | collective-permute-done | bytes 262176 | tf_op jit(solution)/shard_map/ppermute | solution.py:70
  19.7 0.6 %pick.9.refs_2_ = bf16[2,16,4096]{2,1,0:T(8,128)(2,1)S(1)} custom-call(s32[8]{0:T(128)S(1)} %copy-done.5, s32[16]{0:T(128)S(1)} %copy-done.6, bf16[2,16,4096]{2,1,0:T(8,128)(2,1)S(1)} %get-tuple-element.11.refs_0_.refs_4_, bf16[2,16,4096]{2,1,0:T(8,128)(2,1)S(1)} %collective-permute-done.6.refs_1_.refs_5_, bf16[2,16,4736]{2,1,0:T(8,128)(2,1)S(1)} %pick.8.refs_2_), custom_call_target="tpu_custom_call" | custom-call | bytes 524288 | tf_op jit(solution)/shard_map/pick/pallas_call | solution.py:93
  20.6 1.0 %pick.10.refs_2_ = bf16[2,16,4096]{2,1,0:T(8,128)(2,1)S(1)} custom-call(s32[8]{0:T(128)S(1)} %copy-done.5, s32[16]{0:T(128)S(1)} %copy-done.6, bf16[2,16,4096]{2,1,0:T(8,128)(2,1)S(1)} %get-tuple-element.13.refs_0_.refs_8_, bf16[2,16,4096]{2,1,0:T(8,128)(2,1)} %collective-permute-done.5.refs_1_.refs_9_, bf16[2,16,4096]{2,1,0:T(8,128)(2,1)S(1)} %pick.9.refs_2_), custom_call_target="tpu_custom_call" | custom-call | bytes 524288 | tf_op jit(solution)/shard_map/pick/pallas_call | solution.py:93
  21.6 1.9 %collective-permute-start.11 = (bf16[2,16,4096]{2,1,0:T(8,128)(2,1)S(1)}, bf16[2,16,4096]{2,1,0:T(8,128)(2,1)S(1)}, u32[]{:S(2)}, u32[]{:S(2)}) collective-permute-start(bf16[2,16,4096]{2,1,0:T(8,128)(2,1)S(1)} %pick.10.refs_2_), channel_id=1, source_target_pairs={{0,2},{2,0},{4,6},{6,4},{8,10},{10,8},{12,14},{14,12},{1,3},{3,1},... | collective-permute-start | bytes 786440 | tf_op jit(solution)/shard_map/ppermute | solution.py:74
  23.5 1.7 %constant_dynamic-slice_fusion.refs_4_.weight_other = bf16[256,4096]{1,0:T(8,128)(2,1)S(1)} fusion(bf16[256,8192]{1,0:T(8,128)(2,1)} %collective-permute-done.7, s32[]{:T(128)S(6)} %select_n.19), kind=kLoop, calls=%fused_computation.8 | loop fusion | bytes 4194308 | tf_op jit(solution)/shard_map/dynamic_slice | solution.py:317
  25.3 0.6 %pick.11.refs_3_ = bf16[2,16,4096]{2,1,0:T(8,128)(2,1)S(1)} custom-call(s32[8]{0:T(128)S(1)} %copy-done.5, s32[16]{0:T(128)S(1)} %copy-done.6, bf16[2,16,4096]{2,1,0:T(8,128)(2,1)S(1)} %copy-done.2, bf16[2,16,4096]{2,1,0:T(8,128)(2,1)S(1)} %collective-permute-done.4.refs_1_, bf16[2,16,4096]{2,1,0:T(8,128)(2,1)S(1)} %pick.10.refs_2_, ...), custom_call_target="tpu_custom_call" | custom-call | bytes 524288 | tf_op jit(solution)/shard_map/pick/pallas_call | solution.py:93
  25.9 1.0 %collective-permute-start.15 = (bf16[2,16,4096]{2,1,0:T(8,128)(2,1)S(1)}, bf16[2,16,4096]{2,1,0:T(8,128)(2,1)S(1)}, u32[]{:S(2)}, u32[]{:S(2)}) collective-permute-start(bf16[2,16,4096]{2,1,0:T(8,128)(2,1)S(1)} %pick.11.refs_3_), channel_id=1, source_target_pairs={{0,4},{2,6},{4,0},{6,2},{8,12},{10,14},{12,8},{14,10},{1,5},{3,7},... | collective-permute-start | bytes 786440 | tf_op jit(solution)/shard_map/ppermute | solution.py:74
  26.9 0.6 %pick.12.refs_3_ = bf16[1,16,4736]{2,1,0:T(8,128)(2,1)S(1)} custom-call(s32[8]{0:T(128)S(1)} %copy-done.5, s32[16]{0:T(128)S(1)} %copy-done.6, bf16[2,16,4736]{2,1,0:T(8,128)(2,1)S(1)} %pad_maximum_fusion.3.refs_0_, bf16[2,16,4736]{2,1,0:T(8,128)(2,1)S(1)} %collective-permute-done.2.refs_1_, bf16[2,16,4736]{2,1,0:T(8,128)(2,1)S(1)} %collective-permute-done.3.refs_2_, ...), custom_call_target="tpu_custom_call" | custom-call | bytes 303104 | tf_op jit(solution)/shard_map/pick/pallas_call | solution.py:93
  27.5 2.0 %collective-permute-start.8 = (bf16[1,16,4736]{2,1,0:T(8,128)(2,1)S(1)}, bf16[1,16,4736]{2,1,0:T(8,128)(2,1)S(1)}, u32[]{:S(2)}, u32[]{:S(2)}) collective-permute-start(bf16[1,16,4736]{2,1,0:T(8,128)(2,1)S(1)} %pick.12.refs_3_), channel_id=1, source_target_pairs={{0,8},{2,10},{4,12},{6,14},{8,0},{10,2},{12,4},{14,6},{1,9},{3,11}... | collective-permute-start | bytes 454664 | tf_op jit(solution)/shard_map/ppermute | solution.py:74
  29.6 0.6 %pick.13.refs_3_ = bf16[1,16,4096]{2,1,0:T(8,128)(2,1)S(1)} custom-call(s32[8]{0:T(128)S(1)} %copy-done.5, s32[16]{0:T(128)S(1)} %copy-done.6, bf16[2,16,4096]{2,1,0:T(8,128)(2,1)S(1)} %get-tuple-element.11.refs_0_.refs_4_, bf16[2,16,4096]{2,1,0:T(8,128)(2,1)S(1)} %collective-permute-done.6.refs_1_.refs_5_, ...), custom_call_target="tpu_custom_call" | custom-call | bytes 262144 | tf_op jit(solution)/shard_map/pick/pallas_call | solution.py:93
  30.2 2.2 %collective-permute-done.11.refs_2_.refs_10_ = bf16[2,16,4096]{2,1,0:T(8,128)(2,1)S(1)} collective-permute-done((bf16[2,16,4096]{2,1,0:T(8,128)(2,1)S(1)}, bf16[2,16,4096]{2,1,0:T(8,128)(2,1)S(1)}, u32[]{:S(2)}, u32[]{:S(2)}) %collective-permute-start.11) | collective-permute-done | bytes 262176 | tf_op jit(solution)/shard_map/ppermute | solution.py:74
  32.4 1.0 %pick.14.refs_3_ = bf16[1,16,4096]{2,1,0:T(8,128)(2,1)S(1)} custom-call(s32[8]{0:T(128)S(1)} %copy-done.5, s32[16]{0:T(128)S(1)} %copy-done.6, bf16[2,16,4096]{2,1,0:T(8,128)(2,1)S(1)} %get-tuple-element.13.refs_0_.refs_8_, bf16[2,16,4096]{2,1,0:T(8,128)(2,1)} %collective-permute-done.5.refs_1_.refs_9_, ...), custom_call_target="tpu_custom_call" | custom-call | bytes 262144 | tf_op jit(solution)/shard_map/pick/pallas_call | solution.py:93
  33.5 3.2 %collective-permute-start.10 = (bf16[1,16,4096]{2,1,0:T(8,128)(2,1)S(1)}, bf16[1,16,4096]{2,1,0:T(8,128)(2,1)S(1)}, u32[]{:S(2)}, u32[]{:S(2)}) collective-permute-start(bf16[1,16,4096]{2,1,0:T(8,128)(2,1)S(1)} %pick.13.refs_3_), channel_id=1, source_target_pairs={{0,8},{2,10},{4,12},{6,14},{8,0},{10,2},{12,4},{14,6},{1,9},{3,11}... | collective-permute-start | bytes 393224 | tf_op jit(solution)/shard_map/ppermute | solution.py:74
  36.6 0.6 %pick.15 = bf16[1,16,4096]{2,1,0:T(8,128)(2,1)S(1)} custom-call(s32[8]{0:T(128)S(1)} %copy-done.5, s32[16]{0:T(128)S(1)} %copy-done.6, bf16[2,16,4096]{2,1,0:T(8,128)(2,1)S(1)} %copy-done.2, bf16[2,16,4096]{2,1,0:T(8,128)(2,1)S(1)} %collective-permute-done.4.refs_1_, bf16[2,16,4096]{2,1,0:T(8,128)(2,1)S(1)} %collective-permute-done.15.refs_2_, ...), custom_call_target="tpu_custom_call" | custom-call | bytes 262144 | tf_op jit(solution)/shard_map/pick/pallas_call | solution.py:93
  38.0 2.2 %collective-permute-done.12.refs_11_ = bf16[1,16,4096]{2,1,0:T(8,128)(2,1)S(1)} collective-permute-done((bf16[1,16,4096]{2,1,0:T(8,128)(2,1)S(1)}, bf16[1,16,4096]{2,1,0:T(8,128)(2,1)S(1)}, u32[]{:S(2)}, u32[]{:S(2)}) %collective-permute-start.12) | collective-permute-done | bytes 131104 | tf_op jit(solution)/shard_map/ppermute | solution.py:74
  40.2 1.0 %collective-permute-done.10.refs_7_ = bf16[1,16,4096]{2,1,0:T(8,128)(2,1)S(1)} collective-permute-done((bf16[1,16,4096]{2,1,0:T(8,128)(2,1)S(1)}, bf16[1,16,4096]{2,1,0:T(8,128)(2,1)S(1)}, u32[]{:S(2)}, u32[]{:S(2)}) %collective-permute-start.10) | collective-permute-done | bytes 131104 | tf_op jit(solution)/shard_map/ppermute | solution.py:74
  41.2 1.5 %shrink.1 = (f32[128,48]{1,0:T(8,128)S(1)}, bf16[16,640]{1,0:T(8,128)(2,1)S(1)}) custom-call(s32[8]{0:T(128)S(1)} %copy-done.5, s32[16]{0:T(128)S(1)} %copy-done.6, bf16[128,4096]{1,0:T(8,128)(2,1)S(1)} %copy-done.1, bf16[2,16,4736]{2,1,0:T(8,128)(2,1)S(1)} %pad_maximum_fusion.3.refs_0_, bf16[2,16,4736]{2,1,0:T(8,128)(2,1)S(1)} %collective-permute-done.2.refs_1_, ...), custom_call_target="tpu_custom_call" | custom-call | flops 50331648 | bytes 1048576 | tf_op jit(solution)/shard_map/shrink/pallas_call | solution.py:139
  43.4 0.8 %collective-permute-done.14.small_other = bf16[16,640]{1,0:T(8,128)(2,1)S(1)} collective-permute-done((bf16[16,640]{1,0:T(8,128)(2,1)S(1)}, bf16[16,640]{1,0:T(8,128)(2,1)S(1)}, u32[]{:S(2)}, u32[]{:S(2)}) %collective-permute-start.14) | collective-permute-done | bytes 20512 | tf_op jit(solution)/shard_map/ppermute | solution.py:295
  44.1 3.7 %collective-permute-done.16.refs_3_ = bf16[1,16,4096]{2,1,0:T(8,128)(2,1)S(1)} collective-permute-done((bf16[1,16,4096]{2,1,0:T(8,128)(2,1)S(1)}, bf16[1,16,4096]{2,1,0:T(8,128)(2,1)S(1)}, u32[]{:S(2)}, u32[]{:S(2)}) %collective-permute-start.16) | collective-permute-done | bytes 131104 | tf_op jit(solution)/shard_map/ppermute | solution.py:74
  47.9 3.8 %attention.1 = bf16[128,4096]{1,0:T(8,128)(2,1)} custom-call(s32[8]{0:T(128)S(1)} %copy-done.5, s32[16]{0:T(128)S(1)} %copy-done.6, s32[2]{0:T(128)S(1)} %pad_add_fusion.place, f32[128,384]{1,0:T(8,128)S(1)} %pad_maximum_fusion.4.refs_2_.base_own, f32[128,384]{1,0:T(8,128)S(1)} %collective-permute-done.1.base_other, ...), custom_call_target="tpu_custom_call" | custom-call | flops 536870912 | bytes 4194304 | tf_op jit(solution)/shard_map/attention/pallas_call | solution.py:247
  (37 shorter events, 2.1 us)
Async XLA Ops:
  0.0 14.9 %copy-start = (bf16[8192,128]{1,0:T(8,128)(2,1)S(1)}, bf16[8192,128]{1,0:T(8,128)(2,1)}, u32[]{:S(2)}) copy-start(bf16[8192,128]{1,0:T(8,128)(2,1)} %param.16) | copy-start | bytes 6291460
  0.0 23.5 %collective-permute-start.7 = (bf16[256,8192]{1,0:T(8,128)(2,1)}, bf16[256,8192]{1,0:T(8,128)(2,1)}, u32[]{:S(2)}, u32[]{:S(2)}) collective-permute-start(bf16[256,8192]{1,0:T(8,128)(2,1)} %param.17), channel_id=1, source_target_pairs={{0,1},{1,0},{2,3},{3,2},{4,5},{5,4},{6,7},{7,6},{8,9},{9,8},{10,11... | collective-permute-start | bytes 12582920 | tf_op jit(solution)/shard_map/ppermute | solution.py:295
  0.5 11.2 %collective-permute-start = (bf16[128,4096]{1,0:T(8,128)(2,1)}, bf16[128,4096]{1,0:T(8,128)(2,1)}, u32[]{:S(2)}, u32[]{:S(2)}) collective-permute-start(bf16[128,4096]{1,0:T(8,128)(2,1)} %rows_ref.1), channel_id=1, source_target_pairs={{0,1},{1,0},{2,3},{3,2},{4,5},{5,4},{6,7},{7,6},{8,9},{9,8},{10,11... | collective-permute-start | bytes 3145736 | tf_op jit(solution)/shard_map/ppermute | solution.py:295
  2.6 13.1 %collective-permute-start.2 = (bf16[2,16,4736]{2,1,0:T(8,128)(2,1)S(1)}, bf16[2,16,4736]{2,1,0:T(8,128)(2,1)S(1)}, u32[]{:S(2)}, u32[]{:S(2)}) collective-permute-start(bf16[2,16,4736]{2,1,0:T(8,128)(2,1)S(1)} %pad_maximum_fusion.3.refs_0_), channel_id=1, source_target_pairs={{0,2},{2,0},{4,6},{6,4},{8,10},{10,8},{12,14},{14,12},{1,3},{3,1},... | collective-permute-start | bytes 909320 | tf_op jit(solution)/shard_map/ppermute | solution.py:70
  5.6 14.1 %collective-permute-start.6 = (bf16[2,16,4096]{2,1,0:T(8,128)(2,1)S(1)}, bf16[2,16,4096]{2,1,0:T(8,128)(2,1)S(1)}, u32[]{:S(2)}, u32[]{:S(2)}) collective-permute-start(bf16[2,16,4096]{2,1,0:T(8,128)(2,1)S(1)} %get-tuple-element.11.refs_0_.refs_4_), channel_id=1, source_target_pairs={{0,4},{2,6},{4,0},{6,2},{8,12},{10,14},{12,8},{14,10},{1,5},{3,7},... | collective-permute-start | bytes 786440 | tf_op jit(solution)/shard_map/ppermute | solution.py:70
  7.2 13.4 %collective-permute-start.5 = (bf16[2,16,4096]{2,1,0:T(8,128)(2,1)S(1)}, bf16[2,16,4096]{2,1,0:T(8,128)(2,1)}, u32[]{:S(2)}, u32[]{:S(2)}) collective-permute-start(bf16[2,16,4096]{2,1,0:T(8,128)(2,1)S(1)} %get-tuple-element.13.refs_0_.refs_8_), channel_id=1, source_target_pairs={{0,8},{2,10},{4,12},{6,14},{8,0},{10,2},{12,4},{14,6},{1,9},{3,11}... | collective-permute-start | bytes 786440 | tf_op jit(solution)/shard_map/ppermute | solution.py:70
  9.8 1.9 %copy-start.2 = (bf16[2,16,4096]{2,1,0:T(8,128)(2,1)S(1)}, bf16[2,16,4096]{2,1,0:T(8,128)(2,1)}, u32[]{:S(2)}) copy-start(bf16[2,16,4096]{2,1,0:T(8,128)(2,1)} %refs_0_.5) | copy-start | bytes 786436
  9.8 2.4 %copy-start.1 = (bf16[128,4096]{1,0:T(8,128)(2,1)S(1)}, bf16[128,4096]{1,0:T(8,128)(2,1)}, u32[]{:S(2)}) copy-start(bf16[128,4096]{1,0:T(8,128)(2,1)} %rows_ref.1) | copy-start | bytes 3145732
  11.6 2.5 %copy-start.7 = (bf16[8192,256]{1,0:T(8,128)(2,1)S(1)}, bf16[8192,256]{1,0:T(8,128)(2,1)}, u32[]{:S(2)}) copy-start(bf16[8192,256]{1,0:T(8,128)(2,1)} %param.15) | copy-start | bytes 12582916
  11.6 13.6 %collective-permute-start.4 = (bf16[2,16,4096]{2,1,0:T(8,128)(2,1)S(1)}, bf16[2,16,4096]{2,1,0:T(8,128)(2,1)S(1)}, u32[]{:S(2)}, u32[]{:S(2)}) collective-permute-start(bf16[2,16,4096]{2,1,0:T(8,128)(2,1)S(1)} %copy-done.2), channel_id=1, source_target_pairs={{0,2},{2,0},{4,6},{6,4},{8,10},{10,8},{12,14},{14,12},{1,3},{3,1},... | collective-permute-start | bytes 786440 | tf_op jit(solution)/shard_map/ppermute | solution.py:70
  14.9 0.8 %copy-start.5 = (s32[8]{0:T(128)S(1)}, s32[8]{0:T(128)}, u32[]{:S(2)}) copy-start(s32[8]{0:T(128)} %requests.19) | copy-start | bytes 100
  14.9 0.8 %copy-start.6 = (s32[16]{0:T(128)S(1)}, s32[16]{0:T(128)}, u32[]{:S(2)}) copy-start(s32[16]{0:T(128)} %pool.19) | copy-start | bytes 196
  16.3 10.6 %collective-permute-start.3 = (bf16[2,16,4736]{2,1,0:T(8,128)(2,1)S(1)}, bf16[2,16,4736]{2,1,0:T(8,128)(2,1)S(1)}, u32[]{:S(2)}, u32[]{:S(2)}) collective-permute-start(bf16[2,16,4736]{2,1,0:T(8,128)(2,1)S(1)} %pick.8.refs_2_), channel_id=1, source_target_pairs={{0,4},{2,6},{4,0},{6,2},{8,12},{10,14},{12,8},{14,10},{1,5},{3,7},... | collective-permute-start | bytes 909320 | tf_op jit(solution)/shard_map/ppermute | solution.py:74
  20.3 9.2 %collective-permute-start.9 = (bf16[2,16,4096]{2,1,0:T(8,128)(2,1)S(1)}, bf16[2,16,4096]{2,1,0:T(8,128)(2,1)S(1)}, u32[]{:S(2)}, u32[]{:S(2)}) collective-permute-start(bf16[2,16,4096]{2,1,0:T(8,128)(2,1)S(1)} %pick.9.refs_2_), channel_id=1, source_target_pairs={{0,2},{2,0},{4,6},{6,4},{8,10},{10,8},{12,14},{14,12},{1,3},{3,1},... | collective-permute-start | bytes 786440 | tf_op jit(solution)/shard_map/ppermute | solution.py:74
  21.6 10.8 %collective-permute-start.11 = (bf16[2,16,4096]{2,1,0:T(8,128)(2,1)S(1)}, bf16[2,16,4096]{2,1,0:T(8,128)(2,1)S(1)}, u32[]{:S(2)}, u32[]{:S(2)}) collective-permute-start(bf16[2,16,4096]{2,1,0:T(8,128)(2,1)S(1)} %pick.10.refs_2_), channel_id=1, source_target_pairs={{0,2},{2,0},{4,6},{6,4},{8,10},{10,8},{12,14},{14,12},{1,3},{3,1},... | collective-permute-start | bytes 786440 | tf_op jit(solution)/shard_map/ppermute | solution.py:74
  25.9 10.7 %collective-permute-start.15 = (bf16[2,16,4096]{2,1,0:T(8,128)(2,1)S(1)}, bf16[2,16,4096]{2,1,0:T(8,128)(2,1)S(1)}, u32[]{:S(2)}, u32[]{:S(2)}) collective-permute-start(bf16[2,16,4096]{2,1,0:T(8,128)(2,1)S(1)} %pick.11.refs_3_), channel_id=1, source_target_pairs={{0,4},{2,6},{4,0},{6,2},{8,12},{10,14},{12,8},{14,10},{1,5},{3,7},... | collective-permute-start | bytes 786440 | tf_op jit(solution)/shard_map/ppermute | solution.py:74
  27.5 13.7 %collective-permute-start.8 = (bf16[1,16,4736]{2,1,0:T(8,128)(2,1)S(1)}, bf16[1,16,4736]{2,1,0:T(8,128)(2,1)S(1)}, u32[]{:S(2)}, u32[]{:S(2)}) collective-permute-start(bf16[1,16,4736]{2,1,0:T(8,128)(2,1)S(1)} %pick.12.refs_3_), channel_id=1, source_target_pairs={{0,8},{2,10},{4,12},{6,14},{8,0},{10,2},{12,4},{14,6},{1,9},{3,11}... | collective-permute-start | bytes 454664 | tf_op jit(solution)/shard_map/ppermute | solution.py:74
  33.4 6.9 %collective-permute-start.12 = (bf16[1,16,4096]{2,1,0:T(8,128)(2,1)S(1)}, bf16[1,16,4096]{2,1,0:T(8,128)(2,1)S(1)}, u32[]{:S(2)}, u32[]{:S(2)}) collective-permute-start(bf16[1,16,4096]{2,1,0:T(8,128)(2,1)S(1)} %pick.14.refs_3_), channel_id=1, source_target_pairs={{0,4},{2,6},{4,0},{6,2},{8,12},{10,14},{12,8},{14,10},{1,5},{3,7},... | collective-permute-start | bytes 393224 | tf_op jit(solution)/shard_map/ppermute | solution.py:74
  33.5 7.7 %collective-permute-start.10 = (bf16[1,16,4096]{2,1,0:T(8,128)(2,1)S(1)}, bf16[1,16,4096]{2,1,0:T(8,128)(2,1)S(1)}, u32[]{:S(2)}, u32[]{:S(2)}) collective-permute-start(bf16[1,16,4096]{2,1,0:T(8,128)(2,1)S(1)} %pick.13.refs_3_), channel_id=1, source_target_pairs={{0,8},{2,10},{4,12},{6,14},{8,0},{10,2},{12,4},{14,6},{1,9},{3,11}... | collective-permute-start | bytes 393224 | tf_op jit(solution)/shard_map/ppermute | solution.py:74
  36.6 6.8 %collective-permute-start.1 = (f32[128,384]{1,0:T(8,128)S(1)}, f32[128,384]{1,0:T(8,128)S(1)}, u32[]{:S(2)}, u32[]{:S(2)}) collective-permute-start(f32[128,384]{1,0:T(8,128)S(1)} %pad_maximum_fusion.4.refs_2_.base_own), channel_id=1, source_target_pairs={{0,1},{1,0},{2,3},{3,2},{4,5},{5,4},{6,7},{7,6},{8,9},{9,8},{10,11... | collective-permute-start | bytes 589832 | tf_op jit(solution)/shard_map/ppermute | solution.py:295
  37.2 10.6 %copy-start.3 = (f32[128,128]{1,0:T(8,128)S(1)}, f32[128,128]{1,0:T(8,128)}, u32[]{:S(2)}) copy-start(f32[128,128]{1,0:T(8,128)} %constant.14.clone.cosine) | copy-start | bytes 196612
  37.2 10.6 %copy-start.4 = (f32[128,128]{1,0:T(8,128)S(1)}, f32[128,128]{1,0:T(8,128)}, u32[]{:S(2)}) copy-start(f32[128,128]{1,0:T(8,128)} %constant.15.clone.sine) | copy-start | bytes 196612
  37.2 10.6 %collective-permute-start.16 = (bf16[1,16,4096]{2,1,0:T(8,128)(2,1)S(1)}, bf16[1,16,4096]{2,1,0:T(8,128)(2,1)S(1)}, u32[]{:S(2)}, u32[]{:S(2)}) collective-permute-start(bf16[1,16,4096]{2,1,0:T(8,128)(2,1)S(1)} %pick.15), channel_id=1, source_target_pairs={{0,8},{2,10},{4,12},{6,14},{8,0},{10,2},{12,4},{14,6},{1,9},{3,11}... | collective-permute-start | bytes 393224 | tf_op jit(solution)/shard_map/ppermute | solution.py:74
  42.7 1.4 %collective-permute-start.13 = (f32[128,48]{1,0:T(8,128)S(1)}, f32[128,48]{1,0:T(8,128)S(1)}, u32[]{:S(2)}, u32[]{:S(2)}) collective-permute-start(f32[128,48]{1,0:T(8,128)S(1)} %get-tuple-element.7.shrink_own), channel_id=1, source_target_pairs={{0,1},{1,0},{2,3},{3,2},{4,5},{5,4},{6,7},{7,6},{8,9},{9,8},{10,11... | collective-permute-start | bytes 73736 | tf_op jit(solution)/shard_map/ppermute | solution.py:295
  42.8 1.3 %collective-permute-start.14 = (bf16[16,640]{1,0:T(8,128)(2,1)S(1)}, bf16[16,640]{1,0:T(8,128)(2,1)S(1)}, u32[]{:S(2)}, u32[]{:S(2)}) collective-permute-start(bf16[16,640]{1,0:T(8,128)(2,1)S(1)} %get-tuple-element.8.small_own), channel_id=1, source_target_pairs={{0,1},{1,0},{2,3},{3,2},{4,5},{5,4},{6,7},{7,6},{8,9},{9,8},{10,11... | collective-permute-start | bytes 61448 | tf_op jit(solution)/shard_map/ppermute | solution.py:295

commit v5 on v4

--- a/solution.py
+++ b/solution.py
@@ -115,7 +115,7 @@
     return jnp.concatenate([product(query_weight), product(key_value_weight)], axis=1)
 
 
-def shrink_partial(routes, tokens, small_width):
+def shrink_partial(routes, tokens, small_width, after):
     rows, half = tokens.shape
     rank = routes[0].parts[0].shape[1]
     counts = [len(route.arrays()) for route in routes]
@@ -138,7 +138,7 @@
 
     return pl.pallas_call(
         kernel,
-        in_specs=[SMEM, SMEM] + [VMEM] * (1 + len(arrays)),
+        in_specs=[SMEM, SMEM] + [VMEM] * (1 + len(arrays)) + [ANY] * len(after),
         out_specs=(VMEM, VMEM),
         out_shape=(
             jax.ShapeDtypeStruct((rows, rank * len(routes)), jnp.float32),
@@ -148,7 +148,7 @@
         compiler_params=params(6),
         cost_estimate=cost(2 * rows * half * rank * len(routes), 2 * rows * half),
         name="shrink",
-    )(*routes[0].tables, tokens, *arrays)
+    )(*routes[0].tables, tokens, *arrays, *after)
 
 
 def rotary_tables(rows, width):
@@ -163,16 +163,10 @@
 
 
 def attention_kernel(
-    requests, pool, place, base_own, base_other, shrink_own, shrink_other, small_own, small_other, cosine, sine,
-    weight_own, weight_other, *refs, query_columns, key_columns, route,
+    place, base_own, base_other, shrink_own, shrink_other, small_own, small_other, cosine, sine,
+    weight_own, weight_other, out, low_out, *, query_columns, key_columns,
 ):
-    out, up_map, tiles, sems = refs[-4:]
     tensor, length = place[0], place[1]
-
-    def store(ref, index):
-        up_map[...] = ref[index]
-
-    route.choose((requests, pool), refs[:-4], 0, store)
     rank = small_own.shape[0]
     rows = base_own.shape[0]
     size = HEAD_SIZE
@@ -220,33 +214,60 @@
             attended, small[:, query_columns + key_columns:], (((1,), (1,)), ((), ())),
             preferred_element_type=jnp.float32)
 
-    low = (down(attended_own, small_own) + down(attended_other, small_other)).astype(jnp.bfloat16)
-    valid = lax.broadcasted_iota(jnp.int32, (rows, 1), 0) < length
-    count, _, tile = tiles.shape
-    copies = []
-    for i in range(count):
-        cut = slice(i * tile, (i + 1) * tile)
+    low_out[...] = (down(attended_own, small_own) + down(attended_other, small_other)).astype(jnp.bfloat16)
+    tile = 512
+    for start in range(0, out.shape[1], tile):
+        cut = slice(start, start + tile)
         own = jnp.dot(attended_own, weight_own[:, cut], preferred_element_type=jnp.float32)
         other = jnp.dot(attended_other, weight_other[:, cut], preferred_element_type=jnp.float32)
-        base = own.astype(jnp.bfloat16).astype(jnp.float32) + other.astype(jnp.bfloat16).astype(jnp.float32)
-        delta = jnp.dot(low, up_map[:, cut], preferred_element_type=jnp.float32)
-        tiles[i] = jnp.where(valid, base + delta, 0.0).astype(tiles.dtype)
-        copies.append(pltpu.make_async_copy(tiles.at[i], out.at[:, pl.ds(i * tile, tile)], sems.at[i]))
-        copies[-1].start()
-    for copy in copies:
-        copy.wait()
-
-
-def attention(route, place, base, shrink, small, weight, query_columns, key_columns):
+        out[:, cut] = own.astype(jnp.bfloat16).astype(jnp.float32) + other.astype(jnp.bfloat16).astype(jnp.float32)
+
+
+def attention(place, base, shrink, small, weight, query_columns, key_columns):
     rows = base[0].shape[0]
     columns = weight[0].shape[1]
     cosine, sine = rotary_tables(rows, HEAD_SIZE)
+    operands = (*base, *shrink, *small, cosine, sine, *weight)
+    return pl.pallas_call(
+        functools.partial(attention_kernel, query_columns=query_columns, key_columns=key_columns),
+        in_specs=[SMEM] + [VMEM] * len(operands),
+        out_specs=(VMEM, VMEM),
+        out_shape=(
+            jax.ShapeDtypeStruct((rows, columns), jnp.float32),
+            jax.ShapeDtypeStruct((rows, small[0].shape[0]), jnp.bfloat16),
+        ),
+        compiler_params=params(8),
+        cost_estimate=cost(4 * rows * query_columns * columns, 4 * query_columns * columns),
+        name="attention",
+    )(place, *operands)
+
+
+def finish(route, place, base, low):
+    rows, columns = base.shape
     arrays = route.arrays()
-    operands = (*base, *shrink, *small, cosine, sine, *weight, *arrays)
     tile = 512
+
+    def kernel(requests, pool, place, base_ref, low_ref, *refs):
+        out, up_map, tiles, sems = refs[-4:]
+
+        def store(ref, index):
+            up_map[...] = ref[index]
+
+        route.choose((requests, pool), refs[:-4], 0, store)
+        valid = lax.broadcasted_iota(jnp.int32, (rows, 1), 0) < place[1]
+        copies = []
+        for i in range(columns // tile):
+            cut = slice(i * tile, (i + 1) * tile)
+            delta = jnp.dot(low_ref[...], up_map[:, cut], preferred_element_type=jnp.float32)
+            tiles[i] = jnp.where(valid, base_ref[:, cut] + delta, 0.0).astype(tiles.dtype)
+            copies.append(pltpu.make_async_copy(tiles.at[i], out.at[:, pl.ds(i * tile, tile)], sems.at[i]))
+            copies[-1].start()
+        for copy in copies:
+            copy.wait()
+
     return pl.pallas_call(
-        functools.partial(attention_kernel, query_columns=query_columns, key_columns=key_columns, route=route),
-        in_specs=[SMEM] * 3 + [VMEM] * len(operands),
+        kernel,
+        in_specs=[SMEM] * 3 + [VMEM] * (2 + len(arrays)),
         out_specs=ANY,
         out_shape=jax.ShapeDtypeStruct((rows, columns), arrays[0].dtype),
         scratch_shapes=[
@@ -255,9 +276,9 @@
             pltpu.SemaphoreType.DMA((columns // tile,)),
         ],
         compiler_params=params(8),
-        cost_estimate=cost(4 * rows * query_columns * columns, 4 * query_columns * columns),
-        name="attention",
-    )(*route.tables, place, *operands)
+        cost_estimate=cost(2 * rows * low.shape[1] * columns, 6 * rows * columns),
+        name="finish",
+    )(*route.tables, place, base, low, *arrays)
 
 
 def orders(bits):
@@ -323,10 +344,11 @@
         sent = each.step(last)
         last = (each.arrays()[-1] if sent is None else sent,)
 
-    shrink_own, small_own = shrink_partial(routes, tokens, small_width)
-    return attention(
-        up_route, place, (base_own, base_other), (shrink_own, swap(shrink_own)), (small_own, swap(small_own)),
+    shrink_own, small_own = shrink_partial(routes, tokens, small_width, last)
+    base, low = attention(
+        place, (base_own, base_other), (shrink_own, swap(shrink_own)), (small_own, swap(small_own)),
         (weight_near, weight_far), query_columns, key_columns)
+    return finish(up_route, place, base, low)
 
 
 def solution(mesh):

time: 52 us -> 51.7 us (level)
  the two profiles are of different devices: /device:TPU:0 before, /device:TPU:27 now
where the time goes in v5:
time: 51.7 us; the launch traced here: 51.3 us
  waiting for transfers between devices  17.8 us (34%)
  starting transfers between devices  12.5 us (24%)
  Pallas kernels  11.6 us (22%)
  local copies, waits for them, and re-layouts  4.76 us (9%)
  other arithmetic  2.23 us (4%)
  matrix products  1.45 us (3%)
  between operations  0.92 us (2%)
    ppermute x8, waiting for transfers between devices, step(): self.packets.append(lax.ppermute(out, 'serve', pairs))  12.3 us
    ppermute x5, starting transfers between devices, swap(): return lax.ppermute(x, 'tensor', pair)  5.82 us
    pallas_call x8, Pallas kernels, pick(): pl.pallas_call(kernel, in_specs=[SMEM, SMEM] + [VMEM] * len(arrays) + [AN...  5.61 us
    ppermute x5, waiting for transfers between devices, swap(): return lax.ppermute(x, 'tensor', pair)  4.27 us
    ppermute x8, starting transfers between devices, step(): self.packets.append(lax.ppermute(out, 'serve', pairs))  3.94 us
    dynamic_slice x2, local copies, waits for them, and re-layouts, local(): lax.dynamic_slice_in_dim(weight, tensor * half, half, 1)  3.56 us
    ppermute x4, starting transfers between devices, step(): self.parts += [lax.ppermute(part, 'serve', pairs) for part in self.parts]  2.77 us
    pallas_call x1, Pallas kernels, attention(): pl.pallas_call(functools.partial(attention_kernel, query_columns=query_co...  2.66 us
  transfers between devices with their start and end apart: 17, of which 6 were waited for; matrix products, arithmetic and copies ran while one was open for 16% of the time, Pallas kernels for 19%

profile of v5, /device:TPU:27, one launch (start us, length us, event | category | flops | bytes accessed | tf_op | source)
XLA Modules:
  0.0 51.3 jit_solution(16867469644555802190)
XLA Ops:
  0.0 0.7 %collective-permute-start.7 = (bf16[256,8192]{1,0:T(8,128)(2,1)}, bf16[256,8192]{1,0:T(8,128)(2,1)}, u32[]{:S(2)}, u32[]{:S(2)}) collective-permute-start(bf16[256,8192]{1,0:T(8,128)(2,1)} %param.17), channel_id=1, source_target_pairs={{0,1},{1,0},{2,3},{3,2},{4,5},{5,4},{6,7},{7,6},{8,9},{9,8},{10,11... | collective-permute-start | bytes 12582920 | tf_op jit(solution)/shard_map/ppermute | solution.py:316
  0.8 1.2 %fusion.4 = (bf16[2,16,4096]{2,1,0:T(8,128)(2,1)S(1)}, bf16[2,16,4096]{2,1,0:T(8,128)(2,1)S(1)}, bf16[2,16,4096]{2,1,0:T(8,128)(2,1)S(1)}) fusion(bf16[2,48,4096]{2,1,0:T(8,128)(2,1)} %param.18), kind=kLoop, calls=%fused_computation.12 | loop fusion | bytes 1572864 | tf_op jit(solution)/shard_map/slice | solution.py:325
  1.9 0.8 %pad_maximum_fusion.3.refs_0_ = bf16[2,16,4736]{2,1,0:T(8,128)(2,1)S(1)} fusion(bf16[2,16,256]{2,1,0:T(8,128)(2,1)} %param.21, bf16[2,16,128]{2,1,0:T(8,128)(2,1)} %param.20, bf16[2,16,256]{2,1,0:T(8,128)(2,1)} %param.19, bf16[2,16,4096]{2,1,0:T(8,128)(2,1)S(1)} %get-tuple-element.16), kind=kLoop, calls=%fused_computation.5 | loop fusion | flops 1212416 | bytes 606208 | tf_op jit(solution)/shard_map/concatenate | solution.py:326
  2.7 1.3 %collective-permute-start.2 = (bf16[2,16,4736]{2,1,0:T(8,128)(2,1)S(1)}, bf16[2,16,4736]{2,1,0:T(8,128)(2,1)S(1)}, u32[]{:S(2)}, u32[]{:S(2)}) collective-permute-start(bf16[2,16,4736]{2,1,0:T(8,128)(2,1)S(1)} %pad_maximum_fusion.3.refs_0_), channel_id=1, source_target_pairs={{0,2},{2,0},{4,6},{6,4},{8,10},{10,8},{12,14},{14,12},{1,3},{3,1},... | collective-permute-start | bytes 909320 | tf_op jit(solution)/shard_map/ppermute | solution.py:70
  4.2 1.8 %constant_dynamic-slice_fusion.1.refs_3_.weight_own = bf16[256,4096]{1,0:T(8,128)(2,1)S(1)} fusion(bf16[256,8192]{1,0:T(8,128)(2,1)} %param.17, s32[]{:T(128)S(6)} %select_n.19), kind=kLoop, calls=%fused_computation.9 | loop fusion | bytes 4194308 | tf_op jit(solution)/shard_map/dynamic_slice | solution.py:338
  6.1 3.2 %collective-permute-done = bf16[128,4096]{1,0:T(8,128)(2,1)} collective-permute-done((bf16[128,4096]{1,0:T(8,128)(2,1)}, bf16[128,4096]{1,0:T(8,128)(2,1)}, u32[]{:S(2)}, u32[]{:S(2)}) %collective-permute-start) | collective-permute-done | bytes 1048608 | tf_op jit(solution)/shard_map/ppermute | solution.py:316
  9.3 1.2 %collective-permute-start.4 = (bf16[2,16,4096]{2,1,0:T(8,128)(2,1)S(1)}, bf16[2,16,4096]{2,1,0:T(8,128)(2,1)S(1)}, u32[]{:S(2)}, u32[]{:S(2)}) collective-permute-start(bf16[2,16,4096]{2,1,0:T(8,128)(2,1)S(1)} %copy-done.2), channel_id=1, source_target_pairs={{0,2},{2,0},{4,6},{6,4},{8,10},{10,8},{12,14},{14,12},{1,3},{3,1},... | collective-permute-start | bytes 786440 | tf_op jit(solution)/shard_map/ppermute | solution.py:70
  10.6 1.4 %broadcast_select_fusion.1 = (bf16[128,4096]{1,0:T(8,128)(2,1)S(1)}, bf16[128,4096]{1,0:T(8,128)(2,1)S(1)}) fusion(bf16[128,4096]{1,0:T(8,128)(2,1)S(1)} %copy-done.1, bf16[128,4096]{1,0:T(8,128)(2,1)} %collective-permute-done, pred[]{:T(512)S(6)} %eq.3), kind=kLoop, calls=%fused_computation.4 | loop fusion | flops 1048576 | bytes 4194305 | tf_op jit(solution)/shard_map/jit(_where)/select_n | solution.py:107
  11.9 0.7 %fusion.1 = f32[128,256]{1,0:T(8,128)S(1)} fusion(bf16[8192,256]{1,0:T(8,128)(2,1)S(1)} %copy-done.7, bf16[128,4096]{1,0:T(8,128)(2,1)S(1)} %get-tuple-element.14, bf16[128,4096]{1,0:T(8,128)(2,1)S(1)} %get-tuple-element.13), kind=kOutput, calls=%fused_computation.2 | convolution fusion | flops 541065216 | bytes 6422528 | tf_op jit(solution)/shard_map/dot_general | solution.py:113
  12.7 0.7 %fusion = f32[128,128]{1,0:T(8,128)S(1)} fusion(bf16[8192,128]{1,0:T(8,128)(2,1)S(1)} %copy-done, bf16[128,4096]{1,0:T(8,128)(2,1)S(1)} %get-tuple-element.14, bf16[128,4096]{1,0:T(8,128)(2,1)S(1)} %get-tuple-element.13), kind=kOutput, calls=%fused_computation.1 | convolution fusion | flops 272629760 | bytes 4259840 | tf_op jit(solution)/shard_map/dot_general | solution.py:113
  13.5 0.6 %pick.8.refs_2_ = bf16[2,16,4736]{2,1,0:T(8,128)(2,1)S(1)} custom-call(s32[8]{0:T(128)S(1)} %copy-done.5, s32[16]{0:T(128)S(1)} %copy-done.6, bf16[2,16,4736]{2,1,0:T(8,128)(2,1)S(1)} %pad_maximum_fusion.3.refs_0_, bf16[2,16,4736]{2,1,0:T(8,128)(2,1)S(1)} %collective-permute-done.2.refs_1_, f32[128,384]{1,0:T(8,128)S(1)} %pad_maximum_fusion.4.refs_2_.base_own), custom_call_target="tpu_custom_call" | custom-call | bytes 606208 | tf_op jit(solution)/shard_map/pick/pallas_call | solution.py:93
  14.3 1.3 %collective-permute-done.6.refs_1_.refs_5_ = bf16[2,16,4096]{2,1,0:T(8,128)(2,1)S(1)} collective-permute-done((bf16[2,16,4096]{2,1,0:T(8,128)(2,1)S(1)}, bf16[2,16,4096]{2,1,0:T(8,128)(2,1)S(1)}, u32[]{:S(2)}, u32[]{:S(2)}) %collective-permute-start.6) | collective-permute-done | bytes 262176 | tf_op jit(solution)/shard_map/ppermute | solution.py:70
  15.6 0.6 %pick.9.refs_2_ = bf16[2,16,4096]{2,1,0:T(8,128)(2,1)S(1)} custom-call(s32[8]{0:T(128)S(1)} %copy-done.5, s32[16]{0:T(128)S(1)} %copy-done.6, bf16[2,16,4096]{2,1,0:T(8,128)(2,1)S(1)} %get-tuple-element.15.refs_0_.refs_4_, bf16[2,16,4096]{2,1,0:T(8,128)(2,1)S(1)} %collective-permute-done.6.refs_1_.refs_5_, bf16[2,16,4736]{2,1,0:T(8,128)(2,1)S(1)} %pick.8.refs_2_), custom_call_target="tpu_custom_call" | custom-call | bytes 524288 | tf_op jit(solution)/shard_map/pick/pallas_call | solution.py:93
  16.5 1.0 %pick.10.refs_2_ = bf16[2,16,4096]{2,1,0:T(8,128)(2,1)S(1)} custom-call(s32[8]{0:T(128)S(1)} %copy-done.5, s32[16]{0:T(128)S(1)} %copy-done.6, bf16[2,16,4096]{2,1,0:T(8,128)(2,1)S(1)} %get-tuple-element.17.refs_0_.refs_8_, bf16[2,16,4096]{2,1,0:T(8,128)(2,1)} %collective-permute-done.5.refs_1_.refs_9_, bf16[2,16,4096]{2,1,0:T(8,128)(2,1)S(1)} %pick.9.refs_2_), custom_call_target="tpu_custom_call" | custom-call | bytes 524288 | tf_op jit(solution)/shard_map/pick/pallas_call | solution.py:93
  17.5 1.3 %collective-permute-start.11 = (bf16[2,16,4096]{2,1,0:T(8,128)(2,1)S(1)}, bf16[2,16,4096]{2,1,0:T(8,128)(2,1)S(1)}, u32[]{:S(2)}, u32[]{:S(2)}) collective-permute-start(bf16[2,16,4096]{2,1,0:T(8,128)(2,1)S(1)} %pick.10.refs_2_), channel_id=1, source_target_pairs={{0,2},{2,0},{4,6},{6,4},{8,10},{10,8},{12,14},{14,12},{1,3},{3,1},... | collective-permute-start | bytes 786440 | tf_op jit(solution)/shard_map/ppermute | solution.py:74
  18.8 1.7 %constant_dynamic-slice_fusion.refs_4_.weight_other = bf16[256,4096]{1,0:T(8,128)(2,1)S(1)} fusion(bf16[256,8192]{1,0:T(8,128)(2,1)} %collective-permute-done.7, s32[]{:T(128)S(6)} %select_n.19), kind=kLoop, calls=%fused_computation.8 | loop fusion | bytes 4194308 | tf_op jit(solution)/shard_map/dynamic_slice | solution.py:338
  20.6 0.6 %pick.11.refs_3_ = bf16[2,16,4096]{2,1,0:T(8,128)(2,1)S(1)} custom-call(s32[8]{0:T(128)S(1)} %copy-done.5, s32[16]{0:T(128)S(1)} %copy-done.6, bf16[2,16,4096]{2,1,0:T(8,128)(2,1)S(1)} %copy-done.2, bf16[2,16,4096]{2,1,0:T(8,128)(2,1)S(1)} %collective-permute-done.4.refs_1_, bf16[2,16,4096]{2,1,0:T(8,128)(2,1)S(1)} %pick.10.refs_2_, ...), custom_call_target="tpu_custom_call" | custom-call | bytes 524288 | tf_op jit(solution)/shard_map/pick/pallas_call | solution.py:93
  21.3 2.7 %collective-permute-done.3.refs_2_ = bf16[2,16,4736]{2,1,0:T(8,128)(2,1)S(1)} collective-permute-done((bf16[2,16,4736]{2,1,0:T(8,128)(2,1)S(1)}, bf16[2,16,4736]{2,1,0:T(8,128)(2,1)S(1)}, u32[]{:S(2)}, u32[]{:S(2)}) %collective-permute-start.3) | collective-permute-done | bytes 303136 | tf_op jit(solution)/shard_map/ppermute | solution.py:74
  24.0 0.6 %pick.12.refs_3_ = bf16[1,16,4736]{2,1,0:T(8,128)(2,1)S(1)} custom-call(s32[8]{0:T(128)S(1)} %copy-done.5, s32[16]{0:T(128)S(1)} %copy-done.6, bf16[2,16,4736]{2,1,0:T(8,128)(2,1)S(1)} %pad_maximum_fusion.3.refs_0_, bf16[2,16,4736]{2,1,0:T(8,128)(2,1)S(1)} %collective-permute-done.2.refs_1_, bf16[2,16,4736]{2,1,0:T(8,128)(2,1)S(1)} %collective-permute-done.3.refs_2_, ...), custom_call_target="tpu_custom_call" | custom-call | bytes 303104 | tf_op jit(solution)/shard_map/pick/pallas_call | solution.py:93
  24.7 0.6 %pick.13.refs_3_ = bf16[1,16,4096]{2,1,0:T(8,128)(2,1)S(1)} custom-call(s32[8]{0:T(128)S(1)} %copy-done.5, s32[16]{0:T(128)S(1)} %copy-done.6, bf16[2,16,4096]{2,1,0:T(8,128)(2,1)S(1)} %get-tuple-element.15.refs_0_.refs_4_, bf16[2,16,4096]{2,1,0:T(8,128)(2,1)S(1)} %collective-permute-done.6.refs_1_.refs_5_, ...), custom_call_target="tpu_custom_call" | custom-call | bytes 262144 | tf_op jit(solution)/shard_map/pick/pallas_call | solution.py:93
  25.3 2.9 %collective-permute-done.11.refs_2_.refs_10_ = bf16[2,16,4096]{2,1,0:T(8,128)(2,1)S(1)} collective-permute-done((bf16[2,16,4096]{2,1,0:T(8,128)(2,1)S(1)}, bf16[2,16,4096]{2,1,0:T(8,128)(2,1)S(1)}, u32[]{:S(2)}, u32[]{:S(2)}) %collective-permute-start.11) | collective-permute-done | bytes 262176 | tf_op jit(solution)/shard_map/ppermute | solution.py:74
  28.2 1.0 %pick.14.refs_3_ = bf16[1,16,4096]{2,1,0:T(8,128)(2,1)S(1)} custom-call(s32[8]{0:T(128)S(1)} %copy-done.5, s32[16]{0:T(128)S(1)} %copy-done.6, bf16[2,16,4096]{2,1,0:T(8,128)(2,1)S(1)} %get-tuple-element.17.refs_0_.refs_8_, bf16[2,16,4096]{2,1,0:T(8,128)(2,1)} %collective-permute-done.5.refs_1_.refs_9_, ...), custom_call_target="tpu_custom_call" | custom-call | bytes 262144 | tf_op jit(solution)/shard_map/pick/pallas_call | solution.py:93
  29.2 0.7 %collective-permute-start.12 = (bf16[1,16,4096]{2,1,0:T(8,128)(2,1)S(1)}, bf16[1,16,4096]{2,1,0:T(8,128)(2,1)S(1)}, u32[]{:S(2)}, u32[]{:S(2)}) collective-permute-start(bf16[1,16,4096]{2,1,0:T(8,128)(2,1)S(1)} %pick.14.refs_3_), channel_id=1, source_target_pairs={{0,4},{2,6},{4,0},{6,2},{8,12},{10,14},{12,8},{14,10},{1,5},{3,7},... | collective-permute-start | bytes 393224 | tf_op jit(solution)/shard_map/ppermute | solution.py:74
  29.9 3.6 %collective-permute-start.1 = (f32[128,384]{1,0:T(8,128)S(1)}, f32[128,384]{1,0:T(8,128)S(1)}, u32[]{:S(2)}, u32[]{:S(2)}) collective-permute-start(f32[128,384]{1,0:T(8,128)S(1)} %pad_maximum_fusion.4.refs_2_.base_own), channel_id=1, source_target_pairs={{0,1},{1,0},{2,3},{3,2},{4,5},{5,4},{6,7},{7,6},{8,9},{9,8},{10,11... | collective-permute-start | bytes 589832 | tf_op jit(solution)/shard_map/ppermute | solution.py:316
  34.1 0.6 %pick.15.refs_12_ = bf16[1,16,4096]{2,1,0:T(8,128)(2,1)S(1)} custom-call(s32[8]{0:T(128)S(1)} %copy-done.5, s32[16]{0:T(128)S(1)} %copy-done.6, bf16[2,16,4096]{2,1,0:T(8,128)(2,1)S(1)} %copy-done.2, bf16[2,16,4096]{2,1,0:T(8,128)(2,1)S(1)} %collective-permute-done.4.refs_1_, bf16[2,16,4096]{2,1,0:T(8,128)(2,1)S(1)} %collective-permute-done.13.refs_2_, ...), custom_call_target="tpu_custom_call" | custom-call | bytes 262144 | tf_op jit(solution)/shard_map/pick/pallas_call | solution.py:93
  34.8 1.3 %collective-permute-start.16 = (bf16[1,16,4096]{2,1,0:T(8,128)(2,1)S(1)}, bf16[1,16,4096]{2,1,0:T(8,128)(2,1)S(1)}, u32[]{:S(2)}, u32[]{:S(2)}) collective-permute-start(bf16[1,16,4096]{2,1,0:T(8,128)(2,1)S(1)} %pick.15.refs_12_), channel_id=1, source_target_pairs={{0,8},{2,10},{4,12},{6,14},{8,0},{10,2},{12,4},{14,6},{1,9},{3,11}... | collective-permute-start | bytes 393224 | tf_op jit(solution)/shard_map/ppermute | solution.py:74
  36.0 6.7 %collective-permute-done.10.refs_7_ = bf16[1,16,4096]{2,1,0:T(8,128)(2,1)S(1)} collective-permute-done((bf16[1,16,4096]{2,1,0:T(8,128)(2,1)S(1)}, bf16[1,16,4096]{2,1,0:T(8,128)(2,1)S(1)}, u32[]{:S(2)}, u32[]{:S(2)}) %collective-permute-start.10) | collective-permute-done | bytes 131104 | tf_op jit(solution)/shard_map/ppermute | solution.py:74
  42.7 1.5 %shrink.1 = (f32[128,48]{1,0:T(8,128)S(1)}, bf16[16,640]{1,0:T(8,128)(2,1)S(1)}) custom-call(s32[8]{0:T(128)S(1)} %copy-done.5, s32[16]{0:T(128)S(1)} %copy-done.6, bf16[128,4096]{1,0:T(8,128)(2,1)S(1)} %copy-done.1, bf16[2,16,4736]{2,1,0:T(8,128)(2,1)S(1)} %pad_maximum_fusion.3.refs_0_, bf16[2,16,4736]{2,1,0:T(8,128)(2,1)S(1)} %collective-permute-done.2.refs_1_, ...), custom_call_target="tpu_custom_call" | custom-call | flops 50331648 | bytes 1048576 | tf_op jit(solution)/shard_map/shrink/pallas_call | solution.py:139
  44.2 1.4 %collective-permute-start.14 = (f32[128,48]{1,0:T(8,128)S(1)}, f32[128,48]{1,0:T(8,128)S(1)}, u32[]{:S(2)}, u32[]{:S(2)}) collective-permute-start(f32[128,48]{1,0:T(8,128)S(1)} %get-tuple-element.9.shrink_own), channel_id=1, source_target_pairs={{0,1},{1,0},{2,3},{3,2},{4,5},{5,4},{6,7},{7,6},{8,9},{9,8},{10,11... | collective-permute-start | bytes 73736 | tf_op jit(solution)/shard_map/ppermute | solution.py:316
  45.8 1.0 %collective-permute-done.15.small_other = bf16[16,640]{1,0:T(8,128)(2,1)S(1)} collective-permute-done((bf16[16,640]{1,0:T(8,128)(2,1)S(1)}, bf16[16,640]{1,0:T(8,128)(2,1)S(1)}, u32[]{:S(2)}, u32[]{:S(2)}) %collective-permute-start.15) | collective-permute-done | bytes 20512 | tf_op jit(solution)/shard_map/ppermute | solution.py:316
  46.8 2.7 %attention.1 = (f32[128,4096]{1,0:T(8,128)S(1)}, bf16[128,16]{1,0:T(8,128)(2,1)S(1)}) custom-call(s32[2]{0:T(128)S(1)} %pad_add_fusion.place, f32[128,384]{1,0:T(8,128)S(1)} %pad_maximum_fusion.4.refs_2_.base_own, f32[128,384]{1,0:T(8,128)S(1)} %collective-permute-done.1.base_other, f32[128,48]{1,0:T(8,128)S(1)} %get-tuple-element.9.shrink_own, ...), custom_call_target="tpu_custom_call" | custom-call | flops 536870912 | bytes 4194304 | tf_op jit(solution)/shard_map/attention/pallas_call | solution.py:231
  49.5 1.8 %finish.1 = bf16[128,4096]{1,0:T(8,128)(2,1)} custom-call(s32[8]{0:T(128)S(1)} %copy-done.5, s32[16]{0:T(128)S(1)} %copy-done.6, s32[2]{0:T(128)S(1)} %pad_add_fusion.place, f32[128,4096]{1,0:T(8,128)S(1)} %get-tuple-element.11.base_ref, bf16[128,16]{1,0:T(8,128)(2,1)S(1)} %get-tuple-element.12.low_ref, bf16[2,16,4096]{2,1,0:T(8,128)(2,1)S(1)} %copy-done.2, ...), custom_call_target="tpu_custom_call" | custom-call | flops 16777216 | bytes 3145728 | tf_op jit(solution)/shard_map/finish/pallas_call | solution.py:268
  (38 shorter events, 1.2 us)
Async XLA Ops:
  0.0 12.7 %copy-start = (bf16[8192,128]{1,0:T(8,128)(2,1)S(1)}, bf16[8192,128]{1,0:T(8,128)(2,1)}, u32[]{:S(2)}) copy-start(bf16[8192,128]{1,0:T(8,128)(2,1)} %param.16) | copy-start | bytes 6291460
  0.0 18.8 %collective-permute-start.7 = (bf16[256,8192]{1,0:T(8,128)(2,1)}, bf16[256,8192]{1,0:T(8,128)(2,1)}, u32[]{:S(2)}, u32[]{:S(2)}) collective-permute-start(bf16[256,8192]{1,0:T(8,128)(2,1)} %param.17), channel_id=1, source_target_pairs={{0,1},{1,0},{2,3},{3,2},{4,5},{5,4},{6,7},{7,6},{8,9},{9,8},{10,11... | collective-permute-start | bytes 12582920 | tf_op jit(solution)/shard_map/ppermute | solution.py:316
  0.7 8.6 %collective-permute-start = (bf16[128,4096]{1,0:T(8,128)(2,1)}, bf16[128,4096]{1,0:T(8,128)(2,1)}, u32[]{:S(2)}, u32[]{:S(2)}) collective-permute-start(bf16[128,4096]{1,0:T(8,128)(2,1)} %rows_ref.1), channel_id=1, source_target_pairs={{0,1},{1,0},{2,3},{3,2},{4,5},{5,4},{6,7},{7,6},{8,9},{9,8},{10,11... | collective-permute-start | bytes 3145736 | tf_op jit(solution)/shard_map/ppermute | solution.py:316
  2.7 10.8 %collective-permute-start.2 = (bf16[2,16,4736]{2,1,0:T(8,128)(2,1)S(1)}, bf16[2,16,4736]{2,1,0:T(8,128)(2,1)S(1)}, u32[]{:S(2)}, u32[]{:S(2)}) collective-permute-start(bf16[2,16,4736]{2,1,0:T(8,128)(2,1)S(1)} %pad_maximum_fusion.3.refs_0_), channel_id=1, source_target_pairs={{0,2},{2,0},{4,6},{6,4},{8,10},{10,8},{12,14},{14,12},{1,3},{3,1},... | collective-permute-start | bytes 909320 | tf_op jit(solution)/shard_map/ppermute | solution.py:70
  4.0 11.6 %collective-permute-start.6 = (bf16[2,16,4096]{2,1,0:T(8,128)(2,1)S(1)}, bf16[2,16,4096]{2,1,0:T(8,128)(2,1)S(1)}, u32[]{:S(2)}, u32[]{:S(2)}) collective-permute-start(bf16[2,16,4096]{2,1,0:T(8,128)(2,1)S(1)} %get-tuple-element.15.refs_0_.refs_4_), channel_id=1, source_target_pairs={{0,4},{2,6},{4,0},{6,2},{8,12},{10,14},{12,8},{14,10},{1,5},{3,7},... | collective-permute-start | bytes 786440 | tf_op jit(solution)/shard_map/ppermute | solution.py:70
  4.2 12.3 %collective-permute-start.5 = (bf16[2,16,4096]{2,1,0:T(8,128)(2,1)S(1)}, bf16[2,16,4096]{2,1,0:T(8,128)(2,1)}, u32[]{:S(2)}, u32[]{:S(2)}) collective-permute-start(bf16[2,16,4096]{2,1,0:T(8,128)(2,1)S(1)} %get-tuple-element.17.refs_0_.refs_8_), channel_id=1, source_target_pairs={{0,8},{2,10},{4,12},{6,14},{8,0},{10,2},{12,4},{14,6},{1,9},{3,11}... | collective-permute-start | bytes 786440 | tf_op jit(solution)/shard_map/ppermute | solution.py:70
  4.2 5.1 %copy-start.2 = (bf16[2,16,4096]{2,1,0:T(8,128)(2,1)S(1)}, bf16[2,16,4096]{2,1,0:T(8,128)(2,1)}, u32[]{:S(2)}) copy-start(bf16[2,16,4096]{2,1,0:T(8,128)(2,1)} %refs_0_.5) | copy-start | bytes 786436
  4.2 6.3 %copy-start.1 = (bf16[128,4096]{1,0:T(8,128)(2,1)S(1)}, bf16[128,4096]{1,0:T(8,128)(2,1)}, u32[]{:S(2)}) copy-start(bf16[128,4096]{1,0:T(8,128)(2,1)} %rows_ref.1) | copy-start | bytes 3145732
  6.1 5.9 %copy-start.7 = (bf16[8192,256]{1,0:T(8,128)(2,1)S(1)}, bf16[8192,256]{1,0:T(8,128)(2,1)}, u32[]{:S(2)}) copy-start(bf16[8192,256]{1,0:T(8,128)(2,1)} %param.15) | copy-start | bytes 12582916
  9.3 11.3 %collective-permute-start.4 = (bf16[2,16,4096]{2,1,0:T(8,128)(2,1)S(1)}, bf16[2,16,4096]{2,1,0:T(8,128)(2,1)S(1)}, u32[]{:S(2)}, u32[]{:S(2)}) collective-permute-start(bf16[2,16,4096]{2,1,0:T(8,128)(2,1)S(1)} %copy-done.2), channel_id=1, source_target_pairs={{0,2},{2,0},{4,6},{6,4},{8,10},{10,8},{12,14},{14,12},{1,3},{3,1},... | collective-permute-start | bytes 786440 | tf_op jit(solution)/shard_map/ppermute | solution.py:70
  12.7 0.8 %copy-start.5 = (s32[8]{0:T(128)S(1)}, s32[8]{0:T(128)}, u32[]{:S(2)}) copy-start(s32[8]{0:T(128)} %requests.19) | copy-start | bytes 100
  12.7 0.8 %copy-start.6 = (s32[16]{0:T(128)S(1)}, s32[16]{0:T(128)}, u32[]{:S(2)}) copy-start(s32[16]{0:T(128)} %pool.19) | copy-start | bytes 196
  14.1 9.9 %collective-permute-start.3 = (bf16[2,16,4736]{2,1,0:T(8,128)(2,1)S(1)}, bf16[2,16,4736]{2,1,0:T(8,128)(2,1)S(1)}, u32[]{:S(2)}, u32[]{:S(2)}) collective-permute-start(bf16[2,16,4736]{2,1,0:T(8,128)(2,1)S(1)} %pick.8.refs_2_), channel_id=1, source_target_pairs={{0,4},{2,6},{4,0},{6,2},{8,12},{10,14},{12,8},{14,10},{1,5},{3,7},... | collective-permute-start | bytes 909320 | tf_op jit(solution)/shard_map/ppermute | solution.py:74
  16.2 8.5 %collective-permute-start.9 = (bf16[2,16,4096]{2,1,0:T(8,128)(2,1)S(1)}, bf16[2,16,4096]{2,1,0:T(8,128)(2,1)S(1)}, u32[]{:S(2)}, u32[]{:S(2)}) collective-permute-start(bf16[2,16,4096]{2,1,0:T(8,128)(2,1)S(1)} %pick.9.refs_2_), channel_id=1, source_target_pairs={{0,2},{2,0},{4,6},{6,4},{8,10},{10,8},{12,14},{14,12},{1,3},{3,1},... | collective-permute-start | bytes 786440 | tf_op jit(solution)/shard_map/ppermute | solution.py:74
  17.5 10.7 %collective-permute-start.11 = (bf16[2,16,4096]{2,1,0:T(8,128)(2,1)S(1)}, bf16[2,16,4096]{2,1,0:T(8,128)(2,1)S(1)}, u32[]{:S(2)}, u32[]{:S(2)}) collective-permute-start(bf16[2,16,4096]{2,1,0:T(8,128)(2,1)S(1)} %pick.10.refs_2_), channel_id=1, source_target_pairs={{0,2},{2,0},{4,6},{6,4},{8,10},{10,8},{12,14},{14,12},{1,3},{3,1},... | collective-permute-start | bytes 786440 | tf_op jit(solution)/shard_map/ppermute | solution.py:74
  21.2 12.9 %collective-permute-start.13 = (bf16[2,16,4096]{2,1,0:T(8,128)(2,1)S(1)}, bf16[2,16,4096]{2,1,0:T(8,128)(2,1)S(1)}, u32[]{:S(2)}, u32[]{:S(2)}) collective-permute-start(bf16[2,16,4096]{2,1,0:T(8,128)(2,1)S(1)} %pick.11.refs_3_), channel_id=1, source_target_pairs={{0,4},{2,6},{4,0},{6,2},{8,12},{10,14},{12,8},{14,10},{1,5},{3,7},... | collective-permute-start | bytes 786440 | tf_op jit(solution)/shard_map/ppermute | solution.py:74
  24.6 18.1 %collective-permute-start.8 = (bf16[1,16,4736]{2,1,0:T(8,128)(2,1)S(1)}, bf16[1,16,4736]{2,1,0:T(8,128)(2,1)S(1)}, u32[]{:S(2)}, u32[]{:S(2)}) collective-permute-start(bf16[1,16,4736]{2,1,0:T(8,128)(2,1)S(1)} %pick.12.refs_3_), channel_id=1, source_target_pairs={{0,8},{2,10},{4,12},{6,14},{8,0},{10,2},{12,4},{14,6},{1,9},{3,11}... | collective-permute-start | bytes 454664 | tf_op jit(solution)/shard_map/ppermute | solution.py:74
  29.2 6.8 %collective-permute-start.12 = (bf16[1,16,4096]{2,1,0:T(8,128)(2,1)S(1)}, bf16[1,16,4096]{2,1,0:T(8,128)(2,1)S(1)}, u32[]{:S(2)}, u32[]{:S(2)}) collective-permute-start(bf16[1,16,4096]{2,1,0:T(8,128)(2,1)S(1)} %pick.14.refs_3_), channel_id=1, source_target_pairs={{0,4},{2,6},{4,0},{6,2},{8,12},{10,14},{12,8},{14,10},{1,5},{3,7},... | collective-permute-start | bytes 393224 | tf_op jit(solution)/shard_map/ppermute | solution.py:74
  29.9 12.8 %collective-permute-start.10 = (bf16[1,16,4096]{2,1,0:T(8,128)(2,1)S(1)}, bf16[1,16,4096]{2,1,0:T(8,128)(2,1)S(1)}, u32[]{:S(2)}, u32[]{:S(2)}) collective-permute-start(bf16[1,16,4096]{2,1,0:T(8,128)(2,1)S(1)} %pick.13.refs_3_), channel_id=1, source_target_pairs={{0,8},{2,10},{4,12},{6,14},{8,0},{10,2},{12,4},{14,6},{1,9},{3,11}... | collective-permute-start | bytes 393224 | tf_op jit(solution)/shard_map/ppermute | solution.py:74
  29.9 15.9 %collective-permute-start.1 = (f32[128,384]{1,0:T(8,128)S(1)}, f32[128,384]{1,0:T(8,128)S(1)}, u32[]{:S(2)}, u32[]{:S(2)}) collective-permute-start(f32[128,384]{1,0:T(8,128)S(1)} %pad_maximum_fusion.4.refs_2_.base_own), channel_id=1, source_target_pairs={{0,1},{1,0},{2,3},{3,2},{4,5},{5,4},{6,7},{7,6},{8,9},{9,8},{10,11... | collective-permute-start | bytes 589832 | tf_op jit(solution)/shard_map/ppermute | solution.py:316
  34.7 12.1 %copy-start.3 = (f32[128,128]{1,0:T(8,128)S(1)}, f32[128,128]{1,0:T(8,128)}, u32[]{:S(2)}) copy-start(f32[128,128]{1,0:T(8,128)} %constant.14.clone.cosine) | copy-start | bytes 196612
  34.7 12.1 %copy-start.4 = (f32[128,128]{1,0:T(8,128)S(1)}, f32[128,128]{1,0:T(8,128)}, u32[]{:S(2)}) copy-start(f32[128,128]{1,0:T(8,128)} %constant.15.clone.sine) | copy-start | bytes 196612
  34.8 14.7 %collective-permute-start.16 = (bf16[1,16,4096]{2,1,0:T(8,128)(2,1)S(1)}, bf16[1,16,4096]{2,1,0:T(8,128)(2,1)S(1)}, u32[]{:S(2)}, u32[]{:S(2)}) collective-permute-start(bf16[1,16,4096]{2,1,0:T(8,128)(2,1)S(1)} %pick.15.refs_12_), channel_id=1, source_target_pairs={{0,8},{2,10},{4,12},{6,14},{8,0},{10,2},{12,4},{14,6},{1,9},{3,11}... | collective-permute-start | bytes 393224 | tf_op jit(solution)/shard_map/ppermute | solution.py:74
  44.2 2.6 %collective-permute-start.14 = (f32[128,48]{1,0:T(8,128)S(1)}, f32[128,48]{1,0:T(8,128)S(1)}, u32[]{:S(2)}, u32[]{:S(2)}) collective-permute-start(f32[128,48]{1,0:T(8,128)S(1)} %get-tuple-element.9.shrink_own), channel_id=1, source_target_pairs={{0,1},{1,0},{2,3},{3,2},{4,5},{5,4},{6,7},{7,6},{8,9},{9,8},{10,11... | collective-permute-start | bytes 73736 | tf_op jit(solution)/shard_map/ppermute | solution.py:316
  45.6 1.2 %collective-permute-start.15 = (bf16[16,640]{1,0:T(8,128)(2,1)S(1)}, bf16[16,640]{1,0:T(8,128)(2,1)S(1)}, u32[]{:S(2)}, u32[]{:S(2)}) collective-permute-start(bf16[16,640]{1,0:T(8,128)(2,1)S(1)} %get-tuple-element.10.small_own), channel_id=1, source_target_pairs={{0,1},{1,0},{2,3},{3,2},{4,5},{5,4},{6,7},{7,6},{8,9},{9,8},{10,11... | collective-permute-start | bytes 61448 | tf_op jit(solution)/shard_map/ppermute | solution.py:316

commit v6 on v5

--- a/solution.py
+++ b/solution.py
@@ -215,7 +215,7 @@
             preferred_element_type=jnp.float32)
 
     low_out[...] = (down(attended_own, small_own) + down(attended_other, small_other)).astype(jnp.bfloat16)
-    tile = 512
+    tile = 1024
     for start in range(0, out.shape[1], tile):
         cut = slice(start, start + tile)
         own = jnp.dot(attended_own, weight_own[:, cut], preferred_element_type=jnp.float32)
@@ -245,7 +245,7 @@
 def finish(route, place, base, low):
     rows, columns = base.shape
     arrays = route.arrays()
-    tile = 512
+    tile = 1024
 
     def kernel(requests, pool, place, base_ref, low_ref, *refs):
         out, up_map, tiles, sems = refs[-4:]

time: 51.7 us -> 51.7 us (level)
  the two profiles are of different devices: /device:TPU:27 before, /device:TPU:25 now
where the time goes in v6:
time: 51.7 us; the launch traced here: 51.3 us
  waiting for transfers between devices  17.9 us (35%)
  starting transfers between devices  12.5 us (24%)
  Pallas kernels  11.6 us (22%)
  local copies, waits for them, and re-layouts  4.76 us (9%)
  other arithmetic  2.23 us (4%)
  matrix products  1.45 us (3%)
  between operations  0.92 us (2%)
    ppermute x8, waiting for transfers between devices, step(): self.packets.append(lax.ppermute(out, 'serve', pairs))  12.3 us
    ppermute x5, starting transfers between devices, swap(): return lax.ppermute(x, 'tensor', pair)  5.81 us
    pallas_call x8, Pallas kernels, pick(): pl.pallas_call(kernel, in_specs=[SMEM, SMEM] + [VMEM] * len(arrays) + [AN...  5.59 us
    ppermute x5, waiting for transfers between devices, swap(): return lax.ppermute(x, 'tensor', pair)  4.27 us
    ppermute x8, starting transfers between devices, step(): self.packets.append(lax.ppermute(out, 'serve', pairs))  3.91 us
    dynamic_slice x2, local copies, waits for them, and re-layouts, local(): lax.dynamic_slice_in_dim(weight, tensor * half, half, 1)  3.56 us
    ppermute x4, starting transfers between devices, step(): self.parts += [lax.ppermute(part, 'serve', pairs) for part in self.parts]  2.77 us
    pallas_call x1, Pallas kernels, attention(): pl.pallas_call(functools.partial(attention_kernel, query_columns=query_co...  2.65 us
  transfers between devices with their start and end apart: 17, of which 6 were waited for; matrix products, arithmetic and copies ran while one was open for 16% of the time, Pallas kernels for 19%

profile of v6, /device:TPU:25, one launch (start us, length us, event | category | flops | bytes accessed | tf_op | source)
XLA Modules:
  0.0 51.3 jit_solution(11281353546095525890)
XLA Ops:
  0.0 0.7 %collective-permute-start.7 = (bf16[256,8192]{1,0:T(8,128)(2,1)}, bf16[256,8192]{1,0:T(8,128)(2,1)}, u32[]{:S(2)}, u32[]{:S(2)}) collective-permute-start(bf16[256,8192]{1,0:T(8,128)(2,1)} %param.17), channel_id=1, source_target_pairs={{0,1},{1,0},{2,3},{3,2},{4,5},{5,4},{6,7},{7,6},{8,9},{9,8},{10,11... | collective-permute-start | bytes 12582920 | tf_op jit(solution)/shard_map/ppermute | solution.py:316
  0.8 1.2 %fusion.4 = (bf16[2,16,4096]{2,1,0:T(8,128)(2,1)S(1)}, bf16[2,16,4096]{2,1,0:T(8,128)(2,1)S(1)}, bf16[2,16,4096]{2,1,0:T(8,128)(2,1)S(1)}) fusion(bf16[2,48,4096]{2,1,0:T(8,128)(2,1)} %param.18), kind=kLoop, calls=%fused_computation.12 | loop fusion | bytes 1572864 | tf_op jit(solution)/shard_map/slice | solution.py:325
  1.9 0.8 %pad_maximum_fusion.3.refs_0_ = bf16[2,16,4736]{2,1,0:T(8,128)(2,1)S(1)} fusion(bf16[2,16,256]{2,1,0:T(8,128)(2,1)} %param.21, bf16[2,16,128]{2,1,0:T(8,128)(2,1)} %param.20, bf16[2,16,256]{2,1,0:T(8,128)(2,1)} %param.19, bf16[2,16,4096]{2,1,0:T(8,128)(2,1)S(1)} %get-tuple-element.16), kind=kLoop, calls=%fused_computation.5 | loop fusion | flops 1212416 | bytes 606208 | tf_op jit(solution)/shard_map/concatenate | solution.py:326
  2.7 1.3 %collective-permute-start.2 = (bf16[2,16,4736]{2,1,0:T(8,128)(2,1)S(1)}, bf16[2,16,4736]{2,1,0:T(8,128)(2,1)S(1)}, u32[]{:S(2)}, u32[]{:S(2)}) collective-permute-start(bf16[2,16,4736]{2,1,0:T(8,128)(2,1)S(1)} %pad_maximum_fusion.3.refs_0_), channel_id=1, source_target_pairs={{0,2},{2,0},{4,6},{6,4},{8,10},{10,8},{12,14},{14,12},{1,3},{3,1},... | collective-permute-start | bytes 909320 | tf_op jit(solution)/shard_map/ppermute | solution.py:70
  4.2 1.8 %constant_dynamic-slice_fusion.1.refs_3_.weight_own = bf16[256,4096]{1,0:T(8,128)(2,1)S(1)} fusion(bf16[256,8192]{1,0:T(8,128)(2,1)} %param.17, s32[]{:T(128)S(6)} %select_n.19), kind=kLoop, calls=%fused_computation.9 | loop fusion | bytes 4194308 | tf_op jit(solution)/shard_map/dynamic_slice | solution.py:338
  6.1 3.2 %collective-permute-done = bf16[128,4096]{1,0:T(8,128)(2,1)} collective-permute-done((bf16[128,4096]{1,0:T(8,128)(2,1)}, bf16[128,4096]{1,0:T(8,128)(2,1)}, u32[]{:S(2)}, u32[]{:S(2)}) %collective-permute-start) | collective-permute-done | bytes 1048608 | tf_op jit(solution)/shard_map/ppermute | solution.py:316
  9.3 1.2 %collective-permute-start.4 = (bf16[2,16,4096]{2,1,0:T(8,128)(2,1)S(1)}, bf16[2,16,4096]{2,1,0:T(8,128)(2,1)S(1)}, u32[]{:S(2)}, u32[]{:S(2)}) collective-permute-start(bf16[2,16,4096]{2,1,0:T(8,128)(2,1)S(1)} %copy-done.2), channel_id=1, source_target_pairs={{0,2},{2,0},{4,6},{6,4},{8,10},{10,8},{12,14},{14,12},{1,3},{3,1},... | collective-permute-start | bytes 786440 | tf_op jit(solution)/shard_map/ppermute | solution.py:70
  10.6 1.4 %broadcast_select_fusion.1 = (bf16[128,4096]{1,0:T(8,128)(2,1)S(1)}, bf16[128,4096]{1,0:T(8,128)(2,1)S(1)}) fusion(bf16[128,4096]{1,0:T(8,128)(2,1)S(1)} %copy-done.1, bf16[128,4096]{1,0:T(8,128)(2,1)} %collective-permute-done, pred[]{:T(512)S(6)} %eq.3), kind=kLoop, calls=%fused_computation.4 | loop fusion | flops 1048576 | bytes 4194305 | tf_op jit(solution)/shard_map/jit(_where)/select_n | solution.py:107
  11.9 0.7 %fusion.1 = f32[128,256]{1,0:T(8,128)S(1)} fusion(bf16[8192,256]{1,0:T(8,128)(2,1)S(1)} %copy-done.7, bf16[128,4096]{1,0:T(8,128)(2,1)S(1)} %get-tuple-element.14, bf16[128,4096]{1,0:T(8,128)(2,1)S(1)} %get-tuple-element.13), kind=kOutput, calls=%fused_computation.2 | convolution fusion | flops 541065216 | bytes 6422528 | tf_op jit(solution)/shard_map/dot_general | solution.py:113
  12.7 0.7 %fusion = f32[128,128]{1,0:T(8,128)S(1)} fusion(bf16[8192,128]{1,0:T(8,128)(2,1)S(1)} %copy-done, bf16[128,4096]{1,0:T(8,128)(2,1)S(1)} %get-tuple-element.14, bf16[128,4096]{1,0:T(8,128)(2,1)S(1)} %get-tuple-element.13), kind=kOutput, calls=%fused_computation.1 | convolution fusion | flops 272629760 | bytes 4259840 | tf_op jit(solution)/shard_map/dot_general | solution.py:113
  13.5 0.6 %pick.8.refs_2_ = bf16[2,16,4736]{2,1,0:T(8,128)(2,1)S(1)} custom-call(s32[8]{0:T(128)S(1)} %copy-done.5, s32[16]{0:T(128)S(1)} %copy-done.6, bf16[2,16,4736]{2,1,0:T(8,128)(2,1)S(1)} %pad_maximum_fusion.3.refs_0_, bf16[2,16,4736]{2,1,0:T(8,128)(2,1)S(1)} %collective-permute-done.2.refs_1_, f32[128,384]{1,0:T(8,128)S(1)} %pad_maximum_fusion.4.refs_2_.base_own), custom_call_target="tpu_custom_call" | custom-call | bytes 606208 | tf_op jit(solution)/shard_map/pick/pallas_call | solution.py:93
  14.3 1.3 %collective-permute-done.6.refs_1_.refs_5_ = bf16[2,16,4096]{2,1,0:T(8,128)(2,1)S(1)} collective-permute-done((bf16[2,16,4096]{2,1,0:T(8,128)(2,1)S(1)}, bf16[2,16,4096]{2,1,0:T(8,128)(2,1)S(1)}, u32[]{:S(2)}, u32[]{:S(2)}) %collective-permute-start.6) | collective-permute-done | bytes 262176 | tf_op jit(solution)/shard_map/ppermute | solution.py:70
  15.6 0.6 %pick.9.refs_2_ = bf16[2,16,4096]{2,1,0:T(8,128)(2,1)S(1)} custom-call(s32[8]{0:T(128)S(1)} %copy-done.5, s32[16]{0:T(128)S(1)} %copy-done.6, bf16[2,16,4096]{2,1,0:T(8,128)(2,1)S(1)} %get-tuple-element.15.refs_0_.refs_4_, bf16[2,16,4096]{2,1,0:T(8,128)(2,1)S(1)} %collective-permute-done.6.refs_1_.refs_5_, bf16[2,16,4736]{2,1,0:T(8,128)(2,1)S(1)} %pick.8.refs_2_), custom_call_target="tpu_custom_call" | custom-call | bytes 524288 | tf_op jit(solution)/shard_map/pick/pallas_call | solution.py:93
  16.5 1.0 %pick.10.refs_2_ = bf16[2,16,4096]{2,1,0:T(8,128)(2,1)S(1)} custom-call(s32[8]{0:T(128)S(1)} %copy-done.5, s32[16]{0:T(128)S(1)} %copy-done.6, bf16[2,16,4096]{2,1,0:T(8,128)(2,1)S(1)} %get-tuple-element.17.refs_0_.refs_8_, bf16[2,16,4096]{2,1,0:T(8,128)(2,1)} %collective-permute-done.5.refs_1_.refs_9_, bf16[2,16,4096]{2,1,0:T(8,128)(2,1)S(1)} %pick.9.refs_2_), custom_call_target="tpu_custom_call" | custom-call | bytes 524288 | tf_op jit(solution)/shard_map/pick/pallas_call | solution.py:93
  17.5 1.3 %collective-permute-start.11 = (bf16[2,16,4096]{2,1,0:T(8,128)(2,1)S(1)}, bf16[2,16,4096]{2,1,0:T(8,128)(2,1)S(1)}, u32[]{:S(2)}, u32[]{:S(2)}) collective-permute-start(bf16[2,16,4096]{2,1,0:T(8,128)(2,1)S(1)} %pick.10.refs_2_), channel_id=1, source_target_pairs={{0,2},{2,0},{4,6},{6,4},{8,10},{10,8},{12,14},{14,12},{1,3},{3,1},... | collective-permute-start | bytes 786440 | tf_op jit(solution)/shard_map/ppermute | solution.py:74
  18.8 1.7 %constant_dynamic-slice_fusion.refs_4_.weight_other = bf16[256,4096]{1,0:T(8,128)(2,1)S(1)} fusion(bf16[256,8192]{1,0:T(8,128)(2,1)} %collective-permute-done.7, s32[]{:T(128)S(6)} %select_n.19), kind=kLoop, calls=%fused_computation.8 | loop fusion | bytes 4194308 | tf_op jit(solution)/shard_map/dynamic_slice | solution.py:338
  20.6 0.6 %pick.11.refs_3_ = bf16[2,16,4096]{2,1,0:T(8,128)(2,1)S(1)} custom-call(s32[8]{0:T(128)S(1)} %copy-done.5, s32[16]{0:T(128)S(1)} %copy-done.6, bf16[2,16,4096]{2,1,0:T(8,128)(2,1)S(1)} %copy-done.2, bf16[2,16,4096]{2,1,0:T(8,128)(2,1)S(1)} %collective-permute-done.4.refs_1_, bf16[2,16,4096]{2,1,0:T(8,128)(2,1)S(1)} %pick.10.refs_2_, ...), custom_call_target="tpu_custom_call" | custom-call | bytes 524288 | tf_op jit(solution)/shard_map/pick/pallas_call | solution.py:93
  21.3 2.7 %collective-permute-done.3.refs_2_ = bf16[2,16,4736]{2,1,0:T(8,128)(2,1)S(1)} collective-permute-done((bf16[2,16,4736]{2,1,0:T(8,128)(2,1)S(1)}, bf16[2,16,4736]{2,1,0:T(8,128)(2,1)S(1)}, u32[]{:S(2)}, u32[]{:S(2)}) %collective-permute-start.3) | collective-permute-done | bytes 303136 | tf_op jit(solution)/shard_map/ppermute | solution.py:74
  24.0 0.6 %pick.12.refs_3_ = bf16[1,16,4736]{2,1,0:T(8,128)(2,1)S(1)} custom-call(s32[8]{0:T(128)S(1)} %copy-done.5, s32[16]{0:T(128)S(1)} %copy-done.6, bf16[2,16,4736]{2,1,0:T(8,128)(2,1)S(1)} %pad_maximum_fusion.3.refs_0_, bf16[2,16,4736]{2,1,0:T(8,128)(2,1)S(1)} %collective-permute-done.2.refs_1_, bf16[2,16,4736]{2,1,0:T(8,128)(2,1)S(1)} %collective-permute-done.3.refs_2_, ...), custom_call_target="tpu_custom_call" | custom-call | bytes 303104 | tf_op jit(solution)/shard_map/pick/pallas_call | solution.py:93
  24.7 0.6 %pick.13.refs_3_ = bf16[1,16,4096]{2,1,0:T(8,128)(2,1)S(1)} custom-call(s32[8]{0:T(128)S(1)} %copy-done.5, s32[16]{0:T(128)S(1)} %copy-done.6, bf16[2,16,4096]{2,1,0:T(8,128)(2,1)S(1)} %get-tuple-element.15.refs_0_.refs_4_, bf16[2,16,4096]{2,1,0:T(8,128)(2,1)S(1)} %collective-permute-done.6.refs_1_.refs_5_, ...), custom_call_target="tpu_custom_call" | custom-call | bytes 262144 | tf_op jit(solution)/shard_map/pick/pallas_call | solution.py:93
  25.3 2.9 %collective-permute-done.11.refs_2_.refs_10_ = bf16[2,16,4096]{2,1,0:T(8,128)(2,1)S(1)} collective-permute-done((bf16[2,16,4096]{2,1,0:T(8,128)(2,1)S(1)}, bf16[2,16,4096]{2,1,0:T(8,128)(2,1)S(1)}, u32[]{:S(2)}, u32[]{:S(2)}) %collective-permute-start.11) | collective-permute-done | bytes 262176 | tf_op jit(solution)/shard_map/ppermute | solution.py:74
  28.2 1.0 %pick.14.refs_3_ = bf16[1,16,4096]{2,1,0:T(8,128)(2,1)S(1)} custom-call(s32[8]{0:T(128)S(1)} %copy-done.5, s32[16]{0:T(128)S(1)} %copy-done.6, bf16[2,16,4096]{2,1,0:T(8,128)(2,1)S(1)} %get-tuple-element.17.refs_0_.refs_8_, bf16[2,16,4096]{2,1,0:T(8,128)(2,1)} %collective-permute-done.5.refs_1_.refs_9_, ...), custom_call_target="tpu_custom_call" | custom-call | bytes 262144 | tf_op jit(solution)/shard_map/pick/pallas_call | solution.py:93
  29.2 0.7 %collective-permute-start.12 = (bf16[1,16,4096]{2,1,0:T(8,128)(2,1)S(1)}, bf16[1,16,4096]{2,1,0:T(8,128)(2,1)S(1)}, u32[]{:S(2)}, u32[]{:S(2)}) collective-permute-start(bf16[1,16,4096]{2,1,0:T(8,128)(2,1)S(1)} %pick.14.refs_3_), channel_id=1, source_target_pairs={{0,4},{2,6},{4,0},{6,2},{8,12},{10,14},{12,8},{14,10},{1,5},{3,7},... | collective-permute-start | bytes 393224 | tf_op jit(solution)/shard_map/ppermute | solution.py:74
  29.9 3.6 %collective-permute-start.1 = (f32[128,384]{1,0:T(8,128)S(1)}, f32[128,384]{1,0:T(8,128)S(1)}, u32[]{:S(2)}, u32[]{:S(2)}) collective-permute-start(f32[128,384]{1,0:T(8,128)S(1)} %pad_maximum_fusion.4.refs_2_.base_own), channel_id=1, source_target_pairs={{0,1},{1,0},{2,3},{3,2},{4,5},{5,4},{6,7},{7,6},{8,9},{9,8},{10,11... | collective-permute-start | bytes 589832 | tf_op jit(solution)/shard_map/ppermute | solution.py:316
  34.1 0.6 %pick.15.refs_12_ = bf16[1,16,4096]{2,1,0:T(8,128)(2,1)S(1)} custom-call(s32[8]{0:T(128)S(1)} %copy-done.5, s32[16]{0:T(128)S(1)} %copy-done.6, bf16[2,16,4096]{2,1,0:T(8,128)(2,1)S(1)} %copy-done.2, bf16[2,16,4096]{2,1,0:T(8,128)(2,1)S(1)} %collective-permute-done.4.refs_1_, bf16[2,16,4096]{2,1,0:T(8,128)(2,1)S(1)} %collective-permute-done.13.refs_2_, ...), custom_call_target="tpu_custom_call" | custom-call | bytes 262144 | tf_op jit(solution)/shard_map/pick/pallas_call | solution.py:93
  34.8 1.2 %collective-permute-start.16 = (bf16[1,16,4096]{2,1,0:T(8,128)(2,1)S(1)}, bf16[1,16,4096]{2,1,0:T(8,128)(2,1)S(1)}, u32[]{:S(2)}, u32[]{:S(2)}) collective-permute-start(bf16[1,16,4096]{2,1,0:T(8,128)(2,1)S(1)} %pick.15.refs_12_), channel_id=1, source_target_pairs={{0,8},{2,10},{4,12},{6,14},{8,0},{10,2},{12,4},{14,6},{1,9},{3,11}... | collective-permute-start | bytes 393224 | tf_op jit(solution)/shard_map/ppermute | solution.py:74
  36.0 6.7 %collective-permute-done.10.refs_7_ = bf16[1,16,4096]{2,1,0:T(8,128)(2,1)S(1)} collective-permute-done((bf16[1,16,4096]{2,1,0:T(8,128)(2,1)S(1)}, bf16[1,16,4096]{2,1,0:T(8,128)(2,1)S(1)}, u32[]{:S(2)}, u32[]{:S(2)}) %collective-permute-start.10) | collective-permute-done | bytes 131104 | tf_op jit(solution)/shard_map/ppermute | solution.py:74
  42.7 1.5 %shrink.1 = (f32[128,48]{1,0:T(8,128)S(1)}, bf16[16,640]{1,0:T(8,128)(2,1)S(1)}) custom-call(s32[8]{0:T(128)S(1)} %copy-done.5, s32[16]{0:T(128)S(1)} %copy-done.6, bf16[128,4096]{1,0:T(8,128)(2,1)S(1)} %copy-done.1, bf16[2,16,4736]{2,1,0:T(8,128)(2,1)S(1)} %pad_maximum_fusion.3.refs_0_, bf16[2,16,4736]{2,1,0:T(8,128)(2,1)S(1)} %collective-permute-done.2.refs_1_, ...), custom_call_target="tpu_custom_call" | custom-call | flops 50331648 | bytes 1048576 | tf_op jit(solution)/shard_map/shrink/pallas_call | solution.py:139
  44.2 1.4 %collective-permute-start.14 = (f32[128,48]{1,0:T(8,128)S(1)}, f32[128,48]{1,0:T(8,128)S(1)}, u32[]{:S(2)}, u32[]{:S(2)}) collective-permute-start(f32[128,48]{1,0:T(8,128)S(1)} %get-tuple-element.9.shrink_own), channel_id=1, source_target_pairs={{0,1},{1,0},{2,3},{3,2},{4,5},{5,4},{6,7},{7,6},{8,9},{9,8},{10,11... | collective-permute-start | bytes 73736 | tf_op jit(solution)/shard_map/ppermute | solution.py:316
  45.8 1.0 %collective-permute-done.15.small_other = bf16[16,640]{1,0:T(8,128)(2,1)S(1)} collective-permute-done((bf16[16,640]{1,0:T(8,128)(2,1)S(1)}, bf16[16,640]{1,0:T(8,128)(2,1)S(1)}, u32[]{:S(2)}, u32[]{:S(2)}) %collective-permute-start.15) | collective-permute-done | bytes 20512 | tf_op jit(solution)/shard_map/ppermute | solution.py:316
  46.8 2.6 %attention.1 = (f32[128,4096]{1,0:T(8,128)S(1)}, bf16[128,16]{1,0:T(8,128)(2,1)S(1)}) custom-call(s32[2]{0:T(128)S(1)} %pad_add_fusion.place, f32[128,384]{1,0:T(8,128)S(1)} %pad_maximum_fusion.4.refs_2_.base_own, f32[128,384]{1,0:T(8,128)S(1)} %collective-permute-done.1.base_other, f32[128,48]{1,0:T(8,128)S(1)} %get-tuple-element.9.shrink_own, ...), custom_call_target="tpu_custom_call" | custom-call | flops 536870912 | bytes 4194304 | tf_op jit(solution)/shard_map/attention/pallas_call | solution.py:231
  49.5 1.8 %finish.1 = bf16[128,4096]{1,0:T(8,128)(2,1)} custom-call(s32[8]{0:T(128)S(1)} %copy-done.5, s32[16]{0:T(128)S(1)} %copy-done.6, s32[2]{0:T(128)S(1)} %pad_add_fusion.place, f32[128,4096]{1,0:T(8,128)S(1)} %get-tuple-element.11.base_ref, bf16[128,16]{1,0:T(8,128)(2,1)S(1)} %get-tuple-element.12.low_ref, bf16[2,16,4096]{2,1,0:T(8,128)(2,1)S(1)} %copy-done.2, ...), custom_call_target="tpu_custom_call" | custom-call | flops 16777216 | bytes 3145728 | tf_op jit(solution)/shard_map/finish/pallas_call | solution.py:268
  (38 shorter events, 1.2 us)
Async XLA Ops:
  0.0 12.7 %copy-start = (bf16[8192,128]{1,0:T(8,128)(2,1)S(1)}, bf16[8192,128]{1,0:T(8,128)(2,1)}, u32[]{:S(2)}) copy-start(bf16[8192,128]{1,0:T(8,128)(2,1)} %param.16) | copy-start | bytes 6291460
  0.0 18.8 %collective-permute-start.7 = (bf16[256,8192]{1,0:T(8,128)(2,1)}, bf16[256,8192]{1,0:T(8,128)(2,1)}, u32[]{:S(2)}, u32[]{:S(2)}) collective-permute-start(bf16[256,8192]{1,0:T(8,128)(2,1)} %param.17), channel_id=1, source_target_pairs={{0,1},{1,0},{2,3},{3,2},{4,5},{5,4},{6,7},{7,6},{8,9},{9,8},{10,11... | collective-permute-start | bytes 12582920 | tf_op jit(solution)/shard_map/ppermute | solution.py:316
  0.7 8.6 %collective-permute-start = (bf16[128,4096]{1,0:T(8,128)(2,1)}, bf16[128,4096]{1,0:T(8,128)(2,1)}, u32[]{:S(2)}, u32[]{:S(2)}) collective-permute-start(bf16[128,4096]{1,0:T(8,128)(2,1)} %rows_ref.1), channel_id=1, source_target_pairs={{0,1},{1,0},{2,3},{3,2},{4,5},{5,4},{6,7},{7,6},{8,9},{9,8},{10,11... | collective-permute-start | bytes 3145736 | tf_op jit(solution)/shard_map/ppermute | solution.py:316
  2.7 10.8 %collective-permute-start.2 = (bf16[2,16,4736]{2,1,0:T(8,128)(2,1)S(1)}, bf16[2,16,4736]{2,1,0:T(8,128)(2,1)S(1)}, u32[]{:S(2)}, u32[]{:S(2)}) collective-permute-start(bf16[2,16,4736]{2,1,0:T(8,128)(2,1)S(1)} %pad_maximum_fusion.3.refs_0_), channel_id=1, source_target_pairs={{0,2},{2,0},{4,6},{6,4},{8,10},{10,8},{12,14},{14,12},{1,3},{3,1},... | collective-permute-start | bytes 909320 | tf_op jit(solution)/shard_map/ppermute | solution.py:70
  4.0 11.6 %collective-permute-start.6 = (bf16[2,16,4096]{2,1,0:T(8,128)(2,1)S(1)}, bf16[2,16,4096]{2,1,0:T(8,128)(2,1)S(1)}, u32[]{:S(2)}, u32[]{:S(2)}) collective-permute-start(bf16[2,16,4096]{2,1,0:T(8,128)(2,1)S(1)} %get-tuple-element.15.refs_0_.refs_4_), channel_id=1, source_target_pairs={{0,4},{2,6},{4,0},{6,2},{8,12},{10,14},{12,8},{14,10},{1,5},{3,7},... | collective-permute-start | bytes 786440 | tf_op jit(solution)/shard_map/ppermute | solution.py:70
  4.2 12.3 %collective-permute-start.5 = (bf16[2,16,4096]{2,1,0:T(8,128)(2,1)S(1)}, bf16[2,16,4096]{2,1,0:T(8,128)(2,1)}, u32[]{:S(2)}, u32[]{:S(2)}) collective-permute-start(bf16[2,16,4096]{2,1,0:T(8,128)(2,1)S(1)} %get-tuple-element.17.refs_0_.refs_8_), channel_id=1, source_target_pairs={{0,8},{2,10},{4,12},{6,14},{8,0},{10,2},{12,4},{14,6},{1,9},{3,11}... | collective-permute-start | bytes 786440 | tf_op jit(solution)/shard_map/ppermute | solution.py:70
  4.2 5.1 %copy-start.2 = (bf16[2,16,4096]{2,1,0:T(8,128)(2,1)S(1)}, bf16[2,16,4096]{2,1,0:T(8,128)(2,1)}, u32[]{:S(2)}) copy-start(bf16[2,16,4096]{2,1,0:T(8,128)(2,1)} %refs_0_.5) | copy-start | bytes 786436
  4.2 6.3 %copy-start.1 = (bf16[128,4096]{1,0:T(8,128)(2,1)S(1)}, bf16[128,4096]{1,0:T(8,128)(2,1)}, u32[]{:S(2)}) copy-start(bf16[128,4096]{1,0:T(8,128)(2,1)} %rows_ref.1) | copy-start | bytes 3145732
  6.1 5.9 %copy-start.7 = (bf16[8192,256]{1,0:T(8,128)(2,1)S(1)}, bf16[8192,256]{1,0:T(8,128)(2,1)}, u32[]{:S(2)}) copy-start(bf16[8192,256]{1,0:T(8,128)(2,1)} %param.15) | copy-start | bytes 12582916
  9.3 11.3 %collective-permute-start.4 = (bf16[2,16,4096]{2,1,0:T(8,128)(2,1)S(1)}, bf16[2,16,4096]{2,1,0:T(8,128)(2,1)S(1)}, u32[]{:S(2)}, u32[]{:S(2)}) collective-permute-start(bf16[2,16,4096]{2,1,0:T(8,128)(2,1)S(1)} %copy-done.2), channel_id=1, source_target_pairs={{0,2},{2,0},{4,6},{6,4},{8,10},{10,8},{12,14},{14,12},{1,3},{3,1},... | collective-permute-start | bytes 786440 | tf_op jit(solution)/shard_map/ppermute | solution.py:70
  12.7 0.8 %copy-start.5 = (s32[8]{0:T(128)S(1)}, s32[8]{0:T(128)}, u32[]{:S(2)}) copy-start(s32[8]{0:T(128)} %requests.19) | copy-start | bytes 100
  12.7 0.8 %copy-start.6 = (s32[16]{0:T(128)S(1)}, s32[16]{0:T(128)}, u32[]{:S(2)}) copy-start(s32[16]{0:T(128)} %pool.19) | copy-start | bytes 196
  14.1 9.9 %collective-permute-start.3 = (bf16[2,16,4736]{2,1,0:T(8,128)(2,1)S(1)}, bf16[2,16,4736]{2,1,0:T(8,128)(2,1)S(1)}, u32[]{:S(2)}, u32[]{:S(2)}) collective-permute-start(bf16[2,16,4736]{2,1,0:T(8,128)(2,1)S(1)} %pick.8.refs_2_), channel_id=1, source_target_pairs={{0,4},{2,6},{4,0},{6,2},{8,12},{10,14},{12,8},{14,10},{1,5},{3,7},... | collective-permute-start | bytes 909320 | tf_op jit(solution)/shard_map/ppermute | solution.py:74
  16.2 8.5 %collective-permute-start.9 = (bf16[2,16,4096]{2,1,0:T(8,128)(2,1)S(1)}, bf16[2,16,4096]{2,1,0:T(8,128)(2,1)S(1)}, u32[]{:S(2)}, u32[]{:S(2)}) collective-permute-start(bf16[2,16,4096]{2,1,0:T(8,128)(2,1)S(1)} %pick.9.refs_2_), channel_id=1, source_target_pairs={{0,2},{2,0},{4,6},{6,4},{8,10},{10,8},{12,14},{14,12},{1,3},{3,1},... | collective-permute-start | bytes 786440 | tf_op jit(solution)/shard_map/ppermute | solution.py:74
  17.5 10.7 %collective-permute-start.11 = (bf16[2,16,4096]{2,1,0:T(8,128)(2,1)S(1)}, bf16[2,16,4096]{2,1,0:T(8,128)(2,1)S(1)}, u32[]{:S(2)}, u32[]{:S(2)}) collective-permute-start(bf16[2,16,4096]{2,1,0:T(8,128)(2,1)S(1)} %pick.10.refs_2_), channel_id=1, source_target_pairs={{0,2},{2,0},{4,6},{6,4},{8,10},{10,8},{12,14},{14,12},{1,3},{3,1},... | collective-permute-start | bytes 786440 | tf_op jit(solution)/shard_map/ppermute | solution.py:74
  21.2 12.9 %collective-permute-start.13 = (bf16[2,16,4096]{2,1,0:T(8,128)(2,1)S(1)}, bf16[2,16,4096]{2,1,0:T(8,128)(2,1)S(1)}, u32[]{:S(2)}, u32[]{:S(2)}) collective-permute-start(bf16[2,16,4096]{2,1,0:T(8,128)(2,1)S(1)} %pick.11.refs_3_), channel_id=1, source_target_pairs={{0,4},{2,6},{4,0},{6,2},{8,12},{10,14},{12,8},{14,10},{1,5},{3,7},... | collective-permute-start | bytes 786440 | tf_op jit(solution)/shard_map/ppermute | solution.py:74
  24.6 18.1 %collective-permute-start.8 = (bf16[1,16,4736]{2,1,0:T(8,128)(2,1)S(1)}, bf16[1,16,4736]{2,1,0:T(8,128)(2,1)S(1)}, u32[]{:S(2)}, u32[]{:S(2)}) collective-permute-start(bf16[1,16,4736]{2,1,0:T(8,128)(2,1)S(1)} %pick.12.refs_3_), channel_id=1, source_target_pairs={{0,8},{2,10},{4,12},{6,14},{8,0},{10,2},{12,4},{14,6},{1,9},{3,11}... | collective-permute-start | bytes 454664 | tf_op jit(solution)/shard_map/ppermute | solution.py:74
  29.2 6.8 %collective-permute-start.12 = (bf16[1,16,4096]{2,1,0:T(8,128)(2,1)S(1)}, bf16[1,16,4096]{2,1,0:T(8,128)(2,1)S(1)}, u32[]{:S(2)}, u32[]{:S(2)}) collective-permute-start(bf16[1,16,4096]{2,1,0:T(8,128)(2,1)S(1)} %pick.14.refs_3_), channel_id=1, source_target_pairs={{0,4},{2,6},{4,0},{6,2},{8,12},{10,14},{12,8},{14,10},{1,5},{3,7},... | collective-permute-start | bytes 393224 | tf_op jit(solution)/shard_map/ppermute | solution.py:74
  29.9 12.8 %collective-permute-start.10 = (bf16[1,16,4096]{2,1,0:T(8,128)(2,1)S(1)}, bf16[1,16,4096]{2,1,0:T(8,128)(2,1)S(1)}, u32[]{:S(2)}, u32[]{:S(2)}) collective-permute-start(bf16[1,16,4096]{2,1,0:T(8,128)(2,1)S(1)} %pick.13.refs_3_), channel_id=1, source_target_pairs={{0,8},{2,10},{4,12},{6,14},{8,0},{10,2},{12,4},{14,6},{1,9},{3,11}... | collective-permute-start | bytes 393224 | tf_op jit(solution)/shard_map/ppermute | solution.py:74
  29.9 15.9 %collective-permute-start.1 = (f32[128,384]{1,0:T(8,128)S(1)}, f32[128,384]{1,0:T(8,128)S(1)}, u32[]{:S(2)}, u32[]{:S(2)}) collective-permute-start(f32[128,384]{1,0:T(8,128)S(1)} %pad_maximum_fusion.4.refs_2_.base_own), channel_id=1, source_target_pairs={{0,1},{1,0},{2,3},{3,2},{4,5},{5,4},{6,7},{7,6},{8,9},{9,8},{10,11... | collective-permute-start | bytes 589832 | tf_op jit(solution)/shard_map/ppermute | solution.py:316
  34.7 12.1 %copy-start.3 = (f32[128,128]{1,0:T(8,128)S(1)}, f32[128,128]{1,0:T(8,128)}, u32[]{:S(2)}) copy-start(f32[128,128]{1,0:T(8,128)} %constant.14.clone.cosine) | copy-start | bytes 196612
  34.7 12.1 %copy-start.4 = (f32[128,128]{1,0:T(8,128)S(1)}, f32[128,128]{1,0:T(8,128)}, u32[]{:S(2)}) copy-start(f32[128,128]{1,0:T(8,128)} %constant.15.clone.sine) | copy-start | bytes 196612
  34.8 14.7 %collective-permute-start.16 = (bf16[1,16,4096]{2,1,0:T(8,128)(2,1)S(1)}, bf16[1,16,4096]{2,1,0:T(8,128)(2,1)S(1)}, u32[]{:S(2)}, u32[]{:S(2)}) collective-permute-start(bf16[1,16,4096]{2,1,0:T(8,128)(2,1)S(1)} %pick.15.refs_12_), channel_id=1, source_target_pairs={{0,8},{2,10},{4,12},{6,14},{8,0},{10,2},{12,4},{14,6},{1,9},{3,11}... | collective-permute-start | bytes 393224 | tf_op jit(solution)/shard_map/ppermute | solution.py:74
  44.2 2.6 %collective-permute-start.14 = (f32[128,48]{1,0:T(8,128)S(1)}, f32[128,48]{1,0:T(8,128)S(1)}, u32[]{:S(2)}, u32[]{:S(2)}) collective-permute-start(f32[128,48]{1,0:T(8,128)S(1)} %get-tuple-element.9.shrink_own), channel_id=1, source_target_pairs={{0,1},{1,0},{2,3},{3,2},{4,5},{5,4},{6,7},{7,6},{8,9},{9,8},{10,11... | collective-permute-start | bytes 73736 | tf_op jit(solution)/shard_map/ppermute | solution.py:316
  45.6 1.2 %collective-permute-start.15 = (bf16[16,640]{1,0:T(8,128)(2,1)S(1)}, bf16[16,640]{1,0:T(8,128)(2,1)S(1)}, u32[]{:S(2)}, u32[]{:S(2)}) collective-permute-start(bf16[16,640]{1,0:T(8,128)(2,1)S(1)} %get-tuple-element.10.small_own), channel_id=1, source_target_pairs={{0,1},{1,0},{2,3},{3,2},{4,5},{5,4},{6,7},{7,6},{8,9},{9,8},{10,11... | collective-permute-start | bytes 61448 | tf_op jit(solution)/shard_map/ppermute | solution.py:316
